TPU v7x, 32 devices: a whole 2x2x4 slice. The times are simulated.
32 devices in a mesh: row: 4 (over x, core), col: 8 (over z, y).
Axes of the slice: x: 2, y: 2, z: 4, core: 2. Of those that a mesh axis runs over, the one named last changes fastest.
Arguments:
- grad: bfloat16 [2048, 7168], P('row', 'col'), may hold values from -18 to 18
- weight: float32 [2048, 7168], P('row', 'col'), may hold values from -6 to 6
- moment: float32 [2048, 7168], P('row', 'col'), may hold values from -18 to 18
- second: float32 [2048, 7168], P('row', 'col'), may hold values from 1 to 30
- gram_left: float32 [4, 512, 512], P('row', 'col'), may hold values from -1.2 to 12, as said below
- basis_left: float32 [4, 512, 512], P('row', 'col'), may hold values from -0.5 to 1.5, as said below
- gram_right: float32 [8, 896, 896], P('col', 'row'), may hold values from -1.2 to 12, as said below
- basis_right: float32 [8, 896, 896], P('col', 'row'), may hold values from -0.5 to 1.5, as said below
Outputs:
- new_weight: float32 [2048, 7168], P('row', 'col')
- new_moment: float32 [2048, 7168], P('row', 'col')
- new_second: float32 [2048, 7168], P('row', 'col')
- new_gram_left: float32 [4, 512, 512], P('row', 'col')
- new_basis_left: float32 [4, 512, 512], P('row', 'col')
- new_gram_right: float32 [8, 896, 896], P('col', 'row')
- new_basis_right: float32 [8, 896, 896], P('col', 'row')
Inputs may be any that keep to these rules, and one draw needn't show every extreme that they name: `gram_left`: every block is symmetric and positive definite. `basis_left`: every block is invertible. `gram_right`: every block is symmetric and positive definite. `basis_right`: every block is invertible.
All inputs are finite; a program needn't handle non-finite values.
Results may differ from a plain program's by a relative error of at most 0.0012.
Values may be sent and summed in bfloat16 or wider, within the bound.
No kernel may reach another device: no remote copies, remote signals or barrier semaphores. Data moves between devices by JAX's collectives and lax.ppermute only.
A program may use at most 128 MiB of HBM per device.

v0:
```python
import functools
import jax
import jax.numpy as jnp
from jax import lax
from jax.experimental import pallas as pl
from jax.experimental.pallas import tpu as pltpu

LANES = 128
ROWS = 8


def lane_mask(step):
    lanes = lax.broadcasted_iota(jnp.int32, (ROWS, LANES), 1)
    return (lanes >= step * ROWS) & (lanes < (step + 1) * ROWS)


def sub_row(x, k):
    return jnp.broadcast_to(x[k : k + 1, :], (ROWS, LANES))


def lane_col(x, c):
    return jnp.broadcast_to(x[:, c : c + 1], (ROWS, LANES))


def reciprocal(p):
    guess = pl.reciprocal(p, approx=True)
    return guess * (2.0 - p * guess)


def inverse_factor(rows):
    count = LANES // ROWS
    rows = list(rows)
    subs = lax.broadcasted_iota(jnp.int32, (ROWS, LANES), 0)
    lanes = lax.broadcasted_iota(jnp.int32, (ROWS, LANES), 1)
    out = []
    for s in range(count):
        base = s * ROWS
        pivot = rows[s]
        here = (lanes >= base) & (lanes < base + ROWS)
        cols = [lane_col(pivot, base + k) for k in range(ROWS)]
        full = jnp.where(here, (lanes == subs + base).astype(jnp.float32), pivot)
        forward = full
        inverse = jnp.zeros((ROWS, LANES), jnp.float32)
        pivots = jnp.ones((ROWS, LANES), jnp.float32)
        for j in range(ROWS):
            value = sub_row(cols[j], j)
            inv = reciprocal(value)
            scaled = cols[j] * inv
            m_full = jnp.where(subs == j, 0.0, scaled)
            for k in range(j + 1, ROWS):
                cols[k] = cols[k] - m_full * sub_row(cols[k], j)
            row = sub_row(full, j)
            if j < ROWS - 1:
                forward = forward - jnp.where(subs > j, scaled, 0.0) * sub_row(forward, j)
            full = full - m_full * row
            inverse = jnp.where(subs == j, inv, inverse)
            pivots = jnp.where(subs == j, value, pivots)
        out.append(jnp.where(lanes < base + ROWS, forward * lax.rsqrt(pivots), 0.0))
        full = full * inverse
        if s < count - 1:
            spread = [sub_row(full, k) for k in range(ROWS)]
            for i in range(s + 1, count):
                coeffs = [lane_col(rows[i], base + k) for k in range(ROWS)]
                terms = [coeffs[k] * spread[k] for k in range(ROWS)]
                while len(terms) > 1:
                    terms = [a + b for a, b in zip(terms[::2], terms[1::2])]
                rows[i] = jnp.where(here, 0.0, rows[i]) - terms[0]
    return out


def split(x):
    hi = x.astype(jnp.bfloat16)
    return hi, (x - hi.astype(jnp.float32)).astype(jnp.bfloat16)


def stack_left(x, axis):
    hi, lo = split(x)
    return jnp.concatenate([hi, hi, lo], axis=axis)


def stack_right(x, axis):
    hi, lo = split(x)
    return jnp.concatenate([hi, lo, hi], axis=axis)


def mm(a, b, dims):
    return lax.dot_general(a, b, (dims, ((), ())), preferred_element_type=jnp.float32)


def mm_nn(a, b):
    return mm(stack_left(a, 1), stack_right(b, 0), ((1,), (0,)))


def mm_nt(a, b):
    return mm(stack_left(a, 1), stack_right(b, 1), ((1,), (1,)))


def product(ah, al, bh, bl, dims):
    return mm(ah, bh, dims) + (mm(ah, bl, dims) + mm(al, bh, dims))


def block(i):
    return pl.ds(i * LANES, LANES) if isinstance(i, int) else pl.ds(pl.multiple_of(i * LANES, LANES), LANES)


class Chain:
    def __init__(self, z_ref, d_ref, w_ref, q_ref):
        self.z, self.d, self.w, self.q = z_ref, d_ref, w_ref, q_ref
        self.width = z_ref.shape[1]
        self.blocks = self.width // LANES

    def cross(self):
        hi, lo = split(self.z[self.width :, :])
        dims = ((0,), (0,))
        self.z[: self.width, :] = product(hi, lo, hi, lo, dims)
        self.w[...] = jnp.zeros_like(self.w)

    def step(self, j):
        at, before = block(j), block(lax.max(j - 1, 0))
        w = self.w[...]
        low = mm_nt(self.z[at, before], w)
        self.d[...] = self.z[at, at] - mm_nt(low, low)
        rows = [self.d[i * ROWS : (i + 1) * ROWS, :] for i in range(LANES // ROWS)]
        out = inverse_factor(rows)
        p = mm_nt(self.z[:, before], w)
        self.q[:, before] = p[self.width :, :]
        u = stack_right(mm_nn(w, self.z[before, :]), 0)
        self.z[...] -= mm(stack_left(p, 1), u, ((1,), (0,)))
        for i, row in enumerate(out):
            self.w[i * ROWS : (i + 1) * ROWS, :] = row

    def finish(self):
        last = block(self.blocks - 1)
        self.q[:, last] = mm_nt(self.z[self.width :, last], self.w[...])


from jax.sharding import PartitionSpec as P

STAT_DECAY = 0.95
FIRST_DECAY = 0.9
SECOND_DECAY = 0.95
EPSILON = 1e-08
STEP_SIZE = 0.02
WEIGHT_DECAY = 0.01
HEAD_LIMIT = 34 * 2**20
VMEM_LIMIT = 44 * 2**20


def offsets(size):
    return size // LANES // 2 + 1


def pack_products(cols, out_ref, dims, scale):
    blocks = len(cols)
    for i in range(blocks):
        for o in range(offsets(blocks * LANES)):
            term = mm(cols[i], cols[(i + o) % blocks], dims)
            out_ref[block(i), block(o)] = (term * scale).astype(out_ref.dtype)


def terms_kernel(scale_left, scale_right, grad_ref, right_ref, left_ref):
    rows, columns = grad_ref.shape
    pack_products([grad_ref[:, block(i)] for i in range(columns // LANES)], right_ref, ((0,), (0,)), scale_right)
    pack_products([grad_ref[block(i), :] for i in range(rows // LANES)], left_ref, ((1,), (1,)), scale_left)


def terms(grad, scale_left, scale_right):
    rows, columns = grad.shape
    return pl.pallas_call(
        functools.partial(terms_kernel, scale_left, scale_right),
        out_shape=[
            jax.ShapeDtypeStruct((columns, offsets(columns) * LANES), jnp.bfloat16),
            jax.ShapeDtypeStruct((rows, offsets(rows) * LANES), jnp.bfloat16),
        ],
        compiler_params=pltpu.CompilerParams(vmem_limit_bytes=VMEM_LIMIT),
    )(grad)


def place(ref, me, pieces, scale):
    for distance, piece, first in pieces:
        rows = piece.shape[0]
        at = pl.ds(pl.multiple_of((me ^ distance) * rows, ROWS), rows)
        value = piece[:, first : first + ref.shape[1]].astype(jnp.float32)
        ref[at, :] = value * scale if scale != 1.0 else value


def add_packed(gram_ref, packed_ref):
    blocks = gram_ref.shape[0] // LANES
    count = offsets(gram_ref.shape[0])
    for i in range(blocks):
        for o in range(count):
            k = (i + o) % blocks
            term = packed_ref[block(i), block(o)]
            gram_ref[block(i), block(k)] += term
            if o > 0 and not (blocks % 2 == 0 and o == count - 1):
                gram_ref[block(k), block(i)] += term.T


def image(z_ref, gh_ref, gl_ref, basis_ref):
    width = z_ref.shape[1]
    bh, bl = split(basis_ref[...])
    for i in range(gh_ref.shape[0] // LANES):
        z_ref[pl.ds(width + i * LANES, LANES), :] = product(
            gh_ref[block(i), :], gl_ref[block(i), :], bh, bl, ((1,), (0,))
        )


def split_rows(ref, hi_ref, lo_ref):
    for i in range(ref.shape[0] // LANES):
        hi_ref[block(i), :], lo_ref[block(i), :] = split(ref[block(i), :])


def own_rows(ref, me, rows):
    return ref[pl.ds(pl.multiple_of(me * rows, ROWS), rows), :]


def half_window(size):
    return -(-size // 2 // LANES) * LANES


def fill_halves(gram, me, count, own_in, other_in):
    size = gram.shape[0]
    place(gram, me, own_in, STAT_DECAY)
    if not other_in:
        return
    half = lax.div(2 * me, count)
    window = half_window(size)
    rest = size - window
    for distance, piece, _ in other_in:
        rows = piece.shape[0]
        at = pl.ds(pl.multiple_of((me ^ distance) * rows, ROWS), rows)
        gram[at, pl.ds(pl.multiple_of((1 - half) * rest, LANES), window)] = piece[:, :window] * STAT_DECAY
    near = pl.multiple_of(half * window, LANES)
    far = pl.multiple_of((1 - half) * rest, LANES)
    for i in range(rest // LANES):
        at = pl.ds(pl.multiple_of(near + i * LANES, LANES), LANES)
        gram[pl.ds(far, window), at] = gram[at, pl.ds(far, window)].T


def head_kernel(count, owns, others, sums, *refs):
    me_ref, refs = refs[0], list(refs[1:])
    gram_in = [(d, refs.pop(0), 0) for d in owns]
    basis_in = [(d, refs.pop(0), 0) for d in owns]
    other_in = [(d, refs.pop(0), half_window(refs[-6].shape[0])) for d in others]
    sum_in = [(d, refs.pop(0), 0) for d in sums]
    rows_ref, gh_ref, gl_ref, q_ref, gram, packed, basis, z, d, w = refs
    me = me_ref[0]
    fill_halves(gram, me, count, gram_in, other_in)
    place(packed, lax.rem(me, 2) if len(sums) > 1 else 0, sum_in, 1.0 - STAT_DECAY)
    place(basis, me, basis_in + other_in, 1.0)
    add_packed(gram, packed)
    rows_ref[...] = own_rows(gram, me, rows_ref.shape[0])
    split_rows(gram, gh_ref, gl_ref)
    image(z, gh_ref, gl_ref, basis)
    chain = Chain(z, d, w, q_ref)
    chain.cross()

    def step(j, carry):
        chain.step(j)
        return carry

    lax.fori_loop(0, chain.blocks, step, 0)
    chain.finish()


def in_specs(count):
    return [pl.BlockSpec(memory_space=pltpu.SMEM)] + [pl.BlockSpec(memory_space=pltpu.VMEM)] * count


def chain_scratch(width, rows):
    return [
        pltpu.VMEM((width + rows, width), jnp.float32),
        pltpu.VMEM((LANES, LANES), jnp.float32),
        pltpu.VMEM((LANES, LANES), jnp.float32),
    ]


def head(me, count, grams, bases, others, sums, width):
    args = [p for group in (grams, bases, others, sums) for _, p in group]
    rows, size = grams[0][1].shape
    return pl.pallas_call(
        functools.partial(head_kernel, count, *[[d for d, _ in group] for group in (grams, others, sums)]),
        out_shape=[
            jax.ShapeDtypeStruct((rows, size), jnp.float32),
            jax.ShapeDtypeStruct((size, size), jnp.bfloat16),
            jax.ShapeDtypeStruct((size, size), jnp.bfloat16),
            jax.ShapeDtypeStruct((size, width), jnp.float32),
        ],
        in_specs=in_specs(len(args)),
        scratch_shapes=[
            pltpu.VMEM((size, size), jnp.float32),
            pltpu.VMEM((size, offsets(size) * LANES), jnp.float32),
            pltpu.VMEM((size, width), jnp.float32),
            *chain_scratch(width, size),
        ],
        compiler_params=pltpu.CompilerParams(vmem_limit_bytes=HEAD_LIMIT),
    )(me, *args)


def rest_kernel(bases, others, sums, *refs):
    me_ref, refs = refs[0], list(refs[1:])
    gh, gl, q_first = refs[:3]
    refs = refs[3:]
    basis_in = [(d, refs.pop(0), q_first.shape[1]) for d in bases]
    basis_in += [(d, refs.pop(0), 0) for d in others]
    left = refs.pop(0)
    sum_in = [(d, refs.pop(0), 0) for d in sums]
    right_half, right_rows, left_half, left_rows, gram_rows = refs[:5]
    basis, qr, ql, gram_l, packed_l, basis_l, glh, gll, zr, dr, wr, zl, dl, wl = refs[5:]
    row, col = me_ref[0], me_ref[1]
    size = gram_l.shape[0]
    first = q_first.shape[1]
    place(basis, row, basis_in, 1.0)
    gram_l[...] = left[:, :size] * STAT_DECAY
    basis_l[...] = left[:, size:]
    place(packed_l, lax.rem(col, 2) if len(sums) > 1 else 0, sum_in, 1.0 - STAT_DECAY)
    add_packed(gram_l, packed_l)
    gram_rows[...] = own_rows(gram_l, col, gram_rows.shape[0])
    image(zr, gh, gl, basis)
    width = zr.shape[1]
    qh, qo = split(q_first[...])
    xh, xl = split(zr[width:, :])
    sh, sl = split(product(qh, qo, xh, xl, ((0,), (0,))))
    zr[width:, :] -= product(qh, qo, sh, sl, ((1,), (0,)))
    split_rows(gram_l, glh, gll)
    image(zl, glh, gll, basis_l)
    right, left = Chain(zr, dr, wr, qr), Chain(zl, dl, wl, ql)
    right.cross()
    left.cross()

    def step(j, carry):
        right.step(j)
        left.step(j)
        return carry

    def short(j, carry):
        right.step(j)
        return carry

    lax.fori_loop(0, left.blocks, step, 0)
    lax.fori_loop(left.blocks, right.blocks, short, 0)
    right.finish()
    left.finish()
    right_half[:, :first] = q_first[...].astype(jnp.bfloat16)
    right_half[:, first:] = qr[...].astype(jnp.bfloat16)
    right_rows[:, :first] = own_rows(q_first, row, right_rows.shape[0])
    right_rows[:, first:] = own_rows(qr, row, right_rows.shape[0])
    left_half[...] = ql[...].astype(jnp.bfloat16)
    left_rows[...] = own_rows(ql, col, left_rows.shape[0])


def rest(me, gh, gl, q_first, bases, others, left, sums, rows_l):
    args = [gh, gl, q_first] + [p for _, p in bases + others] + [left] + [p for _, p in sums]
    rows_r, size_r = bases[0][1].shape
    width = size_r - q_first.shape[1]
    size_l = left.shape[0]
    f32, bf16 = jnp.float32, jnp.bfloat16
    return pl.pallas_call(
        functools.partial(rest_kernel, *[[d for d, _ in group] for group in (bases, others, sums)]),
        out_shape=[
            jax.ShapeDtypeStruct((size_r, size_r), bf16),
            jax.ShapeDtypeStruct((rows_r, size_r), f32),
            jax.ShapeDtypeStruct((size_l, size_l), bf16),
            jax.ShapeDtypeStruct((rows_l, size_l), f32),
            jax.ShapeDtypeStruct((rows_l, size_l), f32),
        ],
        in_specs=in_specs(len(args)),
        scratch_shapes=[
            pltpu.VMEM((size_r, width), f32),
            pltpu.VMEM((size_r, width), f32),
            pltpu.VMEM((size_l, size_l), f32),
            pltpu.VMEM((size_l, size_l), f32),
            pltpu.VMEM((size_l, offsets(size_l) * LANES), f32),
            pltpu.VMEM((size_l, size_l), f32),
            pltpu.VMEM((size_l, size_l), bf16),
            pltpu.VMEM((size_l, size_l), bf16),
            *chain_scratch(width, size_r),
            *chain_scratch(size_l, size_l),
        ],
        compiler_params=pltpu.CompilerParams(vmem_limit_bytes=VMEM_LIMIT),
    )(me, *args)


def swap(x, axis, distance):
    count = lax.axis_size(axis)
    return lax.ppermute(x, axis, [(i, i ^ distance) for i in range(count)])


def distances(axis):
    count = lax.axis_size(axis)
    return [1 << b for b in range(count.bit_length() - 1)]


def spread(held, axis, steps):
    for distance in steps:
        held = held + [(at ^ distance, swap(piece, axis, distance)) for at, piece in held]
    return held


def sum_pairs(x, axis):
    me, kind = lax.axis_index(axis), x.dtype
    if lax.axis_size(axis) == 1:
        return x, [(0, x)]
    rows = x.shape[0] // 2
    own = lax.rem(me, 2)
    keep = lax.dynamic_slice_in_dim(x, own * rows, rows, 0)
    other = lax.dynamic_slice_in_dim(x, (1 - own) * rows, rows, 0)
    total = keep.astype(jnp.float32) + swap(other, axis, 1).astype(jnp.float32)
    for distance in distances(axis)[1:]:
        total = total.astype(kind)
        total = total.astype(jnp.float32) + swap(total, axis, distance).astype(jnp.float32)
    total = total.astype(kind)
    return total, [(0, total), (1, swap(total, axis, 1))]


def gather_right(gram, basis, width):
    count = lax.axis_size("row")
    grams, bases = [(0, gram)], [(0, basis)]
    if count == 1:
        return grams, bases, []
    window = half_window(gram.shape[1])
    half = lax.div(2 * lax.axis_index("row"), count)
    mine = lax.dynamic_slice_in_dim(gram, half * (gram.shape[1] - window), window, 1)
    mine = jnp.concatenate([mine, basis[:, :width]], axis=1)
    others = [(count // 2, swap(mine, "row", count // 2))]
    near = distances("row")[-2::-1]
    return spread(grams, "row", near), spread(bases, "row", near), spread(others, "row", near)


def rotate_in(matrix, left_half, right_half):
    inner = lax.dot_general(
        left_half, matrix, (((0,), (0,)), ((), ())), preferred_element_type=jnp.float32
    )
    return jnp.dot(inner.astype(jnp.bfloat16), right_half, preferred_element_type=jnp.float32)


def body(grad, weight, moment, second, gram_left, basis_left, gram_right, basis_right):
    block_left, block_right = grad.shape
    first = max(block_right - block_left, LANES)
    count = lax.axis_size("row")
    me = jnp.stack([lax.axis_index("row"), lax.axis_index("col")])
    lefts = lax.all_gather(
        jnp.concatenate([gram_left[0], basis_left[0]], axis=1), "col", axis=0, tiled=True
    )
    grams, bases, others = gather_right(gram_right[0], basis_right[0], first)
    terms_right, terms_left = terms(
        grad, 1.0 / (block_right * lax.axis_size("col")), 1.0 / (block_left * count)
    )
    sent, sums_right = sum_pairs(terms_right, "row")
    _, sums_left = sum_pairs(terms_left, "col")
    last, _ = lax.optimization_barrier((basis_right[0][:, first:], sent))
    last = [(d, swap(last, "row", d)) for d in range(count // 2, count)] if count > 1 else []
    new_gram_right, gh, gl, q_first = head(me, count, grams, bases, others, sums_right, first)
    right_half, basis_rows_right, left_half, basis_rows_left, new_gram_left = rest(
        me, gh, gl, q_first, bases, last, lefts, sums_left, gram_left.shape[1]
    )
    rotated_grad = rotate_in(grad, left_half, right_half)
    new_moment = FIRST_DECAY * moment + (1.0 - FIRST_DECAY) * grad.astype(jnp.float32)
    new_second = SECOND_DECAY * second + (1.0 - SECOND_DECAY) * rotated_grad * rotated_grad
    rotated_moment = rotate_in(new_moment.astype(jnp.bfloat16), left_half, right_half)
    direction = (rotated_moment / (jnp.sqrt(new_second) + EPSILON)).astype(jnp.bfloat16)
    turned = jnp.dot(left_half, direction, preferred_element_type=jnp.float32).astype(jnp.bfloat16)
    update = lax.dot_general(
        turned, right_half, (((1,), (1,)), ((), ())), preferred_element_type=jnp.float32
    )
    new_weight = weight - STEP_SIZE * (update + WEIGHT_DECAY * weight)
    return (
        new_weight,
        new_moment,
        new_second,
        new_gram_left[None],
        basis_rows_left[None],
        new_gram_right[None],
        basis_rows_right[None],
    )


def solution(mesh):
    specs = (
        P("row", "col"),
        P("row", "col"),
        P("row", "col"),
        P("row", "col"),
        P("row", "col", None),
        P("row", "col", None),
        P("col", "row", None),
        P("col", "row", None),
    )
    out_specs = specs[:3] + specs[4:]
    return jax.shard_map(body, mesh=mesh, in_specs=specs, out_specs=out_specs, check_vma=False)
```

profile of v0, /device:TPU:0, one launch (start us, length us, event | category | flops | bytes accessed | tf_op | source)
XLA Modules:
  0.0 176.4 jit_solution(4579735873885011943)
XLA Ops:
  7.2 0.0 all-gather.2.cloned.1.call-start
  7.2 1.8 %pad_maximum_fusion.1 = f32[64,1024]{1,0:T(8,128)} fusion(f32[64,512]{1,0:T(8,128)} %bitcast.27, f32[64,512]{1,0:T(8,128)} %bitcast.28), kind=kLoop, calls=%fused_computation.17 | loop fusion | flops 65536 | bytes 524288 | tf_op jit(solution)/shard_map/concatenate | solution.py:443
  9.0 0.0 all-gather.2.cloned.1.call-update
  9.0 0.0 copy-start.1
  9.0 1.2 copy-done.1
  10.2 2.0 %shard_map.135 = (bf16[896,512]{1,0:T(8,128)(2,1)S(1)}, bf16[512,384]{1,0:T(8,128)(2,1)S(1)}) custom-call(bf16[512,896]{1,0:T(8,128)(2,1)S(1)} %copy-done.1), custom_call_target="tpu_custom_call" | custom-call | tf_op jit(solution)/shard_map/pallas_call | solution.py:169
  12.2 0.0 copy-start.14
  12.2 0.9 constant_dynamic-slice_fusion.1
  13.1 0.5 collective-permute-start.4
  13.6 2.6 %collective-permute-start.9 = (bf16[256,384]{1,0:T(8,128)(2,1)S(1)}, bf16[256,384]{1,0:T(8,128)(2,1)}, u32[]{:S(2)}, u32[]{:S(2)}) collective-permute-start(bf16[256,384]{1,0:T(8,128)(2,1)S(1)} %constant_dynamic-slice_fusion), channel_id=1, source_target_pairs={{0,1},{1,0},{2,3},{3,2},{4,5},{5,4},{6,7},{7,6},{8,9},{9,8},{10,11... | collective-permute-start | bytes 589832 | tf_op jit(solution)/shard_map/ppermute | solution.py:386
  16.2 0.2 collective-permute-start.1
  16.4 0.8 slice.8
  17.2 1.9 %pad_maximum_fusion = f32[224,896]{1,0:T(8,128)} fusion(f32[224,384]{1,0:T(8,128)} %slice.8, f32[224,512]{1,0:T(8,128)S(1)} %dynamic-slice_bitcast_fusion), kind=kLoop, calls=%fused_computation.12 | loop fusion | flops 200704 | bytes 1605632 | tf_op jit(solution)/shard_map/concatenate | solution.py:424
  19.1 1.5 collective-permute-start.2
  20.6 0.0 collective-permute-done.4
  20.6 1.1 add_convert_fusion.1
  21.8 0.6 collective-permute-start.5
  22.4 0.0 collective-permute-done.9
  22.4 1.1 add_convert_fusion.4
  23.4 0.0 copy-start.2
  23.5 0.0 copy-start.21
  23.5 1.6 collective-permute-start.10
  25.1 0.0 collective-permute-start
  25.2 10.3 %collective-permute-done.10 = bf16[256,384]{1,0:T(8,128)(2,1)S(1)} collective-permute-done((bf16[256,384]{1,0:T(8,128)(2,1)S(1)}, bf16[256,384]{1,0:T(8,128)(2,1)S(1)}, u32[]{:S(2)}, u32[]{:S(2)}) %collective-permute-start.10) | collective-permute-done | bytes 196640 | tf_op jit(solution)/shard_map/ppermute | solution.py:386
  35.4 0.1 add_convert_fusion.3
  35.5 1.9 %collective-permute-start.11 = (bf16[256,384]{1,0:T(8,128)(2,1)S(1)}, bf16[256,384]{1,0:T(8,128)(2,1)S(1)}, u32[]{:S(2)}, u32[]{:S(2)}) collective-permute-start(bf16[256,384]{1,0:T(8,128)(2,1)S(1)} %add_convert_fusion.3), channel_id=1, source_target_pairs={{0,4},{1,5},{2,6},{3,7},{4,0},{5,1},{6,2},{7,3},{8,12},{9,13},{10,... | collective-permute-start | bytes 589832 | tf_op jit(solution)/shard_map/ppermute | solution.py:386
  37.4 2.8 %collective-permute-done.2.refs_5_ = f32[224,896]{1,0:T(8,128)} collective-permute-done((f32[224,896]{1,0:T(8,128)}, f32[224,896]{1,0:T(8,128)}, u32[]{:S(2)}, u32[]{:S(2)}) %collective-permute-start.2) | collective-permute-done | bytes 802848 | tf_op jit(solution)/shard_map/ppermute | solution.py:386
  40.2 0.0 collective-permute-start.3
  40.2 9.1 %collective-permute-done.5 = bf16[448,512]{1,0:T(8,128)(2,1)S(1)} collective-permute-done((bf16[448,512]{1,0:T(8,128)(2,1)S(1)}, bf16[448,512]{1,0:T(8,128)(2,1)S(1)}, u32[]{:S(2)}, u32[]{:S(2)}) %collective-permute-start.5) | collective-permute-done | bytes 458784 | tf_op jit(solution)/shard_map/ppermute | solution.py:386
  49.2 0.1 add_convert_fusion.refs_7_
  49.4 0.1 collective-permute-start.6
  49.4 2.4 %collective-permute-done.11 = bf16[256,384]{1,0:T(8,128)(2,1)S(1)} collective-permute-done((bf16[256,384]{1,0:T(8,128)(2,1)S(1)}, bf16[256,384]{1,0:T(8,128)(2,1)S(1)}, u32[]{:S(2)}, u32[]{:S(2)}) %collective-permute-start.11) | collective-permute-done | bytes 196640 | tf_op jit(solution)/shard_map/ppermute | solution.py:386
  51.9 1.6 collective-permute-start.7
  53.5 0.0 collective-permute-done.1.refs_4_.refs_5_
  53.5 0.0 collective-permute-start.8
  53.5 0.1 add_convert_fusion.2.refs_9_
  53.6 0.0 collective-permute-done.refs_2_
  53.6 3.7 %collective-permute-start.12 = (bf16[256,384]{1,0:T(8,128)(2,1)S(1)}, bf16[256,384]{1,0:T(8,128)(2,1)S(1)}, u32[]{:S(2)}, u32[]{:S(2)}) collective-permute-start(bf16[256,384]{1,0:T(8,128)(2,1)S(1)} %add_convert_fusion.2.refs_9_), channel_id=1, source_target_pairs={{0,1},{1,0},{2,3},{3,2},{4,5},{5,4},{6,7},{7,6},{8,9},{9,8},{10,11... | collective-permute-start | bytes 589832 | tf_op jit(solution)/shard_map/ppermute | solution.py:386
  57.2 1.5 multiply_add_fusion
  58.8 0.1 pad_add_fusion.refs_0_
  58.9 0.0 collective-permute-done.6.refs_8_
  58.9 0.0 collective-permute-done.3.refs_6_
  58.9 24.5 %shard_map.136 = (f32[224,896]{1,0:T(8,128)}, bf16[896,896]{1,0:T(8,128)(2,1)S(1)}, bf16[896,896]{1,0:T(8,128)(2,1)S(1)}, f32[896,384]{1,0:T(8,128)S(1)}) custom-call(s32[2]{0:T(128)S(1)} %pad_add_fusion.refs_0_, f32[224,896]{1,0:T(8,128)S(1)} %bitcast.26, f32[224,896]{1,0:T(8,128)S(1)} %collective-permute-done.refs_2_, f32[224,896]{1,0:T(8,128)S(1)} %bitcast.23, ...), custom_call_target="tpu_custom_call" | custom-call | tf_op jit(solution)/shard_map/pallas_call | solution.py:281
  83.4 1.2 copy-done.4
  84.5 1.2 copy-done.6
  85.7 1.1 copy-done.8
  86.7 0.0 collective-permute-done.12.refs_10_
  86.8 0.7 copy-done.15
  87.5 0.0 collective-permute-done.7.refs_6_
  87.5 0.8 copy-done.10
  88.2 0.0 collective-permute-done.8.refs_7_
  88.2 0.8 copy-done.12
  89.0 1.4 copy-done.5
  90.4 1.4 copy-done.7
  91.8 1.3 copy-done.9
  93.2 1.0 copy-done.11
  94.2 1.0 copy-done.13
  95.2 0.9 copy-done.16
  96.1 57.5 %shard_map.137 = (bf16[896,896]{1,0:T(8,128)(2,1)S(1)}, f32[224,896]{1,0:T(8,128)}, bf16[512,512]{1,0:T(8,128)(2,1)S(1)}, f32[64,512]{1,0:T(8,128)}, f32[64,512]{1,0:T(8,128)}) custom-call(s32[2]{0:T(128)S(1)} %pad_add_fusion.refs_0_, bf16[896,896]{1,0:T(8,128)(2,1)S(1)} %copy-done.5, bf16[896,896]{1,0:T(8,128)(2,1)S(1)} %copy-done.7, ...), custom_call_target="tpu_custom_call" | custom-call | tf_op jit(solution)/shard_map/pallas_call | solution.py:358
  153.7 1.2 copy-done.17
  154.8 0.8 copy-done.19
  155.6 5.3 %fusion = f32[512,896]{1,0:T(8,128)} fusion(f32[512,896]{1,0:T(8,128)} %param.11, bf16[896,896]{1,0:T(8,128)(2,1)} %copy-done.17, bf16[512,512]{1,0:T(8,128)(2,1)} %copy-done.19, bf16[512,896]{1,0:T(8,128)(2,1)S(1)} %copy-done.2), kind=kOutput, calls=%fused_computation.1 | convolution fusion | flops 1294139392 | bytes 6717440 | tf_op jit(solution)/shard_map/dot_general | solution.py:434
  161.0 4.0 %divide_convert_fusion = bf16[512,896]{1,0:T(8,128)(2,1)S(1)} fusion(f32[512,896]{1,0:T(8,128)} %fusion, bf16[896,896]{1,0:T(8,128)(2,1)S(1)} %copy-done.18, bf16[512,512]{1,0:T(8,128)(2,1)S(1)} %copy-done.20, f32[512,896]{1,0:T(8,128)} %multiply_add_fusion), kind=kOutput, calls=%fused_computation.3 | convolution fusion | flops 1294139392 | bytes 6717440 | tf_op jit(solution)/shard_map/dot_general | solution.py:434
  165.0 4.5 %multiply_subtract_fusion = f32[512,896]{1,0:T(8,128)} fusion(f32[512,896]{1,0:T(8,128)} %param.9, bf16[896,896]{1,0:T(8,128)(2,1)S(1)} %copy-done.18, bf16[512,512]{1,0:T(8,128)(2,1)S(1)} %copy-done.20, bf16[512,896]{1,0:T(8,128)(2,1)S(1)} %divide_convert_fusion), kind=kOutput, calls=%fused_computation.2 | convolution fusion | flops 1294139392 | bytes 6717440 | tf_op jit(solution)/shard_map/dot_general | solution.py:463
  (29 shorter events, 0.2 us)
Async XLA Ops:
  7.2 9.0 %copy-start = (f32[1,224,896]{2,1,0:T(8,128)S(1)}, f32[1,224,896]{2,1,0:T(8,128)}, u32[]{:S(2)}) copy-start(f32[1,224,896]{2,1,0:T(8,128)} %param.15) | copy-start | bytes 2408452
  7.2 81.8 %all-gather.2.cloned.1.call-start = ((), (), s32[]{:S(2)}) async-start(), calls=%async_computation | async-start | bytes 2359296 | tf_op jit(solution)/shard_map/all_gather | solution.py:442
  9.0 1.2 copy-start.1
  10.2 6.9 %copy-start.3 = (f32[1,224,896]{2,1,0:T(8,128)S(1)}, f32[1,224,896]{2,1,0:T(8,128)}, u32[]{:S(2)}) copy-start(f32[1,224,896]{2,1,0:T(8,128)} %param.14) | copy-start | bytes 2408452
  12.2 4.0 %copy-start.14 = (bf16[512,384]{1,0:T(8,128)(2,1)}, bf16[512,384]{1,0:T(8,128)(2,1)S(1)}, u32[]{:S(2)}) copy-start(bf16[512,384]{1,0:T(8,128)(2,1)S(1)} %get-tuple-element.24) | copy-start | bytes 1179652
  13.1 7.5 %collective-permute-start.4 = (bf16[448,512]{1,0:T(8,128)(2,1)}, bf16[448,512]{1,0:T(8,128)(2,1)}, u32[]{:S(2)}, u32[]{:S(2)}) collective-permute-start(bf16[448,512]{1,0:T(8,128)(2,1)} %constant_dynamic-slice_fusion.1), channel_id=1, source_target_pairs={{0,8},{8,0},{16,24},{24,16},{1,9},{9,1},{17,25},{25,17},{2,10},{10... | collective-permute-start | bytes 1376264 | tf_op jit(solution)/shard_map/ppermute | solution.py:386
  13.6 8.8 %collective-permute-start.9 = (bf16[256,384]{1,0:T(8,128)(2,1)S(1)}, bf16[256,384]{1,0:T(8,128)(2,1)}, u32[]{:S(2)}, u32[]{:S(2)}) collective-permute-start(bf16[256,384]{1,0:T(8,128)(2,1)S(1)} %constant_dynamic-slice_fusion), channel_id=1, source_target_pairs={{0,1},{1,0},{2,3},{3,2},{4,5},{5,4},{6,7},{7,6},{8,9},{9,8},{10,11... | collective-permute-start | bytes 589832 | tf_op jit(solution)/shard_map/ppermute | solution.py:386
  16.2 37.4 %collective-permute-start.1 = (f32[224,896]{1,0:T(8,128)S(1)}, f32[224,896]{1,0:T(8,128)S(1)}, u32[]{:S(2)}, u32[]{:S(2)}) collective-permute-start(f32[224,896]{1,0:T(8,128)S(1)} %bitcast.20), channel_id=1, source_target_pairs={{0,8},{8,0},{16,24},{24,16},{1,9},{9,1},{17,25},{25,17},{2,10},{10... | collective-permute-start | bytes 2408456 | tf_op jit(solution)/shard_map/ppermute | solution.py:386
  19.1 21.0 %collective-permute-start.2 = (f32[224,896]{1,0:T(8,128)}, f32[224,896]{1,0:T(8,128)}, u32[]{:S(2)}, u32[]{:S(2)}) collective-permute-start(f32[224,896]{1,0:T(8,128)} %pad_maximum_fusion), channel_id=1, source_target_pairs={{0,16},{8,24},{16,0},{24,8},{1,17},{9,25},{17,1},{25,9},{2,18},{10... | collective-permute-start | bytes 2408456 | tf_op jit(solution)/shard_map/ppermute | solution.py:386
  21.8 27.5 %collective-permute-start.5 = (bf16[448,512]{1,0:T(8,128)(2,1)S(1)}, bf16[448,512]{1,0:T(8,128)(2,1)S(1)}, u32[]{:S(2)}, u32[]{:S(2)}) collective-permute-start(bf16[448,512]{1,0:T(8,128)(2,1)S(1)} %add_convert_fusion.1), channel_id=1, source_target_pairs={{0,16},{8,24},{16,0},{24,8},{1,17},{9,25},{17,1},{25,9},{2,18},{10... | collective-permute-start | bytes 1376264 | tf_op jit(solution)/shard_map/ppermute | solution.py:386
  23.4 33.8 %copy-start.2 = (bf16[512,896]{1,0:T(8,128)(2,1)S(1)}, bf16[512,896]{1,0:T(8,128)(2,1)}, u32[]{:S(2)}) copy-start(bf16[512,896]{1,0:T(8,128)(2,1)} %grad_ref.1) | copy-start | bytes 2752516
  23.5 33.8 %copy-start.21 = (f32[512,896]{1,0:T(8,128)S(1)}, f32[512,896]{1,0:T(8,128)}, u32[]{:S(2)}) copy-start(f32[512,896]{1,0:T(8,128)} %param.10) | copy-start | bytes 5505028
  23.5 12.0 %collective-permute-start.10 = (bf16[256,384]{1,0:T(8,128)(2,1)S(1)}, bf16[256,384]{1,0:T(8,128)(2,1)S(1)}, u32[]{:S(2)}, u32[]{:S(2)}) collective-permute-start(bf16[256,384]{1,0:T(8,128)(2,1)S(1)} %add_convert_fusion.4), channel_id=1, source_target_pairs={{0,2},{1,3},{2,0},{3,1},{4,6},{5,7},{6,4},{7,5},{8,10},{9,11},{10,... | collective-permute-start | bytes 589832 | tf_op jit(solution)/shard_map/ppermute | solution.py:386
  25.1 28.5 %collective-permute-start = (f32[224,896]{1,0:T(8,128)S(1)}, f32[224,896]{1,0:T(8,128)S(1)}, u32[]{:S(2)}, u32[]{:S(2)}) collective-permute-start(f32[224,896]{1,0:T(8,128)S(1)} %bitcast.25), channel_id=1, source_target_pairs={{0,8},{8,0},{16,24},{24,16},{1,9},{9,1},{17,25},{25,17},{2,10},{10... | collective-permute-start | bytes 2408456 | tf_op jit(solution)/shard_map/ppermute | solution.py:386
  35.5 16.4 %collective-permute-start.11 = (bf16[256,384]{1,0:T(8,128)(2,1)S(1)}, bf16[256,384]{1,0:T(8,128)(2,1)S(1)}, u32[]{:S(2)}, u32[]{:S(2)}) collective-permute-start(bf16[256,384]{1,0:T(8,128)(2,1)S(1)} %add_convert_fusion.3), channel_id=1, source_target_pairs={{0,4},{1,5},{2,6},{3,7},{4,0},{5,1},{6,2},{7,3},{8,12},{9,13},{10,... | collective-permute-start | bytes 589832 | tf_op jit(solution)/shard_map/ppermute | solution.py:386
  40.2 18.7 %collective-permute-start.3 = (f32[224,896]{1,0:T(8,128)}, f32[224,896]{1,0:T(8,128)S(1)}, u32[]{:S(2)}, u32[]{:S(2)}) collective-permute-start(f32[224,896]{1,0:T(8,128)} %collective-permute-done.2.refs_5_), channel_id=1, source_target_pairs={{0,8},{8,0},{16,24},{24,16},{1,9},{9,1},{17,25},{25,17},{2,10},{10... | collective-permute-start | bytes 2408456 | tf_op jit(solution)/shard_map/ppermute | solution.py:386
  49.4 9.5 %collective-permute-start.6 = (bf16[448,512]{1,0:T(8,128)(2,1)S(1)}, bf16[448,512]{1,0:T(8,128)(2,1)S(1)}, u32[]{:S(2)}, u32[]{:S(2)}) collective-permute-start(bf16[448,512]{1,0:T(8,128)(2,1)S(1)} %add_convert_fusion.refs_7_), channel_id=1, source_target_pairs={{0,8},{8,0},{16,24},{24,16},{1,9},{9,1},{17,25},{25,17},{2,10},{10... | collective-permute-start | bytes 1376264 | tf_op jit(solution)/shard_map/ppermute | solution.py:386
  51.9 35.6 %collective-permute-start.7 = (f32[224,512]{1,0:T(8,128)S(1)}, f32[224,512]{1,0:T(8,128)S(1)}, u32[]{:S(2)}, u32[]{:S(2)}) collective-permute-start(f32[224,512]{1,0:T(8,128)S(1)} %slice.9), channel_id=1, source_target_pairs={{0,16},{8,24},{16,0},{24,8},{1,17},{9,25},{17,1},{25,9},{2,18},{10... | collective-permute-start | bytes 1376264 | tf_op jit(solution)/shard_map/ppermute | solution.py:386
  53.5 34.7 %collective-permute-start.8 = (f32[224,512]{1,0:T(8,128)S(1)}, f32[224,512]{1,0:T(8,128)S(1)}, u32[]{:S(2)}, u32[]{:S(2)}) collective-permute-start(f32[224,512]{1,0:T(8,128)S(1)} %slice.9), channel_id=1, source_target_pairs={{0,24},{8,16},{16,8},{24,0},{1,25},{9,17},{17,9},{25,1},{2,26},{10... | collective-permute-start | bytes 1376264 | tf_op jit(solution)/shard_map/ppermute | solution.py:386
  53.6 33.2 %collective-permute-start.12 = (bf16[256,384]{1,0:T(8,128)(2,1)S(1)}, bf16[256,384]{1,0:T(8,128)(2,1)S(1)}, u32[]{:S(2)}, u32[]{:S(2)}) collective-permute-start(bf16[256,384]{1,0:T(8,128)(2,1)S(1)} %add_convert_fusion.2.refs_9_), channel_id=1, source_target_pairs={{0,1},{1,0},{2,3},{3,2},{4,5},{5,4},{6,7},{7,6},{8,9},{9,8},{10,11... | collective-permute-start | bytes 589832 | tf_op jit(solution)/shard_map/ppermute | solution.py:386
  83.4 1.2 copy-start.4
  84.5 1.2 copy-start.6
  85.7 1.1 copy-start.8
  86.8 0.7 copy-start.15
  87.5 0.8 copy-start.10
  88.2 0.8 copy-start.12
  89.0 1.4 copy-start.5
  90.4 1.4 copy-start.7
  91.8 1.3 copy-start.9
  93.2 1.0 copy-start.11
  94.2 1.0 copy-start.13
  95.2 0.9 copy-start.16
  153.7 1.2 copy-start.17
  154.8 0.8 copy-start.19
  155.6 5.3 %copy-start.18 = (bf16[896,896]{1,0:T(8,128)(2,1)S(1)}, bf16[896,896]{1,0:T(8,128)(2,1)}, u32[]{:S(2)}) copy-start(bf16[896,896]{1,0:T(8,128)(2,1)} %copy-done.17) | copy-start | bytes 4816900
  155.6 5.3 %copy-start.20 = (bf16[512,512]{1,0:T(8,128)(2,1)S(1)}, bf16[512,512]{1,0:T(8,128)(2,1)}, u32[]{:S(2)}) copy-start(bf16[512,512]{1,0:T(8,128)(2,1)} %copy-done.19) | copy-start | bytes 1572868
Sparse Core Ops, SparseCore 0:
  10.1 55.2 all-gather.1
where the time goes:
time: 177 us; the launch traced here: 176 us
  Pallas kernels  84 us (47%)
  waiting for transfers between devices  24.6 us (14%)
  local copies, waits for them, and re-layouts  17.7 us (10%)
  starting transfers between devices  14.3 us (8%)
  between operations  14.2 us (8%)
  matrix products  13.9 us (8%)
  other arithmetic  7.74 us (4%)
    pallas_call x1, Pallas kernels, rest(): pl.pallas_call(functools.partial(rest_kernel, *[[d for d, _ in group] for...  57.5 us
    ppermute x13, waiting for transfers between devices, swap(): return lax.ppermute(x, axis, [(i, i ^ distance) for i in range(count)])  24.6 us
    pallas_call x1, Pallas kernels, head(): pl.pallas_call(functools.partial(head_kernel, count, *[[d for d, _ in gro...  24.5 us
    unnamed x44, local copies, waits for them, and re-layouts  15.9 us
    ppermute x13, starting transfers between devices, swap(): return lax.ppermute(x, axis, [(i, i ^ distance) for i in range(count)])  14.3 us
    dot_general x2, matrix products, rotate_in(): jnp.dot(inner.astype(jnp.bfloat16), right_half, preferred_element_type=jn...  9.33 us
    dot_general x1, matrix products, body(): lax.dot_general(turned, right_half, (((1,), (1,)), ((), ())), preferred_e...  4.53 us
  transfers between devices with their start and end apart: 14, of which 4 were waited for; matrix products, arithmetic and copies ran while one was open for 4% of the time, Pallas kernels for 15%

commit v1 on v0

v1 whole, which is shorter than its diff:
```python
import functools
import jax
import jax.numpy as jnp
from jax import lax
from jax.experimental import pallas as pl
from jax.experimental.pallas import tpu as pltpu
from jax.sharding import PartitionSpec as P

STAT_DECAY = 0.95
FIRST_DECAY = 0.9
SECOND_DECAY = 0.95
EPSILON = 1e-08
STEP_SIZE = 0.02
WEIGHT_DECAY = 0.01
LANES = 128
ROWS = 8
VMEM_LIMIT = 56 * 2**20


def sub_row(x, k):
    return jnp.broadcast_to(x[k : k + 1, :], (ROWS, LANES))


def lane_col(x, c):
    return jnp.broadcast_to(x[:, c : c + 1], (ROWS, LANES))


def reciprocal(p):
    guess = pl.reciprocal(p, approx=True)
    return guess * (2.0 - p * guess)


def inverse_factor(rows):
    count = LANES // ROWS
    rows = list(rows)
    subs = lax.broadcasted_iota(jnp.int32, (ROWS, LANES), 0)
    lanes = lax.broadcasted_iota(jnp.int32, (ROWS, LANES), 1)
    out = []
    for s in range(count):
        base = s * ROWS
        pivot = rows[s]
        here = (lanes >= base) & (lanes < base + ROWS)
        cols = [lane_col(pivot, base + k) for k in range(ROWS)]
        full = jnp.where(here, (lanes == subs + base).astype(jnp.float32), pivot)
        forward = full
        inverse = jnp.zeros((ROWS, LANES), jnp.float32)
        pivots = jnp.ones((ROWS, LANES), jnp.float32)
        yield
        for j in range(ROWS):
            value = sub_row(cols[j], j)
            inv = reciprocal(value)
            scaled = cols[j] * inv
            m_full = jnp.where(subs == j, 0.0, scaled)
            for k in range(j + 1, ROWS):
                cols[k] = cols[k] - m_full * sub_row(cols[k], j)
            row = sub_row(full, j)
            if j < ROWS - 1:
                forward = forward - jnp.where(subs > j, scaled, 0.0) * sub_row(forward, j)
            full = full - m_full * row
            inverse = jnp.where(subs == j, inv, inverse)
            pivots = jnp.where(subs == j, value, pivots)
            yield
        out.append(jnp.where(lanes < base + ROWS, forward * lax.rsqrt(pivots), 0.0))
        full = full * inverse
        if s < count - 1:
            spread = [sub_row(full, k) for k in range(ROWS)]
            for i in range(s + 1, count):
                coeffs = [lane_col(rows[i], base + k) for k in range(ROWS)]
                terms = [coeffs[k] * spread[k] for k in range(ROWS)]
                while len(terms) > 1:
                    terms = [a + b for a, b in zip(terms[::2], terms[1::2])]
                rows[i] = jnp.where(here, 0.0, rows[i]) - terms[0]
                yield
    return out


def in_turns(generators, fills):
    results = [None] * len(generators)
    live = list(enumerate(generators))
    fills = list(fills)
    total, turn, done = 250, 0, 0
    while live:
        for at, generator in list(live):
            try:
                next(generator)
            except StopIteration as stop:
                results[at] = stop.value
                live.remove((at, generator))
        turn += 1
        while done < len(fills) and done * total <= turn * len(fills):
            fills[done]()
            done += 1
    for fill in fills[done:]:
        fill()
    return results


def split(x):
    hi = x.astype(jnp.bfloat16)
    return hi, (x - hi.astype(jnp.float32)).astype(jnp.bfloat16)


def stack_left(x, axis):
    hi, lo = split(x)
    return jnp.concatenate([hi, hi, lo], axis=axis)


def stack_right(x, axis):
    hi, lo = split(x)
    return jnp.concatenate([hi, lo, hi], axis=axis)


def mm(a, b, dims):
    return lax.dot_general(a, b, (dims, ((), ())), preferred_element_type=jnp.float32)


def mm_nn(a, b):
    return mm(stack_left(a, 1), stack_right(b, 0), ((1,), (0,)))


def mm_nt(a, b):
    return mm(stack_left(a, 1), stack_right(b, 1), ((1,), (1,)))


def product(ah, al, bh, bl, dims):
    return mm(ah, bh, dims) + (mm(ah, bl, dims) + mm(al, bh, dims))


def block(i):
    return pl.ds(i * LANES, LANES) if isinstance(i, int) else pl.ds(pl.multiple_of(i * LANES, LANES), LANES)


class Chain:
    def __init__(self, z_ref, w_ref, q_ref):
        self.z, self.w, self.q = z_ref, w_ref, q_ref
        self.width = z_ref.shape[1]
        self.blocks = self.width // LANES

    def cross(self):
        hi, lo = split(self.z[self.width :, :])
        dims = ((0,), (0,))
        self.z[: self.width, :] = product(hi, lo, hi, lo, dims)
        self.w[...] = jnp.zeros_like(self.w)

    def look(self, j):
        self.before = block(lax.max(j - 1, 0))
        self.w_nt = stack_right(self.w[...], 1)
        at = block(j)
        low = mm(stack_left(self.z[at, self.before], 1), self.w_nt, ((1,), (1,)))
        diagonal = self.z[at, at] - mm_nt(low, low)
        return [diagonal[i * ROWS : (i + 1) * ROWS, :] for i in range(LANES // ROWS)]

    def fills(self):
        def rows_of_u():
            self.u = stack_right(mm_nn(self.w[...], self.z[self.before, :]), 0)

        def rows(i):
            at = block(i)
            p = mm(stack_left(self.z[at, self.before], 1), self.w_nt, ((1,), (1,)))
            if i >= self.blocks:
                self.q[block(i - self.blocks), self.before] = p
            self.z[at, :] -= mm(stack_left(p, 1), self.u, ((1,), (0,)))

        return [rows_of_u] + [functools.partial(rows, i) for i in range(self.z.shape[0] // LANES)]

    def store(self, out):
        for i, row in enumerate(out):
            self.w[i * ROWS : (i + 1) * ROWS, :] = row

    def finish(self):
        last = block(self.blocks - 1)
        self.q[:, last] = mm_nt(self.z[self.width :, last], self.w[...])


def run_chains(chains):
    def step_of(members):
        def step(j, carry):
            rows = [chain.look(j) for chain in members]
            fills = [fill for chain in members for fill in chain.fills()]
            for chain, out in zip(members, in_turns([inverse_factor(r) for r in rows], fills)):
                chain.store(out)
            return carry

        return step

    start = 0
    for end in sorted({chain.blocks for chain in chains}):
        lax.fori_loop(start, end, step_of([chain for chain in chains if chain.blocks >= end]), 0)
        start = end
    for chain in chains:
        chain.finish()


class Copies:
    def __init__(self, semaphores):
        self.semaphores, self.used = semaphores, 0

    def start(self, source, target):
        copy = pltpu.make_async_copy(source, target, self.semaphores.at[self.used])
        self.used += 1
        copy.start()
        return copy


def wait(copies):
    for copy in copies:
        copy.wait()


def offsets(size):
    return size // LANES // 2 + 1


def pack_products(cols, out_ref, dims, scale):
    blocks = len(cols)
    for i in range(blocks):
        for o in range(offsets(blocks * LANES)):
            term = mm(cols[i], cols[(i + o) % blocks], dims)
            out_ref[block(i), block(o)] = (term * scale).astype(out_ref.dtype)


def terms_kernel(scale_left, scale_right, grad_ref, right_ref, left_ref):
    rows, columns = grad_ref.shape
    pack_products([grad_ref[:, block(i)] for i in range(columns // LANES)], right_ref, ((0,), (0,)), scale_right)
    pack_products([grad_ref[block(i), :] for i in range(rows // LANES)], left_ref, ((1,), (1,)), scale_left)


def terms(grad, scale_left, scale_right):
    rows, columns = grad.shape
    return pl.pallas_call(
        functools.partial(terms_kernel, scale_left, scale_right),
        out_shape=[
            jax.ShapeDtypeStruct((columns, offsets(columns) * LANES), jnp.bfloat16),
            jax.ShapeDtypeStruct((rows, offsets(rows) * LANES), jnp.bfloat16),
        ],
        compiler_params=pltpu.CompilerParams(vmem_limit_bytes=VMEM_LIMIT),
    )(grad)


def rows_at(me, distance, rows):
    return pl.ds(pl.multiple_of((me ^ distance) * rows, ROWS), rows)


def new_gram(gram_ref, packed_ref, gh_ref, gl_ref):
    blocks = gram_ref.shape[0] // LANES
    count = offsets(gram_ref.shape[0])

    def put(i, k, term):
        value = gram_ref[block(i), block(k)] * STAT_DECAY + term
        gram_ref[block(i), block(k)] = value
        gh_ref[block(i), block(k)], gl_ref[block(i), block(k)] = split(value)

    for i in range(blocks):
        for o in range(count):
            k = (i + o) % blocks
            term = packed_ref[block(i), block(o)].astype(jnp.float32) * (1.0 - STAT_DECAY)
            put(i, k, term)
            if o > 0 and not (blocks % 2 == 0 and o == count - 1):
                put(k, i, term.T)


def image(z_ref, gh_ref, gl_ref, basis_ref):
    width = z_ref.shape[1]
    bh, bl = split(basis_ref[...])
    for i in range(gh_ref.shape[0] // LANES):
        z_ref[pl.ds(width + i * LANES, LANES), :] = product(
            gh_ref[block(i), :], gl_ref[block(i), :], bh, bl, ((1,), (0,))
        )


def own_rows(ref, me, rows):
    return ref[pl.ds(pl.multiple_of(me * rows, ROWS), rows), :]


def half_window(size):
    return -(-size // 2 // LANES) * LANES


def fill_halves(gram, half):
    size = gram.shape[0]
    window = half_window(size)
    rest = size - window
    near = half * window
    far = pl.ds(pl.multiple_of((1 - half) * rest, LANES), window)
    for i in range(rest // LANES):
        at = pl.ds(pl.multiple_of(near + i * LANES, LANES), LANES)
        gram[far, at] = gram[at, far].T


def packed_copies(copies, me, sums, packed):
    side = lax.rem(me, 2) if len(sums) > 1 else 0
    return [copies.start(piece, packed.at[rows_at(side, d, piece.shape[0]), :]) for d, piece in sums]


def take(refs, distances_of):
    return [(d, refs.pop(0)) for d in distances_of]


def head_kernel(count, owns, others, sums, *refs):
    me_ref, refs = refs[0], list(refs[1:])
    gram_in, basis_in, other_in, sum_in = take(refs, owns), take(refs, owns), take(refs, others), take(refs, sums)
    rows_ref, gh_ref, gl_ref, q_ref, gram, packed, basis, gh, gl, rows_own, z, w, semaphores = refs
    me = me_ref[0]
    copies = Copies(semaphores)
    width = basis.shape[1]
    half = lax.div(2 * me, count)
    window = half_window(gram.shape[0])
    others_at = pl.ds(pl.multiple_of((1 - half) * (gram.shape[0] - window), LANES), window)
    first, second = [], []
    for d, piece in gram_in:
        first.append(copies.start(piece, gram.at[rows_at(me, d, piece.shape[0]), :]))
    for d, piece in other_in:
        at = rows_at(me, d, piece.shape[0])
        first.append(copies.start(piece.at[:, pl.ds(0, window)], gram.at[at, others_at]))
    first += packed_copies(copies, me, sum_in, packed)
    for d, piece in basis_in:
        at = rows_at(me, d, piece.shape[0])
        second.append(copies.start(piece.at[:, pl.ds(0, width)], basis.at[at, :]))
    for d, piece in other_in:
        at = rows_at(me, d, piece.shape[0])
        second.append(copies.start(piece.at[:, pl.ds(window, width)], basis.at[at, :]))
    wait(first)
    if other_in:
        fill_halves(gram, half)
    new_gram(gram, packed, gh, gl)
    rows_own[...] = own_rows(gram, me, rows_own.shape[0])
    out = [copies.start(gh, gh_ref), copies.start(gl, gl_ref), copies.start(rows_own, rows_ref)]
    wait(second)
    image(z, gh, gl, basis)
    chain = Chain(z, w, q_ref)
    chain.cross()
    run_chains([chain])
    wait(out)


def any_specs(count):
    return [pl.BlockSpec(memory_space=pltpu.SMEM)] + [pl.BlockSpec(memory_space=pl.ANY)] * count


def chain_scratch(width, rows):
    return [pltpu.VMEM((width + rows, width), jnp.float32), pltpu.VMEM((LANES, LANES), jnp.float32)]


def head(me, count, grams, bases, others, sums, width):
    args = [p for group in (grams, bases, others, sums) for _, p in group]
    rows, size = grams[0][1].shape
    f32, bf16 = jnp.float32, jnp.bfloat16
    return pl.pallas_call(
        functools.partial(head_kernel, count, *[[d for d, _ in group] for group in (grams, others, sums)]),
        out_shape=[
            jax.ShapeDtypeStruct((rows, size), f32),
            jax.ShapeDtypeStruct((size, size), bf16),
            jax.ShapeDtypeStruct((size, size), bf16),
            jax.ShapeDtypeStruct((size, width), f32),
        ],
        in_specs=any_specs(len(args)),
        out_specs=[pl.BlockSpec(memory_space=pl.ANY)] * 3 + [pl.BlockSpec(memory_space=pltpu.VMEM)],
        scratch_shapes=[
            pltpu.VMEM((size, size), f32),
            pltpu.VMEM((size, offsets(size) * LANES), bf16),
            pltpu.VMEM((size, width), f32),
            pltpu.VMEM((size, size), bf16),
            pltpu.VMEM((size, size), bf16),
            pltpu.VMEM((rows, size), f32),
            *chain_scratch(width, size),
            pltpu.SemaphoreType.DMA((len(args) + len(others) + 3,)),
        ],
        compiler_params=pltpu.CompilerParams(vmem_limit_bytes=VMEM_LIMIT),
    )(me, *args)


def rest_kernel(bases, others, sums, *refs):
    me_ref, refs = refs[0], list(refs[1:])
    gh_in, gl_in, q_in, grad_in, weight_in, moment_in, second_in, gram_in, left_in = refs[:9]
    refs = refs[9:]
    basis_in, other_in, sum_in = take(refs, bases), take(refs, others), take(refs, sums)
    weight_out, moment_out, second_out, right_rows, left_rows, gram_rows = refs[:6]
    (gh, gl, q_first, basis, qr, ql, gram_l, packed_l, basis_l, glh, gll, zr, wr, zl, wl) = refs[6:21]
    (grad, weight, moment, second, inner, turn, right_half, left_half, semaphores) = refs[21:]
    row, col = me_ref[0], me_ref[1]
    copies = Copies(semaphores)
    first = q_first.shape[1]
    width = zr.shape[1]
    start = [copies.start(gh_in, gh), copies.start(gl_in, gl)]
    for d, piece in basis_in:
        at = rows_at(row, d, piece.shape[0])
        start.append(copies.start(piece.at[:, pl.ds(first, width)], basis.at[at, :]))
    for d, piece in other_in:
        start.append(copies.start(piece, basis.at[rows_at(row, d, piece.shape[0]), :]))
    project = [copies.start(q_in, q_first)]
    lefts = packed_copies(copies, col, sum_in, packed_l)
    lefts += [copies.start(gram_in, gram_l), copies.start(left_in, basis_l)]
    tail = [copies.start(grad_in, grad), copies.start(moment_in, moment)]
    late = [copies.start(second_in, second), copies.start(weight_in, weight)]

    wait(start)
    image(zr, gh, gl, basis)
    wait(project)
    qh, qo = split(q_first[...])
    xh, xl = split(zr[width:, :])
    sh, sl = split(product(qh, qo, xh, xl, ((0,), (0,))))
    zr[width:, :] -= product(qh, qo, sh, sl, ((1,), (0,)))
    wait(lefts)
    new_gram(gram_l, packed_l, glh, gll)
    gram_rows[...] = own_rows(gram_l, col, gram_rows.shape[0])
    image(zl, glh, gll, basis_l)
    right, left = Chain(zr, wr, qr), Chain(zl, wl, ql)
    right.cross()
    left.cross()
    right_half[:, :first] = q_first[...].astype(jnp.bfloat16)
    wait(tail)
    for i in range(grad.shape[0] // LANES):
        moment[block(i), :] = FIRST_DECAY * moment[block(i), :] + (1.0 - FIRST_DECAY) * grad[block(i), :].astype(
            jnp.float32
        )
    out = [copies.start(moment, moment_out)]
    run_chains([left, right] if left.blocks <= right.blocks else [right, left])
    left_half[...] = ql[...].astype(jnp.bfloat16)
    right_half[:, first:] = qr[...].astype(jnp.bfloat16)
    right_rows[:, :first] = own_rows(q_first, row, right_rows.shape[0])
    right_rows[:, first:] = own_rows(qr, row, right_rows.shape[0])
    left_rows[...] = own_rows(ql, col, left_rows.shape[0])

    wait(late)
    blocks = grad.shape[0] // LANES
    for i in range(blocks):
        part = left_half[:, block(i)]
        both = [grad[...], moment[...].astype(jnp.bfloat16)]
        for n, matrix in enumerate(both):
            inner[pl.ds(n * grad.shape[0] + i * LANES, LANES), :] = mm(part, matrix, ((0,), (0,))).astype(jnp.bfloat16)
    for i in range(blocks):
        rotated_grad = mm(inner[block(i), :], right_half[...], ((1,), (0,)))
        rotated_moment = mm(inner[pl.ds(grad.shape[0] + i * LANES, LANES), :], right_half[...], ((1,), (0,)))
        new_second = SECOND_DECAY * second[block(i), :] + (1.0 - SECOND_DECAY) * rotated_grad * rotated_grad
        second[block(i), :] = new_second
        out.append(copies.start(second.at[block(i), :], second_out.at[block(i), :]))
        turn[block(i), :] = (rotated_moment / (jnp.sqrt(new_second) + EPSILON)).astype(jnp.bfloat16)
    for i in range(blocks):
        turned = mm(left_half[block(i), :], turn[...], ((1,), (0,))).astype(jnp.bfloat16)
        update = mm(turned, right_half[...], ((1,), (1,)))
        old = weight[block(i), :]
        weight[block(i), :] = old - STEP_SIZE * (update + WEIGHT_DECAY * old)
        out.append(copies.start(weight.at[block(i), :], weight_out.at[block(i), :]))
    wait(out)


def rest(me, gh, gl, q_first, tiles, bases, others, left, sums, rows_l):
    args = [gh, gl, q_first, *tiles, *left] + [p for group in (bases, others, sums) for _, p in group]
    rows_r, size_r = bases[0][1].shape
    width = size_r - q_first.shape[1]
    size_l = left[0].shape[0]
    tile = tiles[0].shape
    f32, bf16 = jnp.float32, jnp.bfloat16
    vmem, anywhere = pl.BlockSpec(memory_space=pltpu.VMEM), pl.BlockSpec(memory_space=pl.ANY)
    return pl.pallas_call(
        functools.partial(rest_kernel, *[[d for d, _ in group] for group in (bases, others, sums)]),
        out_shape=[
            jax.ShapeDtypeStruct(tile, f32),
            jax.ShapeDtypeStruct(tile, f32),
            jax.ShapeDtypeStruct(tile, f32),
            jax.ShapeDtypeStruct((rows_r, size_r), f32),
            jax.ShapeDtypeStruct((rows_l, size_l), f32),
            jax.ShapeDtypeStruct((rows_l, size_l), f32),
        ],
        in_specs=any_specs(len(args)),
        out_specs=[anywhere] * 3 + [vmem] * 3,
        scratch_shapes=[
            pltpu.VMEM((size_r, size_r), bf16),
            pltpu.VMEM((size_r, size_r), bf16),
            pltpu.VMEM((size_r, size_r - width), f32),
            pltpu.VMEM((size_r, width), f32),
            pltpu.VMEM((size_r, width), f32),
            pltpu.VMEM((size_l, size_l), f32),
            pltpu.VMEM((size_l, size_l), f32),
            pltpu.VMEM((size_l, offsets(size_l) * LANES), bf16),
            pltpu.VMEM((size_l, size_l), f32),
            pltpu.VMEM((size_l, size_l), bf16),
            pltpu.VMEM((size_l, size_l), bf16),
            *chain_scratch(width, size_r),
            *chain_scratch(size_l, size_l),
            pltpu.VMEM(tile, bf16),
            pltpu.VMEM(tile, f32),
            pltpu.VMEM(tile, f32),
            pltpu.VMEM(tile, f32),
            pltpu.VMEM((2 * tile[0], tile[1]), bf16),
            pltpu.VMEM(tile, bf16),
            pltpu.VMEM((size_r, size_r), bf16),
            pltpu.VMEM((size_l, size_l), bf16),
            pltpu.SemaphoreType.DMA((len(args) + 1 + 2 * (tile[0] // LANES),)),
        ],
        compiler_params=pltpu.CompilerParams(vmem_limit_bytes=VMEM_LIMIT),
    )(me, *args)


def swap(x, axis, distance):
    count = lax.axis_size(axis)
    return lax.ppermute(x, axis, [(i, i ^ distance) for i in range(count)])


def distances(axis):
    count = lax.axis_size(axis)
    return [1 << b for b in range(count.bit_length() - 1)]


def spread(held, axis, steps):
    for distance in steps:
        held = held + [(at ^ distance, swap(piece, axis, distance)) for at, piece in held]
    return held


def sum_halves(x, axis):
    me, kind = lax.axis_index(axis), x.dtype
    if lax.axis_size(axis) == 1:
        return x, [(0, x)]
    rows = x.shape[0] // 2
    own = lax.rem(me, 2)
    keep = lax.dynamic_slice_in_dim(x, own * rows, rows, 0)
    other = lax.dynamic_slice_in_dim(x, (1 - own) * rows, rows, 0)
    total = keep.astype(jnp.float32) + swap(other, axis, 1).astype(jnp.float32)
    for distance in distances(axis)[1:]:
        total = total.astype(kind)
        total = total.astype(jnp.float32) + swap(total, axis, distance).astype(jnp.float32)
    total = total.astype(kind)
    return total, [(0, total), (1, swap(total, axis, 1))]


def gather_right(gram, basis, width):
    count = lax.axis_size("row")
    grams, bases = [(0, gram)], [(0, basis)]
    if count == 1:
        return grams, bases, [], gram
    window = half_window(gram.shape[1])
    half = lax.div(2 * lax.axis_index("row"), count)
    mine = lax.dynamic_slice_in_dim(gram, half * (gram.shape[1] - window), window, 1)
    mine = jnp.concatenate([mine, basis[:, :width]], axis=1)
    others = [(count // 2, swap(mine, "row", count // 2))]
    near = distances("row")[-2::-1]
    return spread(grams, "row", near), spread(bases, "row", near), spread(others, "row", near), mine


def body(grad, weight, moment, second, gram_left, basis_left, gram_right, basis_right):
    block_left, block_right = grad.shape
    first = max(block_right - block_left, LANES)
    count = lax.axis_size("row")
    me = jnp.stack([lax.axis_index("row"), lax.axis_index("col")])
    left = [lax.all_gather(x[0], "col", axis=0, tiled=True) for x in (gram_left, basis_left)]
    grams, bases, others, mine = gather_right(gram_right[0], basis_right[0], first)
    grad_after, _ = lax.optimization_barrier((grad, mine))
    terms_right, terms_left = terms(
        grad_after, 1.0 / (block_right * lax.axis_size("col")), 1.0 / (block_left * count)
    )
    sent, sums_right = sum_halves(terms_right, "row")
    _, sums_left = sum_halves(terms_left, "col")
    last, _ = lax.optimization_barrier((basis_right[0][:, first:], sent))
    last = [(d, swap(last, "row", d)) for d in range(count // 2, count)] if count > 1 else []
    new_gram_right, gh, gl, q_first = head(me, count, grams, bases, others, sums_right, first)
    new_weight, new_moment, new_second, basis_rows_right, basis_rows_left, new_gram_left = rest(
        me, gh, gl, q_first, (grad, weight, moment, second), bases, last, left, sums_left, gram_left.shape[1]
    )
    return (
        new_weight,
        new_moment,
        new_second,
        new_gram_left[None],
        basis_rows_left[None],
        new_gram_right[None],
        basis_rows_right[None],
    )


def solution(mesh):
    specs = (
        P("row", "col"),
        P("row", "col"),
        P("row", "col"),
        P("row", "col"),
        P("row", "col", None),
        P("row", "col", None),
        P("col", "row", None),
        P("col", "row", None),
    )
    out_specs = specs[:3] + specs[4:]
    return jax.shard_map(body, mesh=mesh, in_specs=specs, out_specs=out_specs, check_vma=False)
```

time: 177 us -> 159 us (0.90)
  matrix products: 13.9 us -> 0 us
  waiting for transfers between devices: 24.6 us -> 37.5 us
  local copies, waits for them, and re-layouts: 17.7 us -> 6.6 us
  other arithmetic: 7.74 us -> 3.21 us
    unnamed x44 -> x22, local copies, waits for them, and re-layouts: 15.9 us -> 1.66 us
    dot_general x3 -> x0, matrix products: 13.9 us -> none  [the longest x2 9.33 us: rotate_in(): jnp.dot(inner.astype(jnp.bfloat16), right_half, preferred_element_type=jn...]
    all_gather x1 -> x2, waiting for transfers between devices: 0.01 us -> 7.86 us  [body(): lax.all_gather(x[0], 'col', axis=0, tiled=True)]
    pallas_call x1, Pallas kernels: 57.5 us -> 51 us  [rest(): pl.pallas_call(functools.partial(rest_kernel, *[[d for d, _ in group] for...]
    ppermute x13, waiting for transfers between devices: 24.6 us -> 29 us  [swap(): return lax.ppermute(x, axis, [(i, i ^ distance) for i in range(count)])]
    pallas_call x1, Pallas kernels: 24.5 us -> 28 us  [head(): pl.pallas_call(functools.partial(head_kernel, count, *[[d for d, _ in gro...]
    pallas_call x1, Pallas kernels: 1.97 us -> 3.96 us  [terms(): pl.pallas_call(functools.partial(terms_kernel, scale_left, scale_right),...]
    dynamic_slice x2, local copies, waits for them, and re-layouts: 0.91 us -> 2.84 us  [sum_halves(): other = lax.dynamic_slice_in_dim(x, (1 - own) * rows, rows, 0)]
  transfers between devices with their start and end apart: 14 -> 15, of which waited for: 4 -> 5; matrix products, arithmetic and copies ran while one was open for 4% -> 5% of each run, Pallas kernels for 15% -> 20%
where the time goes in v1:
time: 159 us; the launch traced here: 158 us
  Pallas kernels  82.9 us (52%)
  waiting for transfers between devices  37.5 us (24%)
  between operations  14.3 us (9%)
  starting transfers between devices  13.7 us (9%)
  local copies, waits for them, and re-layouts  6.6 us (4%)
  other arithmetic  3.21 us (2%)
    pallas_call x1, Pallas kernels, rest(): pl.pallas_call(functools.partial(rest_kernel, *[[d for d, _ in group] for...  51 us
    ppermute x13, waiting for transfers between devices, swap(): return lax.ppermute(x, axis, [(i, i ^ distance) for i in range(count)])  29 us
    pallas_call x1, Pallas kernels, head(): pl.pallas_call(functools.partial(head_kernel, count, *[[d for d, _ in gro...  28 us
    ppermute x13, starting transfers between devices, swap(): return lax.ppermute(x, axis, [(i, i ^ distance) for i in range(count)])  13.6 us
    all_gather x2, waiting for transfers between devices, body(): lax.all_gather(x[0], 'col', axis=0, tiled=True)  7.86 us
    pallas_call x1, Pallas kernels, terms(): pl.pallas_call(functools.partial(terms_kernel, scale_left, scale_right),...  3.96 us
  transfers between devices with their start and end apart: 15, of which 5 were waited for; matrix products, arithmetic and copies ran while one was open for 5% of the time, Pallas kernels for 20%

profile of v1, /device:TPU:0, one launch (start us, length us, event | category | flops | bytes accessed | tf_op | source)
XLA Modules:
  0.0 158.2 jit_solution(1804776084815881771)
XLA Ops:
  7.2 0.0 all-gather.5.cloned.1.call-start
  7.2 0.7 all-gather.5.cloned.1.call-update
  7.9 0.0 all-gather.7.cloned.1.call-start
  8.0 1.0 slice.8
  9.0 1.1 dynamic-slice_bitcast_fusion
  10.0 0.0 copy-start
  10.0 0.1 pad_maximum_fusion
  10.1 4.0 %shard_map.135 = (bf16[896,512]{1,0:T(8,128)(2,1)}, bf16[512,384]{1,0:T(8,128)(2,1)}) custom-call(bf16[512,896]{1,0:T(8,128)(2,1)} %refs_4_.1), custom_call_target="tpu_custom_call" | custom-call | tf_op jit(solution)/shard_map/pallas_call | solution.py:230
  14.1 1.9 %constant_dynamic-slice_fusion.1 = bf16[448,512]{1,0:T(8,128)(2,1)} fusion(bf16[896,512]{1,0:T(8,128)(2,1)} %get-tuple-element.22, s32[]{:T(128)S(6)} %select_n.17), kind=kLoop, calls=%fused_computation.8 | loop fusion | bytes 917508 | tf_op jit(solution)/shard_map/dynamic_slice | solution.py:518
  16.0 0.5 collective-permute-start.4
  16.4 0.0 all-gather.7.cloned.1.call-update
  16.4 2.6 %collective-permute-start.2 = (f32[224,896]{1,0:T(8,128)S(1)}, f32[224,896]{1,0:T(8,128)}, u32[]{:S(2)}, u32[]{:S(2)}) collective-permute-start(f32[224,896]{1,0:T(8,128)S(1)} %pad_maximum_fusion), channel_id=1, source_target_pairs={{0,16},{8,24},{16,0},{24,8},{1,17},{9,25},{17,1},{25,9},{2,18},{10... | collective-permute-start | bytes 2408456 | tf_op jit(solution)/shard_map/ppermute | solution.py:497
  19.0 0.0 copy-done
  19.0 0.2 collective-permute-start.1
  19.2 1.0 constant_dynamic-slice_fusion
  20.2 1.6 %collective-permute-start.9 = (bf16[256,384]{1,0:T(8,128)(2,1)S(1)}, bf16[256,384]{1,0:T(8,128)(2,1)}, u32[]{:S(2)}, u32[]{:S(2)}) collective-permute-start(bf16[256,384]{1,0:T(8,128)(2,1)S(1)} %constant_dynamic-slice_fusion), channel_id=1, source_target_pairs={{0,1},{1,0},{2,3},{3,2},{4,5},{5,4},{6,7},{7,6},{8,9},{9,8},{10,11... | collective-permute-start | bytes 589832 | tf_op jit(solution)/shard_map/ppermute | solution.py:497
  21.8 0.0 collective-permute-done.4
  21.8 1.3 add_convert_fusion.1
  23.0 0.6 collective-permute-start.5
  23.6 5.2 %collective-permute-done.9 = bf16[256,384]{1,0:T(8,128)(2,1)} collective-permute-done((bf16[256,384]{1,0:T(8,128)(2,1)S(1)}, bf16[256,384]{1,0:T(8,128)(2,1)}, u32[]{:S(2)}, u32[]{:S(2)}) %collective-permute-start.9) | collective-permute-done | bytes 196640 | tf_op jit(solution)/shard_map/ppermute | solution.py:497
  28.8 1.1 add_convert_fusion.4
  29.9 1.6 %collective-permute-start.10 = (bf16[256,384]{1,0:T(8,128)(2,1)S(1)}, bf16[256,384]{1,0:T(8,128)(2,1)S(1)}, u32[]{:S(2)}, u32[]{:S(2)}) collective-permute-start(bf16[256,384]{1,0:T(8,128)(2,1)S(1)} %add_convert_fusion.4), channel_id=1, source_target_pairs={{0,2},{1,3},{2,0},{3,1},{4,6},{5,7},{6,4},{7,5},{8,10},{9,11},{10,... | collective-permute-start | bytes 589832 | tf_op jit(solution)/shard_map/ppermute | solution.py:497
  31.6 0.0 copy-done.2
  31.6 0.0 collective-permute-start
  31.6 6.2 %collective-permute-done.2.refs_5_ = f32[224,896]{1,0:T(8,128)} collective-permute-done((f32[224,896]{1,0:T(8,128)S(1)}, f32[224,896]{1,0:T(8,128)}, u32[]{:S(2)}, u32[]{:S(2)}) %collective-permute-start.2) | collective-permute-done | bytes 802848 | tf_op jit(solution)/shard_map/ppermute | solution.py:497
  37.8 0.0 collective-permute-start.3
  37.8 0.0 collective-permute-done.10
  37.8 0.1 add_convert_fusion.3
  37.9 3.1 %collective-permute-start.11 = (bf16[256,384]{1,0:T(8,128)(2,1)S(1)}, bf16[256,384]{1,0:T(8,128)(2,1)S(1)}, u32[]{:S(2)}, u32[]{:S(2)}) collective-permute-start(bf16[256,384]{1,0:T(8,128)(2,1)S(1)} %add_convert_fusion.3), channel_id=1, source_target_pairs={{0,4},{1,5},{2,6},{3,7},{4,0},{5,1},{6,2},{7,3},{8,12},{9,13},{10,... | collective-permute-start | bytes 589832 | tf_op jit(solution)/shard_map/ppermute | solution.py:497
  41.0 6.4 %collective-permute-done.5 = bf16[448,512]{1,0:T(8,128)(2,1)S(1)} collective-permute-done((bf16[448,512]{1,0:T(8,128)(2,1)S(1)}, bf16[448,512]{1,0:T(8,128)(2,1)S(1)}, u32[]{:S(2)}, u32[]{:S(2)}) %collective-permute-start.5) | collective-permute-done | bytes 458784 | tf_op jit(solution)/shard_map/ppermute | solution.py:497
  47.4 0.1 add_convert_fusion.refs_7_
  47.5 0.0 copy-start.3
  47.5 0.1 collective-permute-start.6
  47.6 11.2 %collective-permute-done.11 = bf16[256,384]{1,0:T(8,128)(2,1)S(1)} collective-permute-done((bf16[256,384]{1,0:T(8,128)(2,1)S(1)}, bf16[256,384]{1,0:T(8,128)(2,1)S(1)}, u32[]{:S(2)}, u32[]{:S(2)}) %collective-permute-start.11) | collective-permute-done | bytes 196640 | tf_op jit(solution)/shard_map/ppermute | solution.py:497
  58.8 1.2 collective-permute-start.8
  60.0 0.0 collective-permute-done.1.refs_4_.refs_11_
  60.0 0.6 collective-permute-start.7
  60.6 0.1 add_convert_fusion.2.refs_14_
  60.7 0.0 copy-start.6
  60.7 0.0 collective-permute-done.refs_2_
  60.7 0.0 copy-start.4
  60.7 1.5 collective-permute-start.12
  62.2 0.6 pad_add_fusion.refs_0_
  62.8 0.0 collective-permute-done.6.refs_8_
  62.8 0.0 collective-permute-done.3.refs_6_
  62.8 0.0 copy-done.3
  62.8 0.0 copy-done.1
  62.8 0.0 copy-done.4
  62.8 0.7 copy-done.7
  63.6 0.9 copy-done.5
  64.4 28.0 %shard_map.136 = (f32[224,896]{1,0:T(8,128)}, bf16[896,896]{1,0:T(8,128)(2,1)}, bf16[896,896]{1,0:T(8,128)(2,1)}, f32[896,384]{1,0:T(8,128)}) custom-call(s32[2]{0:T(128)} %pad_add_fusion.refs_0_, f32[224,896]{1,0:T(8,128)} %bitcast.17, f32[224,896]{1,0:T(8,128)} %copy-done.4, f32[224,896]{1,0:T(8,128)} %bitcast.13, f32[224,896]{1,0:T(8,128)} %copy-done.1, ...), custom_call_target="tpu_custom_call" | custom-call | tf_op jit(solution)/shard_map/pallas_call | solution.py:348
  92.4 0.0 collective-permute-done.12.refs_15_
  92.4 0.0 copy-start.10
  92.4 0.0 collective-permute-done.8.refs_13_
  92.5 0.0 copy-start.8
  92.5 0.0 collective-permute-done.7.refs_12_
  92.5 0.0 copy-start.9
  92.5 0.0 all-gather.5.cloned.1.call-done
  92.5 7.8 %all-gather.7.cloned.1.call-done = f32[1,512,512]{2,1,0:T(8,128)} async-done(((f32[1,64,512]{2,1,0:T(8,128)}), f32[1,512,512]{2,1,0:T(8,128)}) %all-gather.7.cloned.1.call-update) | async-done | bytes 1048592 | tf_op jit(solution)/shard_map/all_gather | solution.py:546
  100.3 0.0 copy-done.6
  100.3 0.0 copy-done.10
  100.4 0.0 copy-done.8
  100.4 0.0 copy-done.9
  100.4 51.0 %shard_map.137 = (f32[512,896]{1,0:T(8,128)}, f32[512,896]{1,0:T(8,128)}, f32[512,896]{1,0:T(8,128)}, f32[224,896]{1,0:T(8,128)}, f32[64,512]{1,0:T(8,128)}, /*index=5*/f32[64,512]{1,0:T(8,128)}) custom-call(s32[2]{0:T(128)} %pad_add_fusion.refs_0_, bf16[896,896]{1,0:T(8,128)(2,1)} %get-tuple-element.23.refs_1_, bf16[896,896]{1,0:T(8,128)(2,1)} %get-tuple-element.24.refs_2_, ...), custom_call_target="tpu_custom_call" | custom-call | tf_op jit(solution)/shard_map/pallas_call | solution.py:455
  (5 shorter events, 0.1 us)
Async XLA Ops:
  7.2 85.3 %all-gather.5.cloned.1.call-start = ((), (), s32[]{:S(2)}) async-start(), calls=%async_computation | async-start | bytes 1179648 | tf_op jit(solution)/shard_map/all_gather | solution.py:546
  7.9 92.4 %all-gather.7.cloned.1.call-start = ((), (), s32[]{:S(2)}) async-start(), calls=%async_computation.1 | async-start | bytes 1179648 | tf_op jit(solution)/shard_map/all_gather | solution.py:546
  10.0 9.0 %copy-start = (f32[1,224,896]{2,1,0:T(8,128)S(1)}, f32[1,224,896]{2,1,0:T(8,128)}, u32[]{:S(2)}) copy-start(f32[1,224,896]{2,1,0:T(8,128)} %param.15) | copy-start | bytes 2408452
  14.1 17.5 %copy-start.2 = (f32[1,224,896]{2,1,0:T(8,128)S(1)}, f32[1,224,896]{2,1,0:T(8,128)}, u32[]{:S(2)}) copy-start(f32[1,224,896]{2,1,0:T(8,128)} %param.14) | copy-start | bytes 2408452
  16.0 5.8 %collective-permute-start.4 = (bf16[448,512]{1,0:T(8,128)(2,1)}, bf16[448,512]{1,0:T(8,128)(2,1)}, u32[]{:S(2)}, u32[]{:S(2)}) collective-permute-start(bf16[448,512]{1,0:T(8,128)(2,1)} %constant_dynamic-slice_fusion.1), channel_id=1, source_target_pairs={{0,8},{8,0},{16,24},{24,16},{1,9},{9,1},{17,25},{25,17},{2,10},{10... | collective-permute-start | bytes 1376264 | tf_op jit(solution)/shard_map/ppermute | solution.py:497
  16.4 21.4 %collective-permute-start.2 = (f32[224,896]{1,0:T(8,128)S(1)}, f32[224,896]{1,0:T(8,128)}, u32[]{:S(2)}, u32[]{:S(2)}) collective-permute-start(f32[224,896]{1,0:T(8,128)S(1)} %pad_maximum_fusion), channel_id=1, source_target_pairs={{0,16},{8,24},{16,0},{24,8},{1,17},{9,25},{17,1},{25,9},{2,18},{10... | collective-permute-start | bytes 2408456 | tf_op jit(solution)/shard_map/ppermute | solution.py:497
  19.0 41.0 %collective-permute-start.1 = (f32[224,896]{1,0:T(8,128)S(1)}, f32[224,896]{1,0:T(8,128)S(1)}, u32[]{:S(2)}, u32[]{:S(2)}) collective-permute-start(f32[224,896]{1,0:T(8,128)S(1)} %bitcast.15), channel_id=1, source_target_pairs={{0,8},{8,0},{16,24},{24,16},{1,9},{9,1},{17,25},{25,17},{2,10},{10... | collective-permute-start | bytes 2408456 | tf_op jit(solution)/shard_map/ppermute | solution.py:497
  20.2 8.7 %collective-permute-start.9 = (bf16[256,384]{1,0:T(8,128)(2,1)S(1)}, bf16[256,384]{1,0:T(8,128)(2,1)}, u32[]{:S(2)}, u32[]{:S(2)}) collective-permute-start(bf16[256,384]{1,0:T(8,128)(2,1)S(1)} %constant_dynamic-slice_fusion), channel_id=1, source_target_pairs={{0,1},{1,0},{2,3},{3,2},{4,5},{5,4},{6,7},{7,6},{8,9},{9,8},{10,11... | collective-permute-start | bytes 589832 | tf_op jit(solution)/shard_map/ppermute | solution.py:497
  23.0 24.3 %collective-permute-start.5 = (bf16[448,512]{1,0:T(8,128)(2,1)S(1)}, bf16[448,512]{1,0:T(8,128)(2,1)S(1)}, u32[]{:S(2)}, u32[]{:S(2)}) collective-permute-start(bf16[448,512]{1,0:T(8,128)(2,1)S(1)} %add_convert_fusion.1), channel_id=1, source_target_pairs={{0,16},{8,24},{16,0},{24,8},{1,17},{9,25},{17,1},{25,9},{2,18},{10... | collective-permute-start | bytes 1376264 | tf_op jit(solution)/shard_map/ppermute | solution.py:497
  29.9 7.9 %collective-permute-start.10 = (bf16[256,384]{1,0:T(8,128)(2,1)S(1)}, bf16[256,384]{1,0:T(8,128)(2,1)S(1)}, u32[]{:S(2)}, u32[]{:S(2)}) collective-permute-start(bf16[256,384]{1,0:T(8,128)(2,1)S(1)} %add_convert_fusion.4), channel_id=1, source_target_pairs={{0,2},{1,3},{2,0},{3,1},{4,6},{5,7},{6,4},{7,5},{8,10},{9,11},{10,... | collective-permute-start | bytes 589832 | tf_op jit(solution)/shard_map/ppermute | solution.py:497
  31.6 29.1 %collective-permute-start = (f32[224,896]{1,0:T(8,128)S(1)}, f32[224,896]{1,0:T(8,128)S(1)}, u32[]{:S(2)}, u32[]{:S(2)}) collective-permute-start(f32[224,896]{1,0:T(8,128)S(1)} %bitcast.18), channel_id=1, source_target_pairs={{0,8},{8,0},{16,24},{24,16},{1,9},{9,1},{17,25},{25,17},{2,10},{10... | collective-permute-start | bytes 2408456 | tf_op jit(solution)/shard_map/ppermute | solution.py:497
  37.8 24.9 %collective-permute-start.3 = (f32[224,896]{1,0:T(8,128)}, f32[224,896]{1,0:T(8,128)S(1)}, u32[]{:S(2)}, u32[]{:S(2)}) collective-permute-start(f32[224,896]{1,0:T(8,128)} %collective-permute-done.2.refs_5_), channel_id=1, source_target_pairs={{0,8},{8,0},{16,24},{24,16},{1,9},{9,1},{17,25},{25,17},{2,10},{10... | collective-permute-start | bytes 2408456 | tf_op jit(solution)/shard_map/ppermute | solution.py:497
  37.9 20.9 %collective-permute-start.11 = (bf16[256,384]{1,0:T(8,128)(2,1)S(1)}, bf16[256,384]{1,0:T(8,128)(2,1)S(1)}, u32[]{:S(2)}, u32[]{:S(2)}) collective-permute-start(bf16[256,384]{1,0:T(8,128)(2,1)S(1)} %add_convert_fusion.3), channel_id=1, source_target_pairs={{0,4},{1,5},{2,6},{3,7},{4,0},{5,1},{6,2},{7,3},{8,12},{9,13},{10,... | collective-permute-start | bytes 589832 | tf_op jit(solution)/shard_map/ppermute | solution.py:497
  47.5 15.3 %copy-start.3 = (bf16[448,512]{1,0:T(8,128)(2,1)}, bf16[448,512]{1,0:T(8,128)(2,1)S(1)}, u32[]{:S(2)}) copy-start(bf16[448,512]{1,0:T(8,128)(2,1)S(1)} %add_convert_fusion.refs_7_) | copy-start | bytes 1376260
  47.5 15.3 %collective-permute-start.6 = (bf16[448,512]{1,0:T(8,128)(2,1)S(1)}, bf16[448,512]{1,0:T(8,128)(2,1)S(1)}, u32[]{:S(2)}, u32[]{:S(2)}) collective-permute-start(bf16[448,512]{1,0:T(8,128)(2,1)S(1)} %add_convert_fusion.refs_7_), channel_id=1, source_target_pairs={{0,8},{8,0},{16,24},{24,16},{1,9},{9,1},{17,25},{25,17},{2,10},{10... | collective-permute-start | bytes 1376264 | tf_op jit(solution)/shard_map/ppermute | solution.py:497
  58.8 33.7 %collective-permute-start.8 = (f32[224,512]{1,0:T(8,128)S(1)}, f32[224,512]{1,0:T(8,128)S(1)}, u32[]{:S(2)}, u32[]{:S(2)}) collective-permute-start(f32[224,512]{1,0:T(8,128)S(1)} %slice.9), channel_id=1, source_target_pairs={{0,24},{8,16},{16,8},{24,0},{1,25},{9,17},{17,9},{25,1},{2,26},{10... | collective-permute-start | bytes 1376264 | tf_op jit(solution)/shard_map/ppermute | solution.py:497
  60.0 2.8 %copy-start.1 = (f32[224,896]{1,0:T(8,128)}, f32[224,896]{1,0:T(8,128)S(1)}, u32[]{:S(2)}) copy-start(f32[224,896]{1,0:T(8,128)S(1)} %collective-permute-done.1.refs_4_.refs_11_) | copy-start | bytes 2408452
  60.0 32.5 %collective-permute-start.7 = (f32[224,512]{1,0:T(8,128)S(1)}, f32[224,512]{1,0:T(8,128)S(1)}, u32[]{:S(2)}, u32[]{:S(2)}) collective-permute-start(f32[224,512]{1,0:T(8,128)S(1)} %slice.9), channel_id=1, source_target_pairs={{0,16},{8,24},{16,0},{24,8},{1,17},{9,25},{17,1},{25,9},{2,18},{10... | collective-permute-start | bytes 1376264 | tf_op jit(solution)/shard_map/ppermute | solution.py:497
  60.7 39.7 %copy-start.6 = (bf16[256,384]{1,0:T(8,128)(2,1)}, bf16[256,384]{1,0:T(8,128)(2,1)S(1)}, u32[]{:S(2)}) copy-start(bf16[256,384]{1,0:T(8,128)(2,1)S(1)} %add_convert_fusion.2.refs_14_) | copy-start | bytes 589828
  60.7 2.1 %copy-start.4 = (f32[224,896]{1,0:T(8,128)}, f32[224,896]{1,0:T(8,128)S(1)}, u32[]{:S(2)}) copy-start(f32[224,896]{1,0:T(8,128)S(1)} %collective-permute-done.refs_2_) | copy-start | bytes 2408452
  60.7 31.7 %collective-permute-start.12 = (bf16[256,384]{1,0:T(8,128)(2,1)S(1)}, bf16[256,384]{1,0:T(8,128)(2,1)S(1)}, u32[]{:S(2)}, u32[]{:S(2)}) collective-permute-start(bf16[256,384]{1,0:T(8,128)(2,1)S(1)} %add_convert_fusion.2.refs_14_), channel_id=1, source_target_pairs={{0,1},{1,0},{2,3},{3,2},{4,5},{5,4},{6,7},{7,6},{8,9},{9,8},{10,11... | collective-permute-start | bytes 589832 | tf_op jit(solution)/shard_map/ppermute | solution.py:497
  62.8 0.8 copy-start.7
  63.6 0.9 copy-start.5
  92.4 7.9 %copy-start.10 = (bf16[256,384]{1,0:T(8,128)(2,1)}, bf16[256,384]{1,0:T(8,128)(2,1)S(1)}, u32[]{:S(2)}) copy-start(bf16[256,384]{1,0:T(8,128)(2,1)S(1)} %collective-permute-done.12.refs_15_) | copy-start | bytes 589828
  92.5 7.9 %copy-start.8 = (f32[224,512]{1,0:T(8,128)}, f32[224,512]{1,0:T(8,128)S(1)}, u32[]{:S(2)}) copy-start(f32[224,512]{1,0:T(8,128)S(1)} %collective-permute-done.8.refs_13_) | copy-start | bytes 1376260
  92.5 7.9 %copy-start.9 = (f32[224,512]{1,0:T(8,128)}, f32[224,512]{1,0:T(8,128)S(1)}, u32[]{:S(2)}) copy-start(f32[224,512]{1,0:T(8,128)S(1)} %collective-permute-done.7.refs_12_) | copy-start | bytes 1376260
Sparse Core Ops, SparseCore 0:
  10.1 49.1 all-gather.4
  61.4 38.8 all-gather.6

commit v2 on v1

--- a/solution.py
+++ b/solution.py
@@ -43,25 +43,35 @@
         cols = [lane_col(pivot, base + k) for k in range(ROWS)]
         full = jnp.where(here, (lanes == subs + base).astype(jnp.float32), pivot)
         forward = full
-        inverse = jnp.zeros((ROWS, LANES), jnp.float32)
         pivots = jnp.ones((ROWS, LANES), jnp.float32)
         yield
-        for j in range(ROWS):
-            value = sub_row(cols[j], j)
-            inv = reciprocal(value)
-            scaled = cols[j] * inv
-            m_full = jnp.where(subs == j, 0.0, scaled)
-            for k in range(j + 1, ROWS):
-                cols[k] = cols[k] - m_full * sub_row(cols[k], j)
-            row = sub_row(full, j)
-            if j < ROWS - 1:
-                forward = forward - jnp.where(subs > j, scaled, 0.0) * sub_row(forward, j)
-            full = full - m_full * row
-            inverse = jnp.where(subs == j, inv, inverse)
-            pivots = jnp.where(subs == j, value, pivots)
+        for j in range(0, ROWS, 2):
+            a, b, d = sub_row(cols[j], j), sub_row(cols[j], j + 1), sub_row(cols[j + 1], j + 1)
+            det = a * d - b * b
+            inv = reciprocal(det)
+            pair = (subs == j) | (subs == j + 1)
+            one = jnp.where(pair, jnp.where(subs == j, -1.0, 0.0), cols[j])
+            two = jnp.where(pair, jnp.where(subs == j, 0.0, -1.0), cols[j + 1])
+            for k in range(j + 2, min(j + 4, ROWS)):
+                x, y = sub_row(cols[k], j), sub_row(cols[k], j + 1)
+                change = one * (d * x - b * y) + two * (a * y - b * x)
+                cols[k] = jnp.where(pair, 0.0, cols[k]) - change * inv
+            yield
+            one, two = (one * d - two * b) * inv, (two * a - one * b) * inv
+            for k in range(j + 4, ROWS):
+                x, y = sub_row(cols[k], j), sub_row(cols[k], j + 1)
+                cols[k] = jnp.where(pair, 0.0, cols[k]) - (one * x + two * y)
+            full = jnp.where(pair, 0.0, full) - (one * sub_row(full, j) + two * sub_row(full, j + 1))
+            inner = b * reciprocal(a)
+            below = subs > j + 1
+            lower = jnp.where(below, one, jnp.where(subs == j + 1, inner, 0.0))
+            change = lower * sub_row(forward, j)
+            if j + 2 < ROWS:
+                change = change + jnp.where(below, two, 0.0) * sub_row(forward, j + 1)
+            forward = forward - change
+            pivots = jnp.where(subs == j, a, jnp.where(subs == j + 1, d - inner * b, pivots))
             yield
         out.append(jnp.where(lanes < base + ROWS, forward * lax.rsqrt(pivots), 0.0))
-        full = full * inverse
         if s < count - 1:
             spread = [sub_row(full, k) for k in range(ROWS)]
             for i in range(s + 1, count):
@@ -369,11 +379,11 @@
     )(me, *args)
 
 
-def rest_kernel(bases, others, sums, *refs):
+def rest_kernel(bases, others, lefts, *refs):
     me_ref, refs = refs[0], list(refs[1:])
-    gh_in, gl_in, q_in, grad_in, weight_in, moment_in, second_in, gram_in, left_in = refs[:9]
-    refs = refs[9:]
-    basis_in, other_in, sum_in = take(refs, bases), take(refs, others), take(refs, sums)
+    gh_in, gl_in, q_in, grad_in, weight_in, moment_in, second_in, sum_in = refs[:8]
+    refs = refs[8:]
+    basis_in, other_in, left_in = take(refs, bases), take(refs, others), take(refs, lefts)
     weight_out, moment_out, second_out, right_rows, left_rows, gram_rows = refs[:6]
     (gh, gl, q_first, basis, qr, ql, gram_l, packed_l, basis_l, glh, gll, zr, wr, zl, wl) = refs[6:21]
     (grad, weight, moment, second, inner, turn, right_half, left_half, semaphores) = refs[21:]
@@ -388,8 +398,14 @@
     for d, piece in other_in:
         start.append(copies.start(piece, basis.at[rows_at(row, d, piece.shape[0]), :]))
     project = [copies.start(q_in, q_first)]
-    lefts = packed_copies(copies, col, sum_in, packed_l)
-    lefts += [copies.start(gram_in, gram_l), copies.start(left_in, basis_l)]
+    size = gram_l.shape[0]
+    rows = left_rows.shape[0]
+    left_copies = [copies.start(sum_in, packed_l)]
+    for ats, pieces in left_in:
+        for n, at in enumerate(ats):
+            for i, ref in enumerate((gram_l, basis_l)):
+                piece = pieces.at[pl.ds(n * rows, rows), pl.ds(i * size, size)]
+                left_copies.append(copies.start(piece, ref.at[rows_at(col, at, rows), :]))
     tail = [copies.start(grad_in, grad), copies.start(moment_in, moment)]
     late = [copies.start(second_in, second), copies.start(weight_in, weight)]
 
@@ -400,7 +416,7 @@
     xh, xl = split(zr[width:, :])
     sh, sl = split(product(qh, qo, xh, xl, ((0,), (0,))))
     zr[width:, :] -= product(qh, qo, sh, sl, ((1,), (0,)))
-    wait(lefts)
+    wait(left_copies)
     new_gram(gram_l, packed_l, glh, gll)
     gram_rows[...] = own_rows(gram_l, col, gram_rows.shape[0])
     image(zl, glh, gll, basis_l)
@@ -444,16 +460,16 @@
     wait(out)
 
 
-def rest(me, gh, gl, q_first, tiles, bases, others, left, sums, rows_l):
-    args = [gh, gl, q_first, *tiles, *left] + [p for group in (bases, others, sums) for _, p in group]
+def rest(me, gh, gl, q_first, tiles, bases, others, lefts, sums_l):
+    args = [gh, gl, q_first, *tiles, sums_l] + [p for _, p in bases + others + lefts]
     rows_r, size_r = bases[0][1].shape
     width = size_r - q_first.shape[1]
-    size_l = left[0].shape[0]
+    rows_l, size_l = lefts[0][1].shape[0], sums_l.shape[0]
     tile = tiles[0].shape
     f32, bf16 = jnp.float32, jnp.bfloat16
     vmem, anywhere = pl.BlockSpec(memory_space=pltpu.VMEM), pl.BlockSpec(memory_space=pl.ANY)
     return pl.pallas_call(
-        functools.partial(rest_kernel, *[[d for d, _ in group] for group in (bases, others, sums)]),
+        functools.partial(rest_kernel, *[[d for d, _ in group] for group in (bases, others, lefts)]),
         out_shape=[
             jax.ShapeDtypeStruct(tile, f32),
             jax.ShapeDtypeStruct(tile, f32),
@@ -486,7 +502,7 @@
             pltpu.VMEM(tile, bf16),
             pltpu.VMEM((size_r, size_r), bf16),
             pltpu.VMEM((size_l, size_l), bf16),
-            pltpu.SemaphoreType.DMA((len(args) + 1 + 2 * (tile[0] // LANES),)),
+            pltpu.SemaphoreType.DMA((len(args) + 1 + 2 * (size_l // rows_l) + 2 * (tile[0] // LANES),)),
         ],
         compiler_params=pltpu.CompilerParams(vmem_limit_bytes=VMEM_LIMIT),
     )(me, *args)
@@ -508,17 +524,30 @@
     return held
 
 
-def sum_halves(x, axis):
-    me, kind = lax.axis_index(axis), x.dtype
+def parts(x, axis, distance):
+    rows = x.shape[0] // 2
+    own = lax.rem(lax.div(lax.axis_index(axis), distance), 2)
+    return (lax.dynamic_slice_in_dim(x, at * rows, rows, 0) for at in (own, 1 - own))
+
+
+def gather_stacked(x, axis, after):
+    held = [([0], x)]
+    for distance in reversed(distances(axis)):
+        sent = jnp.concatenate([piece for _, piece in held]) if len(held) > 1 else x
+        if distance == 1:
+            sent, _ = lax.optimization_barrier((sent, after))
+        held.append(([at ^ distance for ats, _ in held for at in ats], swap(sent, axis, distance)))
+    return held
+
+
+def sum_halves(x, axis, after):
+    kind = x.dtype
     if lax.axis_size(axis) == 1:
         return x, [(0, x)]
-    rows = x.shape[0] // 2
-    own = lax.rem(me, 2)
-    keep = lax.dynamic_slice_in_dim(x, own * rows, rows, 0)
-    other = lax.dynamic_slice_in_dim(x, (1 - own) * rows, rows, 0)
+    keep, other = parts(x, axis, 1)
     total = keep.astype(jnp.float32) + swap(other, axis, 1).astype(jnp.float32)
     for distance in distances(axis)[1:]:
-        total = total.astype(kind)
+        total, _ = lax.optimization_barrier((total.astype(kind), after))
         total = total.astype(jnp.float32) + swap(total, axis, distance).astype(jnp.float32)
     total = total.astype(kind)
     return total, [(0, total), (1, swap(total, axis, 1))]
@@ -543,19 +572,21 @@
     first = max(block_right - block_left, LANES)
     count = lax.axis_size("row")
     me = jnp.stack([lax.axis_index("row"), lax.axis_index("col")])
-    left = [lax.all_gather(x[0], "col", axis=0, tiled=True) for x in (gram_left, basis_left)]
     grams, bases, others, mine = gather_right(gram_right[0], basis_right[0], first)
-    grad_after, _ = lax.optimization_barrier((grad, mine))
+    both, grad_after, _ = lax.optimization_barrier(((gram_left[0], basis_left[0]), grad, mine))
     terms_right, terms_left = terms(
         grad_after, 1.0 / (block_right * lax.axis_size("col")), 1.0 / (block_left * count)
     )
-    sent, sums_right = sum_halves(terms_right, "row")
-    _, sums_left = sum_halves(terms_left, "col")
+    arrived = others[0][1] if others else mine
+    sent, sums_right = sum_halves(terms_right, "row", arrived)
+    sums_left = lax.psum_scatter(terms_left, "col", scatter_dimension=0, tiled=True)
+    left = gather_stacked(jnp.concatenate(both, axis=1), "col", sums_left)
+    sums_left = lax.all_gather(sums_left, "col", axis=0, tiled=True)
     last, _ = lax.optimization_barrier((basis_right[0][:, first:], sent))
     last = [(d, swap(last, "row", d)) for d in range(count // 2, count)] if count > 1 else []
     new_gram_right, gh, gl, q_first = head(me, count, grams, bases, others, sums_right, first)
     new_weight, new_moment, new_second, basis_rows_right, basis_rows_left, new_gram_left = rest(
-        me, gh, gl, q_first, (grad, weight, moment, second), bases, last, left, sums_left, gram_left.shape[1]
+        me, gh, gl, q_first, (grad, weight, moment, second), bases, last, left, sums_left
     )
     return (
         new_weight,

time: 159 us -> 217 us (1.36)
  blocking collectives: 0 us -> 43.4 us
  waiting for transfers between devices: 37.5 us -> 53.5 us
  other arithmetic: 3.21 us -> 7.65 us
  Pallas kernels: 82.9 us -> 79.2 us
    all_gather x0 -> x1, blocking collectives: none -> 43.4 us  [body(): sums_left = lax.all_gather(sums_left, 'col', axis=0, tiled=True)]
    reduce_scatter x0 -> x1, waiting for transfers between devices: none -> 38 us  [body(): lax.psum_scatter(terms_left, 'col', scatter_dimension=0, tiled=True)]
    ppermute x13 -> x12, waiting for transfers between devices: 29 us -> 15.5 us  [swap(): return lax.ppermute(x, axis, [(i, i ^ distance) for i in range(count)])]
    all_gather x2 -> x0, waiting for transfers between devices: 7.86 us -> none  [body(): lax.all_gather(x[0], 'col', axis=0, tiled=True)]
    pallas_call x1, Pallas kernels: 28 us -> 23.4 us  [head(): pl.pallas_call(functools.partial(head_kernel, count, *[[d for d, _ in gro...]
    ppermute x13 -> x12, starting transfers between devices: 13.6 us -> 11.9 us  [swap(): return lax.ppermute(x, axis, [(i, i ^ distance) for i in range(count)])]
  transfers between devices with their start and end apart: 15 -> 13, of which waited for: 5 -> 4; matrix products, arithmetic and copies ran while one was open for 5% -> 4% of each run, Pallas kernels for 20% -> 13%
where the time goes in v2:
time: 217 us; the launch traced here: 216 us
  Pallas kernels  79.2 us (36%)
  waiting for transfers between devices  53.5 us (25%)
  blocking collectives  43.4 us (20%)
  between operations  14.2 us (7%)
  starting transfers between devices  12 us (6%)
  other arithmetic  7.65 us (4%)
  local copies, waits for them, and re-layouts  6.44 us (3%)
    pallas_call x1, Pallas kernels, rest(): pl.pallas_call(functools.partial(rest_kernel, *[[d for d, _ in group] for...  51.9 us
    all_gather x1, blocking collectives, body(): sums_left = lax.all_gather(sums_left, 'col', axis=0, tiled=True)  43.4 us
    reduce_scatter x1, waiting for transfers between devices, body(): lax.psum_scatter(terms_left, 'col', scatter_dimension=0, tiled=True)  38 us
    pallas_call x1, Pallas kernels, head(): pl.pallas_call(functools.partial(head_kernel, count, *[[d for d, _ in gro...  23.4 us
    ppermute x12, waiting for transfers between devices, swap(): return lax.ppermute(x, axis, [(i, i ^ distance) for i in range(count)])  15.5 us
    ppermute x12, starting transfers between devices, swap(): return lax.ppermute(x, axis, [(i, i ^ distance) for i in range(count)])  11.9 us
  transfers between devices with their start and end apart: 13, of which 4 were waited for; matrix products, arithmetic and copies ran while one was open for 4% of the time, Pallas kernels for 13%

profile of v2, /device:TPU:0, one launch (start us, length us, event | category | flops | bytes accessed | tf_op | source)
XLA Modules:
  0.0 216.4 jit_solution(2817869434059576485)
XLA Ops:
  7.2 0.0 copy-start.10
  7.2 0.0 copy-start.9
  7.2 0.0 reduce-scatter.2.cloned.1.call-start
  7.2 1.0 slice.8
  8.3 1.1 dynamic-slice_bitcast_fusion
  9.3 0.9 pad_maximum_fusion.1
  10.3 0.0 copy-done.9
  10.3 0.0 copy-done.10
  10.3 0.0 copy-start
  10.3 0.0 copy-start.5
  10.4 0.0 copy-start.1
  10.4 4.1 %collective-permute-start.9 = (f32[64,1024]{1,0:T(8,128)S(1)}, f32[64,1024]{1,0:T(8,128)S(1)}, u32[]{:S(2)}, u32[]{:S(2)}) collective-permute-start(f32[64,1024]{1,0:T(8,128)S(1)} %constant_dynamic-update-slice_fusion.refs_13_), channel_id=1, source_target_pairs={{0,4},{1,5},{2,6},{3,7},{4,0},{5,1},{6,2},{7,3},{8,12},{9,13},{10,... | collective-permute-start | bytes 786440 | tf_op jit(solution)/shard_map/ppermute | solution.py:513
  14.5 1.5 collective-permute-start.2
  16.0 3.9 %shard_map.135 = (bf16[896,512]{1,0:T(8,128)(2,1)}, bf16[512,384]{1,0:T(8,128)(2,1)}) custom-call(bf16[512,896]{1,0:T(8,128)(2,1)} %refs_4_.1), custom_call_target="tpu_custom_call" | custom-call | tf_op jit(solution)/shard_map/pallas_call | solution.py:240
  19.9 1.8 constant_dynamic-slice_fusion
  21.7 0.0 collective-permute-start.4
  21.7 0.0 reduce-scatter.2.cloned.1.call-update
  21.7 4.7 %collective-permute-done.9.refs_14_ = f32[64,1024]{1,0:T(8,128)S(1)} collective-permute-done((f32[64,1024]{1,0:T(8,128)S(1)}, f32[64,1024]{1,0:T(8,128)S(1)}, u32[]{:S(2)}, u32[]{:S(2)}) %collective-permute-start.9) | collective-permute-done | bytes 262176 | tf_op jit(solution)/shard_map/ppermute | solution.py:513
  26.4 0.0 copy-start.3
  26.4 0.9 pad_maximum_fusion.2
  27.3 0.7 collective-permute-start.10
  28.0 0.0 copy-done
  28.0 0.0 collective-permute-start.1
  28.0 0.0 copy-done.5
  28.0 0.5 collective-permute-start
  28.5 0.0 collective-permute-done.4
  28.5 2.0 add_convert_fusion.1
  30.6 3.6 %collective-permute-done.2.refs_5_ = f32[224,896]{1,0:T(8,128)} collective-permute-done((f32[224,896]{1,0:T(8,128)}, f32[224,896]{1,0:T(8,128)}, u32[]{:S(2)}, u32[]{:S(2)}) %collective-permute-start.2) | collective-permute-done | bytes 802848 | tf_op jit(solution)/shard_map/ppermute | solution.py:513
  34.1 1.5 collective-permute-start.5
  35.6 7.2 %collective-permute-done.10.refs_15_ = f32[128,1024]{1,0:T(8,128)S(1)} collective-permute-done((f32[128,1024]{1,0:T(8,128)}, f32[128,1024]{1,0:T(8,128)S(1)}, u32[]{:S(2)}, u32[]{:S(2)}) %collective-permute-start.10) | collective-permute-done | bytes 524320 | tf_op jit(solution)/shard_map/ppermute | solution.py:513
  42.8 0.0 copy-done.1
  42.8 0.0 copy-start.4
  42.8 1.1 pad_maximum_fusion
  43.9 0.0 copy-done.3
  43.9 38.0 %reduce-scatter.2.cloned.1.call-done = bf16[64,384]{1,0:T(8,128)(2,1)} async-done(((bf16[512,384]{1,0:T(8,128)(2,1)}), bf16[64,384]{1,0:T(8,128)(2,1)}) %reduce-scatter.2.cloned.1.call-update) | async-done | bytes 49168 | tf_op jit(solution)/shard_map/reduce_scatter | solution.py:582
  82.0 0.0 copy-start.11
  82.0 1.4 collective-permute-start.11
  83.3 0.0 collective-permute-start.3
  83.3 0.8 slice.9
  84.2 0.0 collective-permute-done.5
  84.2 2.0 add_convert_fusion.refs_7_
  86.2 0.0 copy-done.4
  86.2 0.5 collective-permute-start.6
  86.7 0.0 collective-permute-done.1.refs_4_.refs_10_
  86.7 1.1 collective-permute-start.8
  87.9 0.0 collective-permute-done.refs_2_
  87.9 0.6 collective-permute-start.7
  88.4 0.6 pad_add_fusion.refs_0_
  89.1 0.0 copy-done.11
  89.1 43.4 %all_gather.3.refs_8_ = bf16[512,384]{1,0:T(8,128)(2,1)} all-gather(bf16[64,384]{1,0:T(8,128)(2,1)S(1)} %copy-done.11), channel_id=1, replica_groups=mesh['row'=4,'col'=8] {'col'}, dimensions={0}, use_global_device_ids=true | all-gather | bytes 442368 | tf_op jit(solution)/shard_map/all_gather | solution.py:584
  132.5 0.0 collective-permute-done.3.refs_6_
  132.5 0.0 collective-permute-done.6.refs_8_
  132.5 0.0 copy-done.2
  132.5 0.0 copy-start.6
  132.5 0.8 copy-done.6
  133.2 23.4 %shard_map.136 = (f32[224,896]{1,0:T(8,128)}, bf16[896,896]{1,0:T(8,128)(2,1)}, bf16[896,896]{1,0:T(8,128)(2,1)}, f32[896,384]{1,0:T(8,128)}) custom-call(s32[2]{0:T(128)} %pad_add_fusion.refs_0_, f32[224,896]{1,0:T(8,128)} %bitcast.17, f32[224,896]{1,0:T(8,128)} %collective-permute-done.refs_2_, f32[224,896]{1,0:T(8,128)} %bitcast.13, ...), custom_call_target="tpu_custom_call" | custom-call | tf_op jit(solution)/shard_map/pallas_call | solution.py:358
  156.7 0.0 collective-permute-done.8.refs_12_
  156.7 0.0 copy-start.7
  156.7 0.0 collective-permute-done.7.refs_11_
  156.7 0.0 copy-start.8
  156.7 0.0 collective-permute-done.11.refs_16_
  156.7 0.7 copy-done.7
  157.5 0.2 copy-done.8
  157.6 51.9 %shard_map.137 = (f32[512,896]{1,0:T(8,128)}, f32[512,896]{1,0:T(8,128)}, f32[512,896]{1,0:T(8,128)}, f32[224,896]{1,0:T(8,128)}, f32[64,512]{1,0:T(8,128)}, /*index=5*/f32[64,512]{1,0:T(8,128)}) custom-call(s32[2]{0:T(128)} %pad_add_fusion.refs_0_, bf16[896,896]{1,0:T(8,128)(2,1)} %get-tuple-element.28.refs_1_, bf16[896,896]{1,0:T(8,128)(2,1)} %get-tuple-element.29.refs_2_, ...), custom_call_target="tpu_custom_call" | custom-call | tf_op jit(solution)/shard_map/pallas_call | solution.py:471
  (3 shorter events, 0.0 us)
Async XLA Ops:
  7.2 3.1 %copy-start.10 = (f32[1,64,512]{2,1,0:T(8,128)S(1)}, f32[1,64,512]{2,1,0:T(8,128)}, u32[]{:S(2)}) copy-start(f32[1,64,512]{2,1,0:T(8,128)} %param.13) | copy-start | bytes 393220
  7.2 3.1 %copy-start.9 = (f32[1,64,512]{2,1,0:T(8,128)S(1)}, f32[1,64,512]{2,1,0:T(8,128)}, u32[]{:S(2)}) copy-start(f32[1,64,512]{2,1,0:T(8,128)} %param.12) | copy-start | bytes 393220
  7.2 74.8 %reduce-scatter.2.cloned.1.call-start = ((), (), s32[]{:S(2)}) async-start(), calls=%async_computation.1 | async-start | bytes 442368 | tf_op jit(solution)/shard_map/reduce_scatter | solution.py:582
  10.3 17.7 %copy-start = (f32[1,224,896]{2,1,0:T(8,128)S(1)}, f32[1,224,896]{2,1,0:T(8,128)}, u32[]{:S(2)}) copy-start(f32[1,224,896]{2,1,0:T(8,128)} %param.15) | copy-start | bytes 2408452
  10.3 17.7 %copy-start.5 = (f32[1,224,896]{2,1,0:T(8,128)S(1)}, f32[1,224,896]{2,1,0:T(8,128)}, u32[]{:S(2)}) copy-start(f32[1,224,896]{2,1,0:T(8,128)} %param.14) | copy-start | bytes 2408452
  10.4 32.4 %copy-start.1 = (f32[64,1024]{1,0:T(8,128)}, f32[64,1024]{1,0:T(8,128)S(1)}, u32[]{:S(2)}) copy-start(f32[64,1024]{1,0:T(8,128)S(1)} %constant_dynamic-update-slice_fusion.refs_13_) | copy-start | bytes 786436
  10.4 16.0 %collective-permute-start.9 = (f32[64,1024]{1,0:T(8,128)S(1)}, f32[64,1024]{1,0:T(8,128)S(1)}, u32[]{:S(2)}, u32[]{:S(2)}) collective-permute-start(f32[64,1024]{1,0:T(8,128)S(1)} %constant_dynamic-update-slice_fusion.refs_13_), channel_id=1, source_target_pairs={{0,4},{1,5},{2,6},{3,7},{4,0},{5,1},{6,2},{7,3},{8,12},{9,13},{10,... | collective-permute-start | bytes 786440 | tf_op jit(solution)/shard_map/ppermute | solution.py:513
  14.5 19.7 %collective-permute-start.2 = (f32[224,896]{1,0:T(8,128)}, f32[224,896]{1,0:T(8,128)}, u32[]{:S(2)}, u32[]{:S(2)}) collective-permute-start(f32[224,896]{1,0:T(8,128)} %pad_maximum_fusion.1), channel_id=1, source_target_pairs={{0,16},{8,24},{16,0},{24,8},{1,17},{9,25},{17,1},{25,9},{2,18},{10... | collective-permute-start | bytes 2408456 | tf_op jit(solution)/shard_map/ppermute | solution.py:513
  21.7 6.8 %collective-permute-start.4 = (bf16[448,512]{1,0:T(8,128)(2,1)}, bf16[448,512]{1,0:T(8,128)(2,1)}, u32[]{:S(2)}, u32[]{:S(2)}) collective-permute-start(bf16[448,512]{1,0:T(8,128)(2,1)} %constant_dynamic-slice_fusion), channel_id=1, source_target_pairs={{0,8},{8,0},{16,24},{24,16},{1,9},{9,1},{17,25},{25,17},{2,10},{10... | collective-permute-start | bytes 1376264 | tf_op jit(solution)/shard_map/ppermute | solution.py:513
  26.4 17.6 %copy-start.3 = (f32[64,1024]{1,0:T(8,128)}, f32[64,1024]{1,0:T(8,128)S(1)}, u32[]{:S(2)}) copy-start(f32[64,1024]{1,0:T(8,128)S(1)} %collective-permute-done.9.refs_14_) | copy-start | bytes 786436
  27.3 15.5 %collective-permute-start.10 = (f32[128,1024]{1,0:T(8,128)}, f32[128,1024]{1,0:T(8,128)S(1)}, u32[]{:S(2)}, u32[]{:S(2)}) collective-permute-start(f32[128,1024]{1,0:T(8,128)} %pad_maximum_fusion.2), channel_id=1, source_target_pairs={{0,2},{1,3},{2,0},{3,1},{4,6},{5,7},{6,4},{7,5},{8,10},{9,11},{10,... | collective-permute-start | bytes 1572872 | tf_op jit(solution)/shard_map/ppermute | solution.py:513
  28.0 58.7 %collective-permute-start.1 = (f32[224,896]{1,0:T(8,128)S(1)}, f32[224,896]{1,0:T(8,128)S(1)}, u32[]{:S(2)}, u32[]{:S(2)}) collective-permute-start(f32[224,896]{1,0:T(8,128)S(1)} %bitcast.15), channel_id=1, source_target_pairs={{0,8},{8,0},{16,24},{24,16},{1,9},{9,1},{17,25},{25,17},{2,10},{10... | collective-permute-start | bytes 2408456 | tf_op jit(solution)/shard_map/ppermute | solution.py:513
  28.0 59.9 %collective-permute-start = (f32[224,896]{1,0:T(8,128)S(1)}, f32[224,896]{1,0:T(8,128)}, u32[]{:S(2)}, u32[]{:S(2)}) collective-permute-start(f32[224,896]{1,0:T(8,128)S(1)} %bitcast.18), channel_id=1, source_target_pairs={{0,8},{8,0},{16,24},{24,16},{1,9},{9,1},{17,25},{25,17},{2,10},{10... | collective-permute-start | bytes 2408456 | tf_op jit(solution)/shard_map/ppermute | solution.py:513
  34.1 50.0 %collective-permute-start.5 = (bf16[448,512]{1,0:T(8,128)(2,1)}, bf16[448,512]{1,0:T(8,128)(2,1)}, u32[]{:S(2)}, u32[]{:S(2)}) collective-permute-start(bf16[448,512]{1,0:T(8,128)(2,1)} %add_convert_fusion.1), channel_id=1, source_target_pairs={{0,16},{8,24},{16,0},{24,8},{1,17},{9,25},{17,1},{25,9},{2,18},{10... | collective-permute-start | bytes 1376264 | tf_op jit(solution)/shard_map/ppermute | solution.py:513
  42.8 43.4 %copy-start.4 = (f32[128,1024]{1,0:T(8,128)}, f32[128,1024]{1,0:T(8,128)S(1)}, u32[]{:S(2)}) copy-start(f32[128,1024]{1,0:T(8,128)S(1)} %collective-permute-done.10.refs_15_) | copy-start | bytes 1572868
  82.0 7.1 %copy-start.11 = (bf16[64,384]{1,0:T(8,128)(2,1)S(1)}, bf16[64,384]{1,0:T(8,128)(2,1)}, u32[]{:S(2)}) copy-start(bf16[64,384]{1,0:T(8,128)(2,1)} %reduce-scatter.2.cloned.1.call-done) | copy-start | bytes 147460
  82.0 74.8 %collective-permute-start.11 = (f32[256,1024]{1,0:T(8,128)}, f32[256,1024]{1,0:T(8,128)}, u32[]{:S(2)}, u32[]{:S(2)}) collective-permute-start(f32[256,1024]{1,0:T(8,128)} %pad_maximum_fusion), channel_id=1, source_target_pairs={{0,1},{1,0},{2,3},{3,2},{4,5},{5,4},{6,7},{7,6},{8,9},{9,8},{10,11... | collective-permute-start | bytes 3145736 | tf_op jit(solution)/shard_map/ppermute | solution.py:513
  83.3 49.1 %collective-permute-start.3 = (f32[224,896]{1,0:T(8,128)}, f32[224,896]{1,0:T(8,128)}, u32[]{:S(2)}, u32[]{:S(2)}) collective-permute-start(f32[224,896]{1,0:T(8,128)} %collective-permute-done.2.refs_5_), channel_id=1, source_target_pairs={{0,8},{8,0},{16,24},{24,16},{1,9},{9,1},{17,25},{25,17},{2,10},{10... | collective-permute-start | bytes 2408456 | tf_op jit(solution)/shard_map/ppermute | solution.py:513
  86.2 46.2 %collective-permute-start.6 = (bf16[448,512]{1,0:T(8,128)(2,1)}, bf16[448,512]{1,0:T(8,128)(2,1)S(1)}, u32[]{:S(2)}, u32[]{:S(2)}) collective-permute-start(bf16[448,512]{1,0:T(8,128)(2,1)} %add_convert_fusion.refs_7_), channel_id=1, source_target_pairs={{0,8},{8,0},{16,24},{24,16},{1,9},{9,1},{17,25},{25,17},{2,10},{10... | collective-permute-start | bytes 1376264 | tf_op jit(solution)/shard_map/ppermute | solution.py:513
  86.7 45.7 %copy-start.2 = (f32[224,896]{1,0:T(8,128)}, f32[224,896]{1,0:T(8,128)S(1)}, u32[]{:S(2)}) copy-start(f32[224,896]{1,0:T(8,128)S(1)} %collective-permute-done.1.refs_4_.refs_10_) | copy-start | bytes 2408452
  86.7 70.0 %collective-permute-start.8 = (f32[224,512]{1,0:T(8,128)}, f32[224,512]{1,0:T(8,128)S(1)}, u32[]{:S(2)}, u32[]{:S(2)}) collective-permute-start(f32[224,512]{1,0:T(8,128)} %slice.9), channel_id=1, source_target_pairs={{0,24},{8,16},{16,8},{24,0},{1,25},{9,17},{17,9},{25,1},{2,26},{10... | collective-permute-start | bytes 1376264 | tf_op jit(solution)/shard_map/ppermute | solution.py:513
  87.9 68.8 %collective-permute-start.7 = (f32[224,512]{1,0:T(8,128)}, f32[224,512]{1,0:T(8,128)S(1)}, u32[]{:S(2)}, u32[]{:S(2)}) collective-permute-start(f32[224,512]{1,0:T(8,128)} %slice.9), channel_id=1, source_target_pairs={{0,16},{8,24},{16,0},{24,8},{1,17},{9,25},{17,1},{25,9},{2,18},{10... | collective-permute-start | bytes 1376264 | tf_op jit(solution)/shard_map/ppermute | solution.py:513
  132.5 0.8 copy-start.6
  156.7 0.8 copy-start.7
  156.7 0.9 copy-start.8
Sparse Core Ops, SparseCore 0:
  21.8 60.0 reduce-scatter.1

commit v3 on v2

--- a/solution.py
+++ b/solution.py
@@ -1,4 +1,5 @@
 import functools
+from itertools import zip_longest
 import jax
 import jax.numpy as jnp
 from jax import lax
@@ -14,6 +15,7 @@
 WEIGHT_DECAY = 0.01
 LANES = 128
 ROWS = 8
+TILE = 256
 VMEM_LIMIT = 56 * 2**20
 
 
@@ -164,14 +166,16 @@
         def rows_of_u():
             self.u = stack_right(mm_nn(self.w[...], self.z[self.before, :]), 0)
 
-        def rows(i):
-            at = block(i)
-            p = mm(stack_left(self.z[at, self.before], 1), self.w_nt, ((1,), (1,)))
-            if i >= self.blocks:
-                self.q[block(i - self.blocks), self.before] = p
-            self.z[at, :] -= mm(stack_left(p, 1), self.u, ((1,), (0,)))
-
-        return [rows_of_u] + [functools.partial(rows, i) for i in range(self.z.shape[0] // LANES)]
+        def panel():
+            p = mm(stack_left(self.z[:, self.before], 1), self.w_nt, ((1,), (1,)))
+            self.q[:, self.before] = p[self.width :, :]
+            self.p = stack_left(p, 1)
+
+        def columns(at):
+            stop = min(at + TILE, self.width)
+            self.z[:, at:stop] -= mm(self.p, self.u[:, at:stop], ((1,), (0,)))
+
+        return [rows_of_u, panel] + [functools.partial(columns, at) for at in range(0, self.width, TILE)]
 
     def store(self, out):
         for i, row in enumerate(out):
@@ -186,7 +190,7 @@
     def step_of(members):
         def step(j, carry):
             rows = [chain.look(j) for chain in members]
-            fills = [fill for chain in members for fill in chain.fills()]
+            fills = [fill for several in zip_longest(*[chain.fills() for chain in members]) for fill in several if fill]
             for chain, out in zip(members, in_turns([inverse_factor(r) for r in rows], fills)):
                 chain.store(out)
             return carry
@@ -271,11 +275,10 @@
 
 def image(z_ref, gh_ref, gl_ref, basis_ref):
     width = z_ref.shape[1]
-    bh, bl = split(basis_ref[...])
-    for i in range(gh_ref.shape[0] // LANES):
-        z_ref[pl.ds(width + i * LANES, LANES), :] = product(
-            gh_ref[block(i), :], gl_ref[block(i), :], bh, bl, ((1,), (0,))
-        )
+    for at in range(0, width, TILE):
+        stop = min(at + TILE, width)
+        bh, bl = split(basis_ref[:, at:stop])
+        z_ref[width:, at:stop] = product(gh_ref[...], gl_ref[...], bh, bl, ((1,), (0,)))
 
 
 def own_rows(ref, me, rows):
@@ -379,14 +382,14 @@
     )(me, *args)
 
 
-def rest_kernel(bases, others, lefts, *refs):
+def rest_kernel(bases, others, lefts, sums, *refs):
     me_ref, refs = refs[0], list(refs[1:])
-    gh_in, gl_in, q_in, grad_in, weight_in, moment_in, second_in, sum_in = refs[:8]
-    refs = refs[8:]
-    basis_in, other_in, left_in = take(refs, bases), take(refs, others), take(refs, lefts)
+    gh_in, gl_in, q_in, grad_in, weight_in, moment_in, second_in = refs[:7]
+    refs = refs[7:]
+    basis_in, other_in, left_in, sum_in = take(refs, bases), take(refs, others), take(refs, lefts), take(refs, sums)
     weight_out, moment_out, second_out, right_rows, left_rows, gram_rows = refs[:6]
     (gh, gl, q_first, basis, qr, ql, gram_l, packed_l, basis_l, glh, gll, zr, wr, zl, wl) = refs[6:21]
-    (grad, weight, moment, second, inner, turn, right_half, left_half, semaphores) = refs[21:]
+    (grad, weight, moment, second, inner, turn, right_half, left_half, left_t, semaphores) = refs[21:]
     row, col = me_ref[0], me_ref[1]
     copies = Copies(semaphores)
     first = q_first.shape[1]
@@ -399,8 +402,13 @@
         start.append(copies.start(piece, basis.at[rows_at(row, d, piece.shape[0]), :]))
     project = [copies.start(q_in, q_first)]
     size = gram_l.shape[0]
+    left_copies = []
+    for ats, pieces in sum_in:
+        rows = pieces.shape[0] // len(ats)
+        for n, at in enumerate(ats):
+            piece = pieces.at[pl.ds(n * rows, rows), :]
+            left_copies.append(copies.start(piece, packed_l.at[rows_at(me_ref[2], at, rows), :]))
     rows = left_rows.shape[0]
-    left_copies = [copies.start(sum_in, packed_l)]
     for ats, pieces in left_in:
         for n, at in enumerate(ats):
             for i, ref in enumerate((gram_l, basis_l)):
@@ -437,39 +445,40 @@
     right_rows[:, first:] = own_rows(qr, row, right_rows.shape[0])
     left_rows[...] = own_rows(ql, col, left_rows.shape[0])
 
+    rows, columns = grad.shape
+    tiles = [pl.ds(at, min(TILE, columns - at)) for at in range(0, columns, TILE)]
+    left_t[...] = left_half[...].T
+    for tile in tiles:
+        inner[:rows, tile] = mm(left_t[...], grad[:, tile], ((1,), (0,))).astype(jnp.bfloat16)
+        half = moment[:, tile].astype(jnp.bfloat16)
+        inner[rows:, tile] = mm(left_t[...], half, ((1,), (0,))).astype(jnp.bfloat16)
     wait(late)
-    blocks = grad.shape[0] // LANES
-    for i in range(blocks):
-        part = left_half[:, block(i)]
-        both = [grad[...], moment[...].astype(jnp.bfloat16)]
-        for n, matrix in enumerate(both):
-            inner[pl.ds(n * grad.shape[0] + i * LANES, LANES), :] = mm(part, matrix, ((0,), (0,))).astype(jnp.bfloat16)
-    for i in range(blocks):
-        rotated_grad = mm(inner[block(i), :], right_half[...], ((1,), (0,)))
-        rotated_moment = mm(inner[pl.ds(grad.shape[0] + i * LANES, LANES), :], right_half[...], ((1,), (0,)))
-        new_second = SECOND_DECAY * second[block(i), :] + (1.0 - SECOND_DECAY) * rotated_grad * rotated_grad
-        second[block(i), :] = new_second
-        out.append(copies.start(second.at[block(i), :], second_out.at[block(i), :]))
-        turn[block(i), :] = (rotated_moment / (jnp.sqrt(new_second) + EPSILON)).astype(jnp.bfloat16)
-    for i in range(blocks):
-        turned = mm(left_half[block(i), :], turn[...], ((1,), (0,))).astype(jnp.bfloat16)
-        update = mm(turned, right_half[...], ((1,), (1,)))
-        old = weight[block(i), :]
-        weight[block(i), :] = old - STEP_SIZE * (update + WEIGHT_DECAY * old)
-        out.append(copies.start(weight.at[block(i), :], weight_out.at[block(i), :]))
+    for tile in tiles:
+        rotated = mm(inner[...], right_half[:, tile], ((1,), (0,)))
+        rotated_grad, rotated_moment = rotated[:rows, :], rotated[rows:, :]
+        new_second = SECOND_DECAY * second[:, tile] + (1.0 - SECOND_DECAY) * rotated_grad * rotated_grad
+        second[:, tile] = new_second
+        out.append(copies.start(second.at[:, tile], second_out.at[:, tile]))
+        turn[:, tile] = (rotated_moment / (jnp.sqrt(new_second) + EPSILON)).astype(jnp.bfloat16)
+    turned = mm(left_half[...], turn[...], ((1,), (0,))).astype(jnp.bfloat16)
+    for tile in tiles:
+        update = mm(turned, right_half[tile, :], ((1,), (1,)))
+        old = weight[:, tile]
+        weight[:, tile] = old - STEP_SIZE * (update + WEIGHT_DECAY * old)
+        out.append(copies.start(weight.at[:, tile], weight_out.at[:, tile]))
     wait(out)
 
 
-def rest(me, gh, gl, q_first, tiles, bases, others, lefts, sums_l):
-    args = [gh, gl, q_first, *tiles, sums_l] + [p for _, p in bases + others + lefts]
+def rest(me, gh, gl, q_first, tiles, bases, others, lefts, sums):
+    args = [gh, gl, q_first, *tiles] + [p for _, p in bases + others + lefts + sums]
     rows_r, size_r = bases[0][1].shape
     width = size_r - q_first.shape[1]
-    rows_l, size_l = lefts[0][1].shape[0], sums_l.shape[0]
+    rows_l, size_l = lefts[0][1].shape[0], lefts[0][1].shape[1] // 2
     tile = tiles[0].shape
     f32, bf16 = jnp.float32, jnp.bfloat16
     vmem, anywhere = pl.BlockSpec(memory_space=pltpu.VMEM), pl.BlockSpec(memory_space=pl.ANY)
     return pl.pallas_call(
-        functools.partial(rest_kernel, *[[d for d, _ in group] for group in (bases, others, lefts)]),
+        functools.partial(rest_kernel, *[[d for d, _ in group] for group in (bases, others, lefts, sums)]),
         out_shape=[
             jax.ShapeDtypeStruct(tile, f32),
             jax.ShapeDtypeStruct(tile, f32),
@@ -502,7 +511,8 @@
             pltpu.VMEM(tile, bf16),
             pltpu.VMEM((size_r, size_r), bf16),
             pltpu.VMEM((size_l, size_l), bf16),
-            pltpu.SemaphoreType.DMA((len(args) + 1 + 2 * (size_l // rows_l) + 2 * (tile[0] // LANES),)),
+            pltpu.VMEM((size_l, size_l), bf16),
+            pltpu.SemaphoreType.DMA((len(args) + 1 + 3 * (size_l // rows_l) + 2 * -(-tile[1] // TILE),)),
         ],
         compiler_params=pltpu.CompilerParams(vmem_limit_bytes=VMEM_LIMIT),
     )(me, *args)
@@ -530,14 +540,29 @@
     return (lax.dynamic_slice_in_dim(x, at * rows, rows, 0) for at in (own, 1 - own))
 
 
-def gather_stacked(x, axis, after):
+def gather_stacked(x, axis):
     held = [([0], x)]
     for distance in reversed(distances(axis)):
         sent = jnp.concatenate([piece for _, piece in held]) if len(held) > 1 else x
-        if distance == 1:
-            sent, _ = lax.optimization_barrier((sent, after))
         held.append(([at ^ distance for ats, _ in held for at in ats], swap(sent, axis, distance)))
     return held
+
+
+def sum_stacked(x, axis):
+    kind, steps = x.dtype, distances(axis)
+    weights = [1 << n for n in reversed(range(len(steps) - 1))]
+    index = 0
+    for distance, weight in zip(steps, weights):
+        keep, other = parts(x, axis, distance)
+        index = index + weight * lax.rem(lax.div(lax.axis_index(axis), distance), 2)
+        x = (keep.astype(jnp.float32) + swap(other, axis, distance).astype(jnp.float32)).astype(kind)
+    if steps:
+        x = (x.astype(jnp.float32) + swap(x, axis, steps[-1]).astype(jnp.float32)).astype(kind)
+    held = [([0], x)]
+    for distance, weight in reversed(list(zip(steps, weights))):
+        sent = jnp.concatenate([piece for _, piece in held]) if len(held) > 1 else x
+        held.append(([at ^ weight for ats, _ in held for at in ats], swap(sent, axis, distance)))
+    return jnp.int32(index), held
 
 
 def sum_halves(x, axis, after):
@@ -571,7 +596,6 @@
     block_left, block_right = grad.shape
     first = max(block_right - block_left, LANES)
     count = lax.axis_size("row")
-    me = jnp.stack([lax.axis_index("row"), lax.axis_index("col")])
     grams, bases, others, mine = gather_right(gram_right[0], basis_right[0], first)
     both, grad_after, _ = lax.optimization_barrier(((gram_left[0], basis_left[0]), grad, mine))
     terms_right, terms_left = terms(
@@ -579,9 +603,9 @@
     )
     arrived = others[0][1] if others else mine
     sent, sums_right = sum_halves(terms_right, "row", arrived)
-    sums_left = lax.psum_scatter(terms_left, "col", scatter_dimension=0, tiled=True)
-    left = gather_stacked(jnp.concatenate(both, axis=1), "col", sums_left)
-    sums_left = lax.all_gather(sums_left, "col", axis=0, tiled=True)
+    left = gather_stacked(jnp.concatenate(both, axis=1), "col")
+    piece, sums_left = sum_stacked(terms_left, "col")
+    me = jnp.stack([lax.axis_index("row"), lax.axis_index("col"), piece])
     last, _ = lax.optimization_barrier((basis_right[0][:, first:], sent))
     last = [(d, swap(last, "row", d)) for d in range(count // 2, count)] if count > 1 else []
     new_gram_right, gh, gl, q_first = head(me, count, grams, bases, others, sums_right, first)

time: 217 us -> 126 us (0.58)
  blocking collectives: 43.4 us -> 0 us
  waiting for transfers between devices: 53.5 us -> 20.1 us
  between operations: 14.2 us -> 1.07 us
  Pallas kernels: 79.2 us -> 71.3 us
  starting transfers between devices: 12 us -> 17.5 us
  local copies, waits for them, and re-layouts: 6.44 us -> 9.17 us
    all_gather x1 -> x0, blocking collectives: 43.4 us -> none  [body(): sums_left = lax.all_gather(sums_left, 'col', axis=0, tiled=True)]
    reduce_scatter x1 -> x0, waiting for transfers between devices: 38 us -> none  [body(): lax.psum_scatter(terms_left, 'col', scatter_dimension=0, tiled=True)]
    pallas_call x1, Pallas kernels: 51.9 us -> 44.5 us  [rest(): pl.pallas_call(functools.partial(rest_kernel, *[[d for d, _ in group] for...]
    ppermute x12 -> x17, starting transfers between devices: 11.9 us -> 17.5 us  [swap(): return lax.ppermute(x, axis, [(i, i ^ distance) for i in range(count)])]
    ppermute x12 -> x17, waiting for transfers between devices: 15.5 us -> 20.1 us  [swap(): return lax.ppermute(x, axis, [(i, i ^ distance) for i in range(count)])]
  transfers between devices with their start and end apart: 13 -> 17, of which waited for: 4 -> 5; matrix products, arithmetic and copies ran while one was open for 4% -> 8% of each run, Pallas kernels for 13% -> 21%
where the time goes in v3:
time: 126 us
  Pallas kernels  71.3 us (57%)
  waiting for transfers between devices  20.1 us (16%)
  starting transfers between devices  17.5 us (14%)
  local copies, waits for them, and re-layouts  9.17 us (7%)
  other arithmetic  6.85 us (5%)
    pallas_call x1, Pallas kernels, rest(): pl.pallas_call(functools.partial(rest_kernel, *[[d for d, _ in group] for...  44.5 us
    pallas_call x1, Pallas kernels, head(): pl.pallas_call(functools.partial(head_kernel, count, *[[d for d, _ in gro...  22.9 us
    ppermute x17, waiting for transfers between devices, swap(): return lax.ppermute(x, axis, [(i, i ^ distance) for i in range(count)])  20.1 us
    ppermute x17, starting transfers between devices, swap(): return lax.ppermute(x, axis, [(i, i ^ distance) for i in range(count)])  17.5 us
    pallas_call x1, Pallas kernels, terms(): pl.pallas_call(functools.partial(terms_kernel, scale_left, scale_right),...  3.91 us
    unnamed x35, local copies, waits for them, and re-layouts  3.28 us
    dynamic_slice x3, local copies, waits for them, and re-layouts, parts(): lax.dynamic_slice_in_dim(x, at * rows, rows, 0)  2.92 us
  transfers between devices with their start and end apart: 17, of which 5 were waited for; matrix products, arithmetic and copies ran while one was open for 8% of the time, Pallas kernels for 21%

profile of v3, /device:TPU:0, one launch (start us, length us, event | category | flops | bytes accessed | tf_op | source)
XLA Modules:
  0.0 126.0 jit_solution(13453021174429107569)
XLA Ops:
  0.6 1.0 slice.8
  1.7 0.0 copy-start.15
  1.7 0.0 copy-start.16
  1.7 1.1 dynamic-slice_bitcast_fusion
  2.8 0.9 pad_maximum_fusion.1
  3.7 2.9 %collective-permute-start.2 = (f32[224,896]{1,0:T(8,128)}, f32[224,896]{1,0:T(8,128)}, u32[]{:S(2)}, u32[]{:S(2)}) collective-permute-start(f32[224,896]{1,0:T(8,128)} %pad_maximum_fusion.1), channel_id=1, source_target_pairs={{0,16},{8,24},{16,0},{24,8},{1,17},{9,25},{17,1},{25,9},{2,18},{10... | collective-permute-start | bytes 2408456 | tf_op jit(solution)/shard_map/ppermute | solution.py:523
  6.7 3.9 %shard_map.135 = (bf16[896,512]{1,0:T(8,128)(2,1)}, bf16[512,384]{1,0:T(8,128)(2,1)}) custom-call(bf16[512,896]{1,0:T(8,128)(2,1)} %refs_4_.1), custom_call_target="tpu_custom_call" | custom-call | tf_op jit(solution)/shard_map/pallas_call | solution.py:244
  10.6 1.1 constant_dynamic-slice_fusion.1
  11.7 1.6 %collective-permute-start.12 = (bf16[256,384]{1,0:T(8,128)(2,1)S(1)}, bf16[256,384]{1,0:T(8,128)(2,1)S(1)}, u32[]{:S(2)}, u32[]{:S(2)}) collective-permute-start(bf16[256,384]{1,0:T(8,128)(2,1)S(1)} %constant_dynamic-slice_fusion.1), channel_id=1, source_target_pairs={{0,1},{1,0},{2,3},{3,2},{4,5},{5,4},{6,7},{7,6},{8,9},{9,8},{10,11... | collective-permute-start | bytes 589832 | tf_op jit(solution)/shard_map/ppermute | solution.py:523
  13.2 0.0 copy-done.15
  13.3 0.0 copy-done.16
  13.3 0.0 copy-start.1
  13.3 2.7 %collective-permute-start.9 = (f32[64,1024]{1,0:T(8,128)S(1)}, f32[64,1024]{1,0:T(8,128)S(1)}, u32[]{:S(2)}, u32[]{:S(2)}) collective-permute-start(f32[64,1024]{1,0:T(8,128)S(1)} %constant_dynamic-update-slice_fusion.refs_12_), channel_id=1, source_target_pairs={{0,4},{1,5},{2,6},{3,7},{4,0},{5,1},{6,2},{7,3},{8,12},{9,13},{10,... | collective-permute-start | bytes 786440 | tf_op jit(solution)/shard_map/ppermute | solution.py:523
  15.9 1.8 %constant_dynamic-slice_fusion.2 = bf16[448,512]{1,0:T(8,128)(2,1)} fusion(bf16[896,512]{1,0:T(8,128)(2,1)} %get-tuple-element.25, s32[]{:T(128)S(6)} %select_n.23), kind=kLoop, calls=%fused_computation.14 | loop fusion | bytes 917508 | tf_op jit(solution)/shard_map/dynamic_slice | solution.py:540
  17.8 0.0 collective-permute-start.4
  17.8 0.3 collective-permute-done.12
  18.1 0.1 add_convert_fusion.2
  18.1 0.0 copy-start.8
  18.2 0.6 copy-done.8
  18.8 1.6 %collective-permute-start.13 = (bf16[128,384]{1,0:T(8,128)(2,1)S(1)}, bf16[128,384]{1,0:T(8,128)(2,1)}, u32[]{:S(2)}, u32[]{:S(2)}) collective-permute-start(bf16[128,384]{1,0:T(8,128)(2,1)S(1)} %constant_dynamic-slice_fusion), channel_id=1, source_target_pairs={{0,2},{1,3},{2,0},{3,1},{4,6},{5,7},{6,4},{7,5},{8,10},{9,11},{10,... | collective-permute-start | bytes 294920 | tf_op jit(solution)/shard_map/ppermute | solution.py:523
  20.4 7.1 %collective-permute-done.9.refs_13_ = f32[64,1024]{1,0:T(8,128)S(1)} collective-permute-done((f32[64,1024]{1,0:T(8,128)S(1)}, f32[64,1024]{1,0:T(8,128)S(1)}, u32[]{:S(2)}, u32[]{:S(2)}) %collective-permute-start.9) | collective-permute-done | bytes 262176 | tf_op jit(solution)/shard_map/ppermute | solution.py:523
  27.5 0.9 pad_maximum_fusion.2
  28.3 0.6 collective-permute-start.10
  29.0 0.0 collective-permute-start.1
  29.0 0.0 collective-permute-done.13
  29.0 0.5 collective-permute-start
  29.5 1.0 add_convert_fusion.4
  30.4 0.0 collective-permute-done.4
  30.5 3.5 %collective-permute-start.14 = (bf16[128,384]{1,0:T(8,128)(2,1)S(1)}, bf16[128,384]{1,0:T(8,128)(2,1)S(1)}, u32[]{:S(2)}, u32[]{:S(2)}) collective-permute-start(bf16[128,384]{1,0:T(8,128)(2,1)S(1)} %add_convert_fusion.4), channel_id=1, source_target_pairs={{0,4},{1,5},{2,6},{3,7},{4,0},{5,1},{6,2},{7,3},{8,12},{9,13},{10,... | collective-permute-start | bytes 294920 | tf_op jit(solution)/shard_map/ppermute | solution.py:523
  34.0 1.3 %add_convert_fusion.1 = bf16[448,512]{1,0:T(8,128)(2,1)S(1)} fusion(bf16[448,512]{1,0:T(8,128)(2,1)} %collective-permute-done.4, bf16[896,512]{1,0:T(8,128)(2,1)} %get-tuple-element.25, s32[]{:T(128)S(6)} %select_n.22), kind=kLoop, calls=%fused_computation.2 | loop fusion | flops 917504 | bytes 1376260 | tf_op jit(solution)/shard_map/convert_element_type | solution.py:575
  35.2 0.0 collective-permute-done.2.refs_5_
  35.2 0.6 collective-permute-start.5
  35.9 7.5 %collective-permute-done.10.refs_14_ = f32[128,1024]{1,0:T(8,128)S(1)} collective-permute-done((f32[128,1024]{1,0:T(8,128)}, f32[128,1024]{1,0:T(8,128)S(1)}, u32[]{:S(2)}, u32[]{:S(2)}) %collective-permute-start.10) | collective-permute-done | bytes 524320 | tf_op jit(solution)/shard_map/ppermute | solution.py:523
  43.4 1.1 pad_maximum_fusion
  44.5 0.5 collective-permute-start.11
  45.0 0.0 collective-permute-done.14
  45.0 0.0 collective-permute-start.3
  45.0 0.9 slice.9
  45.9 0.0 copy-start.6
  45.9 1.6 %collective-permute-done.5 = bf16[448,512]{1,0:T(8,128)(2,1)S(1)} collective-permute-done((bf16[448,512]{1,0:T(8,128)(2,1)S(1)}, bf16[448,512]{1,0:T(8,128)(2,1)S(1)}, u32[]{:S(2)}, u32[]{:S(2)}) %collective-permute-start.5) | collective-permute-done | bytes 458784 | tf_op jit(solution)/shard_map/ppermute | solution.py:523
  47.5 0.2 collective-permute-start.15
  47.7 0.9 add_convert_fusion.refs_7_
  48.6 3.5 %collective-permute-done.15.refs_17_ = bf16[128,384]{1,0:T(8,128)(2,1)S(1)} collective-permute-done((bf16[128,384]{1,0:T(8,128)(2,1)S(1)}, bf16[128,384]{1,0:T(8,128)(2,1)S(1)}, u32[]{:S(2)}, u32[]{:S(2)}) %collective-permute-start.15) | collective-permute-done | bytes 98336 | tf_op jit(solution)/shard_map/ppermute | solution.py:523
  52.2 0.0 collective-permute-start.6
  52.2 0.0 collective-permute-done.1.refs_4_.refs_9_
  52.2 0.7 collective-permute-start.8
  52.8 0.0 collective-permute-done.refs_2_
  52.8 0.9 copy-done.7
  53.7 1.5 %collective-permute-start.7 = (f32[224,512]{1,0:T(8,128)}, f32[224,512]{1,0:T(8,128)S(1)}, u32[]{:S(2)}, u32[]{:S(2)}) collective-permute-start(f32[224,512]{1,0:T(8,128)} %slice.9), channel_id=1, source_target_pairs={{0,16},{8,24},{16,0},{24,8},{1,17},{9,25},{17,1},{25,9},{2,18},{10... | collective-permute-start | bytes 1376264 | tf_op jit(solution)/shard_map/ppermute | solution.py:523
  55.2 0.0 collective-permute-done.3.refs_6_
  55.2 0.6 collective-permute-start.16
  55.9 0.7 pad_add_fusion.refs_0_
  56.6 0.0 collective-permute-done.6.refs_8_
  56.6 0.8 copy-done.9
  57.3 22.9 %shard_map.136 = (f32[224,896]{1,0:T(8,128)}, bf16[896,896]{1,0:T(8,128)(2,1)}, bf16[896,896]{1,0:T(8,128)(2,1)}, f32[896,384]{1,0:T(8,128)}) custom-call(s32[3]{0:T(128)} %pad_add_fusion.refs_0_, f32[224,896]{1,0:T(8,128)} %bitcast.18, f32[224,896]{1,0:T(8,128)} %copy-done.7, f32[224,896]{1,0:T(8,128)} %bitcast.14, f32[224,896]{1,0:T(8,128)} %copy-done.2, ...), custom_call_target="tpu_custom_call" | custom-call | tf_op jit(solution)/shard_map/pallas_call | solution.py:361
  80.3 0.0 collective-permute-done.16.refs_18_
  80.3 0.0 copy-start.14
  80.3 0.0 collective-permute-done.8.refs_11_
  80.3 0.0 collective-permute-done.7.refs_10_
  80.3 0.0 collective-permute-done.11.refs_15_
  80.4 0.6 copy-done.14
  81.0 0.2 copy-done.10
  81.1 0.1 copy-done.11
  81.3 44.5 %shard_map.137 = (f32[512,896]{1,0:T(8,128)}, f32[512,896]{1,0:T(8,128)}, f32[512,896]{1,0:T(8,128)}, f32[224,896]{1,0:T(8,128)}, f32[64,512]{1,0:T(8,128)}, /*index=5*/f32[64,512]{1,0:T(8,128)}) custom-call(s32[3]{0:T(128)} %pad_add_fusion.refs_0_, bf16[896,896]{1,0:T(8,128)(2,1)} %get-tuple-element.27.refs_1_, bf16[896,896]{1,0:T(8,128)(2,1)} %get-tuple-element.28.refs_2_, ...), custom_call_target="tpu_custom_call" | custom-call | tf_op jit(solution)/shard_map/pallas_call | solution.py:480
  (25 shorter events, 0.1 us)
Async XLA Ops:
  1.7 11.6 %copy-start.15 = (f32[1,64,512]{2,1,0:T(8,128)S(1)}, f32[1,64,512]{2,1,0:T(8,128)}, u32[]{:S(2)}) copy-start(f32[1,64,512]{2,1,0:T(8,128)} %param.12) | copy-start | bytes 393220
  1.7 11.6 %copy-start.16 = (f32[1,64,512]{2,1,0:T(8,128)S(1)}, f32[1,64,512]{2,1,0:T(8,128)}, u32[]{:S(2)}) copy-start(f32[1,64,512]{2,1,0:T(8,128)} %param.13) | copy-start | bytes 393220
  3.7 31.5 %collective-permute-start.2 = (f32[224,896]{1,0:T(8,128)}, f32[224,896]{1,0:T(8,128)}, u32[]{:S(2)}, u32[]{:S(2)}) collective-permute-start(f32[224,896]{1,0:T(8,128)} %pad_maximum_fusion.1), channel_id=1, source_target_pairs={{0,16},{8,24},{16,0},{24,8},{1,17},{9,25},{17,1},{25,9},{2,18},{10... | collective-permute-start | bytes 2408456 | tf_op jit(solution)/shard_map/ppermute | solution.py:523
  10.6 7.5 %copy-start.13 = (bf16[512,384]{1,0:T(8,128)(2,1)S(1)}, bf16[512,384]{1,0:T(8,128)(2,1)}, u32[]{:S(2)}) copy-start(bf16[512,384]{1,0:T(8,128)(2,1)} %get-tuple-element.33) | copy-start | bytes 1179652
  10.6 18.4 %copy-start = (f32[1,224,896]{2,1,0:T(8,128)S(1)}, f32[1,224,896]{2,1,0:T(8,128)}, u32[]{:S(2)}) copy-start(f32[1,224,896]{2,1,0:T(8,128)} %param.15) | copy-start | bytes 2408452
  10.6 18.4 %copy-start.5 = (f32[1,224,896]{2,1,0:T(8,128)S(1)}, f32[1,224,896]{2,1,0:T(8,128)}, u32[]{:S(2)}) copy-start(f32[1,224,896]{2,1,0:T(8,128)} %param.14) | copy-start | bytes 2408452
  11.7 6.4 %collective-permute-start.12 = (bf16[256,384]{1,0:T(8,128)(2,1)S(1)}, bf16[256,384]{1,0:T(8,128)(2,1)S(1)}, u32[]{:S(2)}, u32[]{:S(2)}) collective-permute-start(bf16[256,384]{1,0:T(8,128)(2,1)S(1)} %constant_dynamic-slice_fusion.1), channel_id=1, source_target_pairs={{0,1},{1,0},{2,3},{3,2},{4,5},{5,4},{6,7},{7,6},{8,9},{9,8},{10,11... | collective-permute-start | bytes 589832 | tf_op jit(solution)/shard_map/ppermute | solution.py:523
  13.3 30.1 %copy-start.1 = (f32[64,1024]{1,0:T(8,128)}, f32[64,1024]{1,0:T(8,128)S(1)}, u32[]{:S(2)}) copy-start(f32[64,1024]{1,0:T(8,128)S(1)} %constant_dynamic-update-slice_fusion.refs_12_) | copy-start | bytes 786436
  13.3 14.2 %collective-permute-start.9 = (f32[64,1024]{1,0:T(8,128)S(1)}, f32[64,1024]{1,0:T(8,128)S(1)}, u32[]{:S(2)}, u32[]{:S(2)}) collective-permute-start(f32[64,1024]{1,0:T(8,128)S(1)} %constant_dynamic-update-slice_fusion.refs_12_), channel_id=1, source_target_pairs={{0,4},{1,5},{2,6},{3,7},{4,0},{5,1},{6,2},{7,3},{8,12},{9,13},{10,... | collective-permute-start | bytes 786440 | tf_op jit(solution)/shard_map/ppermute | solution.py:523
  17.8 12.7 %collective-permute-start.4 = (bf16[448,512]{1,0:T(8,128)(2,1)}, bf16[448,512]{1,0:T(8,128)(2,1)}, u32[]{:S(2)}, u32[]{:S(2)}) collective-permute-start(bf16[448,512]{1,0:T(8,128)(2,1)} %constant_dynamic-slice_fusion.2), channel_id=1, source_target_pairs={{0,8},{8,0},{16,24},{24,16},{1,9},{9,1},{17,25},{25,17},{2,10},{10... | collective-permute-start | bytes 1376264 | tf_op jit(solution)/shard_map/ppermute | solution.py:523
  18.1 0.7 copy-start.8
  18.8 10.1 %collective-permute-start.13 = (bf16[128,384]{1,0:T(8,128)(2,1)S(1)}, bf16[128,384]{1,0:T(8,128)(2,1)}, u32[]{:S(2)}, u32[]{:S(2)}) collective-permute-start(bf16[128,384]{1,0:T(8,128)(2,1)S(1)} %constant_dynamic-slice_fusion), channel_id=1, source_target_pairs={{0,2},{1,3},{2,0},{3,1},{4,6},{5,7},{6,4},{7,5},{8,10},{9,11},{10,... | collective-permute-start | bytes 294920 | tf_op jit(solution)/shard_map/ppermute | solution.py:523
  27.5 17.1 %copy-start.3 = (f32[64,1024]{1,0:T(8,128)}, f32[64,1024]{1,0:T(8,128)S(1)}, u32[]{:S(2)}) copy-start(f32[64,1024]{1,0:T(8,128)S(1)} %collective-permute-done.9.refs_13_) | copy-start | bytes 786436
  28.3 15.0 %collective-permute-start.10 = (f32[128,1024]{1,0:T(8,128)}, f32[128,1024]{1,0:T(8,128)S(1)}, u32[]{:S(2)}, u32[]{:S(2)}) collective-permute-start(f32[128,1024]{1,0:T(8,128)} %pad_maximum_fusion.2), channel_id=1, source_target_pairs={{0,2},{1,3},{2,0},{3,1},{4,6},{5,7},{6,4},{7,5},{8,10},{9,11},{10,... | collective-permute-start | bytes 1572872 | tf_op jit(solution)/shard_map/ppermute | solution.py:523
  29.0 23.2 %collective-permute-start.1 = (f32[224,896]{1,0:T(8,128)S(1)}, f32[224,896]{1,0:T(8,128)S(1)}, u32[]{:S(2)}, u32[]{:S(2)}) collective-permute-start(f32[224,896]{1,0:T(8,128)S(1)} %bitcast.16), channel_id=1, source_target_pairs={{0,8},{8,0},{16,24},{24,16},{1,9},{9,1},{17,25},{25,17},{2,10},{10... | collective-permute-start | bytes 2408456 | tf_op jit(solution)/shard_map/ppermute | solution.py:523
  29.0 23.9 %collective-permute-start = (f32[224,896]{1,0:T(8,128)S(1)}, f32[224,896]{1,0:T(8,128)S(1)}, u32[]{:S(2)}, u32[]{:S(2)}) collective-permute-start(f32[224,896]{1,0:T(8,128)S(1)} %bitcast.19), channel_id=1, source_target_pairs={{0,8},{8,0},{16,24},{24,16},{1,9},{9,1},{17,25},{25,17},{2,10},{10... | collective-permute-start | bytes 2408456 | tf_op jit(solution)/shard_map/ppermute | solution.py:523
  30.5 14.6 %collective-permute-start.14 = (bf16[128,384]{1,0:T(8,128)(2,1)S(1)}, bf16[128,384]{1,0:T(8,128)(2,1)S(1)}, u32[]{:S(2)}, u32[]{:S(2)}) collective-permute-start(bf16[128,384]{1,0:T(8,128)(2,1)S(1)} %add_convert_fusion.4), channel_id=1, source_target_pairs={{0,4},{1,5},{2,6},{3,7},{4,0},{5,1},{6,2},{7,3},{8,12},{9,13},{10,... | collective-permute-start | bytes 294920 | tf_op jit(solution)/shard_map/ppermute | solution.py:523
  35.2 12.3 %collective-permute-start.5 = (bf16[448,512]{1,0:T(8,128)(2,1)S(1)}, bf16[448,512]{1,0:T(8,128)(2,1)S(1)}, u32[]{:S(2)}, u32[]{:S(2)}) collective-permute-start(bf16[448,512]{1,0:T(8,128)(2,1)S(1)} %add_convert_fusion.1), channel_id=1, source_target_pairs={{0,16},{8,24},{16,0},{24,8},{1,17},{9,25},{17,1},{25,9},{2,18},{10... | collective-permute-start | bytes 1376264 | tf_op jit(solution)/shard_map/ppermute | solution.py:523
  43.4 5.2 %copy-start.4 = (f32[128,1024]{1,0:T(8,128)}, f32[128,1024]{1,0:T(8,128)S(1)}, u32[]{:S(2)}) copy-start(f32[128,1024]{1,0:T(8,128)S(1)} %collective-permute-done.10.refs_14_) | copy-start | bytes 1572868
  44.5 35.8 %collective-permute-start.11 = (f32[256,1024]{1,0:T(8,128)}, f32[256,1024]{1,0:T(8,128)}, u32[]{:S(2)}, u32[]{:S(2)}) collective-permute-start(f32[256,1024]{1,0:T(8,128)} %pad_maximum_fusion), channel_id=1, source_target_pairs={{0,1},{1,0},{2,3},{3,2},{4,5},{5,4},{6,7},{7,6},{8,9},{9,8},{10,11... | collective-permute-start | bytes 3145736 | tf_op jit(solution)/shard_map/ppermute | solution.py:523
  45.0 10.2 %collective-permute-start.3 = (f32[224,896]{1,0:T(8,128)}, f32[224,896]{1,0:T(8,128)}, u32[]{:S(2)}, u32[]{:S(2)}) collective-permute-start(f32[224,896]{1,0:T(8,128)} %collective-permute-done.2.refs_5_), channel_id=1, source_target_pairs={{0,8},{8,0},{16,24},{24,16},{1,9},{9,1},{17,25},{25,17},{2,10},{10... | collective-permute-start | bytes 2408456 | tf_op jit(solution)/shard_map/ppermute | solution.py:523
  45.9 34.3 %copy-start.6 = (bf16[128,384]{1,0:T(8,128)(2,1)}, bf16[128,384]{1,0:T(8,128)(2,1)S(1)}, u32[]{:S(2)}) copy-start(bf16[128,384]{1,0:T(8,128)(2,1)S(1)} %add_convert_fusion.3.refs_16_) | copy-start | bytes 294916
  47.5 4.6 %collective-permute-start.15 = (bf16[128,384]{1,0:T(8,128)(2,1)S(1)}, bf16[128,384]{1,0:T(8,128)(2,1)S(1)}, u32[]{:S(2)}, u32[]{:S(2)}) collective-permute-start(bf16[128,384]{1,0:T(8,128)(2,1)S(1)} %add_convert_fusion.3.refs_16_), channel_id=1, source_target_pairs={{0,2},{1,3},{2,0},{3,1},{4,6},{5,7},{6,4},{7,5},{8,10},{9,11},{10,... | collective-permute-start | bytes 294920 | tf_op jit(solution)/shard_map/ppermute | solution.py:523
  52.2 28.2 %copy-start.12 = (bf16[128,384]{1,0:T(8,128)(2,1)}, bf16[128,384]{1,0:T(8,128)(2,1)S(1)}, u32[]{:S(2)}) copy-start(bf16[128,384]{1,0:T(8,128)(2,1)S(1)} %collective-permute-done.15.refs_17_) | copy-start | bytes 294916
  52.2 4.4 %collective-permute-start.6 = (bf16[448,512]{1,0:T(8,128)(2,1)}, bf16[448,512]{1,0:T(8,128)(2,1)S(1)}, u32[]{:S(2)}, u32[]{:S(2)}) collective-permute-start(bf16[448,512]{1,0:T(8,128)(2,1)} %add_convert_fusion.refs_7_), channel_id=1, source_target_pairs={{0,8},{8,0},{16,24},{24,16},{1,9},{9,1},{17,25},{25,17},{2,10},{10... | collective-permute-start | bytes 1376264 | tf_op jit(solution)/shard_map/ppermute | solution.py:523
  52.2 4.4 %copy-start.2 = (f32[224,896]{1,0:T(8,128)}, f32[224,896]{1,0:T(8,128)S(1)}, u32[]{:S(2)}) copy-start(f32[224,896]{1,0:T(8,128)S(1)} %collective-permute-done.1.refs_4_.refs_9_) | copy-start | bytes 2408452
  52.2 28.1 %collective-permute-start.8 = (f32[224,512]{1,0:T(8,128)}, f32[224,512]{1,0:T(8,128)S(1)}, u32[]{:S(2)}, u32[]{:S(2)}) collective-permute-start(f32[224,512]{1,0:T(8,128)} %slice.9), channel_id=1, source_target_pairs={{0,24},{8,16},{16,8},{24,0},{1,25},{9,17},{17,9},{25,1},{2,26},{10... | collective-permute-start | bytes 1376264 | tf_op jit(solution)/shard_map/ppermute | solution.py:523
  52.8 0.9 copy-start.7
  53.7 26.6 %collective-permute-start.7 = (f32[224,512]{1,0:T(8,128)}, f32[224,512]{1,0:T(8,128)S(1)}, u32[]{:S(2)}, u32[]{:S(2)}) collective-permute-start(f32[224,512]{1,0:T(8,128)} %slice.9), channel_id=1, source_target_pairs={{0,16},{8,24},{16,0},{24,8},{1,17},{9,25},{17,1},{25,9},{2,18},{10... | collective-permute-start | bytes 1376264 | tf_op jit(solution)/shard_map/ppermute | solution.py:523
  55.2 25.0 %collective-permute-start.16 = (bf16[256,384]{1,0:T(8,128)(2,1)S(1)}, bf16[256,384]{1,0:T(8,128)(2,1)S(1)}, u32[]{:S(2)}, u32[]{:S(2)}) collective-permute-start(bf16[256,384]{1,0:T(8,128)(2,1)S(1)} %pad_maximum_fusion.3), channel_id=1, source_target_pairs={{0,1},{1,0},{2,3},{3,2},{4,5},{5,4},{6,7},{7,6},{8,9},{9,8},{10,11... | collective-permute-start | bytes 589832 | tf_op jit(solution)/shard_map/ppermute | solution.py:523
  56.6 0.8 copy-start.9
  80.3 0.7 copy-start.14
  80.3 0.8 copy-start.10
  80.3 1.0 copy-start.11

commit v4 on v3

--- a/solution.py
+++ b/solution.py
@@ -233,22 +233,69 @@
             out_ref[block(i), block(o)] = (term * scale).astype(out_ref.dtype)
 
 
-def terms_kernel(scale_left, scale_right, grad_ref, right_ref, left_ref):
+def terms_kernel(scale_left, scale_right, grad_ref, *refs):
+    right_refs, left_refs, (right, left, semaphores) = refs[:2], refs[2:4], refs[4:]
     rows, columns = grad_ref.shape
-    pack_products([grad_ref[:, block(i)] for i in range(columns // LANES)], right_ref, ((0,), (0,)), scale_right)
-    pack_products([grad_ref[block(i), :] for i in range(rows // LANES)], left_ref, ((1,), (1,)), scale_left)
+    copies = Copies(semaphores)
+    pack_products([grad_ref[:, block(i)] for i in range(columns // LANES)], right, ((0,), (0,)), scale_right)
+    out = []
+    for axis, packed, targets in (("row", right, right_refs), ("col", left, left_refs)):
+        if axis == "col":
+            pack_products([grad_ref[block(i), :] for i in range(rows // LANES)], left, ((1,), (1,)), scale_left)
+        own = lax.rem(lax.axis_index(axis), 2)
+        size = packed.shape[0] // 2
+        for side, target in zip((own, 1 - own), targets):
+            at = pl.ds(pl.multiple_of(side * size, 2 * ROWS), size)
+            out.append(copies.start(packed.at[at, :], target))
+    wait(out)
 
 
 def terms(grad, scale_left, scale_right):
     rows, columns = grad.shape
+    right, left = (columns, offsets(columns) * LANES), (rows, offsets(rows) * LANES)
     return pl.pallas_call(
         functools.partial(terms_kernel, scale_left, scale_right),
         out_shape=[
-            jax.ShapeDtypeStruct((columns, offsets(columns) * LANES), jnp.bfloat16),
-            jax.ShapeDtypeStruct((rows, offsets(rows) * LANES), jnp.bfloat16),
+            jax.ShapeDtypeStruct((shape[0] // 2, shape[1]), jnp.bfloat16) for shape in (right, right, left, left)
+        ],
+        out_specs=any_specs(4),
+        scratch_shapes=[
+            pltpu.VMEM(right, jnp.bfloat16),
+            pltpu.VMEM(left, jnp.bfloat16),
+            pltpu.SemaphoreType.DMA((4,)),
         ],
         compiler_params=pltpu.CompilerParams(vmem_limit_bytes=VMEM_LIMIT),
     )(grad)
+
+
+def pack_kernel(count, width, gram, basis, gram_left, basis_left, right_ref, left_ref, semaphores):
+    copies = Copies(semaphores)
+    window = half_window(gram.shape[1])
+    half = lax.div(2 * lax.axis_index("row"), count)
+    at = pl.ds(pl.multiple_of(half * (gram.shape[1] - window), LANES), window)
+    size = gram_left.shape[1]
+    wait(
+        [
+            copies.start(gram.at[:, at], right_ref.at[:, pl.ds(0, window)]),
+            copies.start(basis.at[:, pl.ds(0, width)], right_ref.at[:, pl.ds(window, width)]),
+            copies.start(gram_left, left_ref.at[:, pl.ds(0, size)]),
+            copies.start(basis_left, left_ref.at[:, pl.ds(size, size)]),
+        ]
+    )
+
+
+def pack(count, width, gram, basis, gram_left, basis_left):
+    return pl.pallas_call(
+        functools.partial(pack_kernel, count, width),
+        out_shape=[
+            jax.ShapeDtypeStruct((gram.shape[0], half_window(gram.shape[1]) + width), jnp.float32),
+            jax.ShapeDtypeStruct((gram_left.shape[0], 2 * gram_left.shape[1]), jnp.float32),
+        ],
+        in_specs=any_specs(4),
+        out_specs=any_specs(2),
+        scratch_shapes=[pltpu.SemaphoreType.DMA((4,))],
+        compiler_params=pltpu.CompilerParams(vmem_limit_bytes=VMEM_LIMIT),
+    )(gram, basis, gram_left, basis_left)
 
 
 def rows_at(me, distance, rows):
@@ -310,10 +357,10 @@
 
 
 def head_kernel(count, owns, others, sums, *refs):
-    me_ref, refs = refs[0], list(refs[1:])
+    refs = list(refs)
     gram_in, basis_in, other_in, sum_in = take(refs, owns), take(refs, owns), take(refs, others), take(refs, sums)
     rows_ref, gh_ref, gl_ref, q_ref, gram, packed, basis, gh, gl, rows_own, z, w, semaphores = refs
-    me = me_ref[0]
+    me = lax.axis_index("row")
     copies = Copies(semaphores)
     width = basis.shape[1]
     half = lax.div(2 * me, count)
@@ -347,14 +394,14 @@
 
 
 def any_specs(count):
-    return [pl.BlockSpec(memory_space=pltpu.SMEM)] + [pl.BlockSpec(memory_space=pl.ANY)] * count
+    return [pl.BlockSpec(memory_space=pl.ANY)] * count
 
 
 def chain_scratch(width, rows):
     return [pltpu.VMEM((width + rows, width), jnp.float32), pltpu.VMEM((LANES, LANES), jnp.float32)]
 
 
-def head(me, count, grams, bases, others, sums, width):
+def head(count, grams, bases, others, sums, width):
     args = [p for group in (grams, bases, others, sums) for _, p in group]
     rows, size = grams[0][1].shape
     f32, bf16 = jnp.float32, jnp.bfloat16
@@ -379,18 +426,18 @@
             pltpu.SemaphoreType.DMA((len(args) + len(others) + 3,)),
         ],
         compiler_params=pltpu.CompilerParams(vmem_limit_bytes=VMEM_LIMIT),
-    )(me, *args)
+    )(*args)
 
 
 def rest_kernel(bases, others, lefts, sums, *refs):
-    me_ref, refs = refs[0], list(refs[1:])
+    refs = list(refs)
     gh_in, gl_in, q_in, grad_in, weight_in, moment_in, second_in = refs[:7]
     refs = refs[7:]
     basis_in, other_in, left_in, sum_in = take(refs, bases), take(refs, others), take(refs, lefts), take(refs, sums)
     weight_out, moment_out, second_out, right_rows, left_rows, gram_rows = refs[:6]
     (gh, gl, q_first, basis, qr, ql, gram_l, packed_l, basis_l, glh, gll, zr, wr, zl, wl) = refs[6:21]
     (grad, weight, moment, second, inner, turn, right_half, left_half, left_t, semaphores) = refs[21:]
-    row, col = me_ref[0], me_ref[1]
+    row, col = lax.axis_index("row"), lax.axis_index("col")
     copies = Copies(semaphores)
     first = q_first.shape[1]
     width = zr.shape[1]
@@ -407,7 +454,7 @@
         rows = pieces.shape[0] // len(ats)
         for n, at in enumerate(ats):
             piece = pieces.at[pl.ds(n * rows, rows), :]
-            left_copies.append(copies.start(piece, packed_l.at[rows_at(me_ref[2], at, rows), :]))
+            left_copies.append(copies.start(piece, packed_l.at[rows_at(piece_index("col"), at, rows), :]))
     rows = left_rows.shape[0]
     for ats, pieces in left_in:
         for n, at in enumerate(ats):
@@ -469,7 +516,7 @@
     wait(out)
 
 
-def rest(me, gh, gl, q_first, tiles, bases, others, lefts, sums):
+def rest(gh, gl, q_first, tiles, bases, others, lefts, sums):
     args = [gh, gl, q_first, *tiles] + [p for _, p in bases + others + lefts + sums]
     rows_r, size_r = bases[0][1].shape
     width = size_r - q_first.shape[1]
@@ -515,7 +562,7 @@
             pltpu.SemaphoreType.DMA((len(args) + 1 + 3 * (size_l // rows_l) + 2 * -(-tile[1] // TILE),)),
         ],
         compiler_params=pltpu.CompilerParams(vmem_limit_bytes=VMEM_LIMIT),
-    )(me, *args)
+    )(*args)
 
 
 def swap(x, axis, distance):
@@ -537,7 +584,7 @@
 def parts(x, axis, distance):
     rows = x.shape[0] // 2
     own = lax.rem(lax.div(lax.axis_index(axis), distance), 2)
-    return (lax.dynamic_slice_in_dim(x, at * rows, rows, 0) for at in (own, 1 - own))
+    return tuple(lax.dynamic_slice_in_dim(x, at * rows, rows, 0) for at in (own, 1 - own))
 
 
 def gather_stacked(x, axis):
@@ -548,69 +595,66 @@
     return held
 
 
-def sum_stacked(x, axis):
-    kind, steps = x.dtype, distances(axis)
-    weights = [1 << n for n in reversed(range(len(steps) - 1))]
-    index = 0
-    for distance, weight in zip(steps, weights):
-        keep, other = parts(x, axis, distance)
-        index = index + weight * lax.rem(lax.div(lax.axis_index(axis), distance), 2)
-        x = (keep.astype(jnp.float32) + swap(other, axis, distance).astype(jnp.float32)).astype(kind)
-    if steps:
-        x = (x.astype(jnp.float32) + swap(x, axis, steps[-1]).astype(jnp.float32)).astype(kind)
+def add(x, y):
+    return (x.astype(jnp.float32) + y.astype(jnp.float32)).astype(x.dtype)
+
+
+def piece_weights(axis):
+    return [1 << n for n in reversed(range(len(distances(axis)) - 1))]
+
+
+def piece_index(axis):
+    me, index = lax.axis_index(axis), 0
+    for distance, weight in zip(distances(axis), piece_weights(axis)):
+        index = index + weight * lax.rem(lax.div(me, distance), 2)
+    return index
+
+
+def sum_stacked(keep, other, axis):
+    steps, weights = distances(axis), piece_weights(axis)
+    x = None
+    for distance in steps[:-1]:
+        if x is not None:
+            keep, other = parts(x, axis, distance)
+        x = add(keep, swap(other, axis, distance))
+    x = add(x, swap(x, axis, steps[-1]))
     held = [([0], x)]
     for distance, weight in reversed(list(zip(steps, weights))):
         sent = jnp.concatenate([piece for _, piece in held]) if len(held) > 1 else x
         held.append(([at ^ weight for ats, _ in held for at in ats], swap(sent, axis, distance)))
-    return jnp.int32(index), held
-
-
-def sum_halves(x, axis, after):
-    kind = x.dtype
-    if lax.axis_size(axis) == 1:
-        return x, [(0, x)]
-    keep, other = parts(x, axis, 1)
-    total = keep.astype(jnp.float32) + swap(other, axis, 1).astype(jnp.float32)
+    return held
+
+
+def sum_halves(keep, other, axis, after):
+    total, _ = lax.optimization_barrier((add(keep, swap(other, axis, 1)), after))
     for distance in distances(axis)[1:]:
-        total, _ = lax.optimization_barrier((total.astype(kind), after))
-        total = total.astype(jnp.float32) + swap(total, axis, distance).astype(jnp.float32)
-    total = total.astype(kind)
+        total = add(total, swap(total, axis, distance))
     return total, [(0, total), (1, swap(total, axis, 1))]
-
-
-def gather_right(gram, basis, width):
-    count = lax.axis_size("row")
-    grams, bases = [(0, gram)], [(0, basis)]
-    if count == 1:
-        return grams, bases, [], gram
-    window = half_window(gram.shape[1])
-    half = lax.div(2 * lax.axis_index("row"), count)
-    mine = lax.dynamic_slice_in_dim(gram, half * (gram.shape[1] - window), window, 1)
-    mine = jnp.concatenate([mine, basis[:, :width]], axis=1)
-    others = [(count // 2, swap(mine, "row", count // 2))]
-    near = distances("row")[-2::-1]
-    return spread(grams, "row", near), spread(bases, "row", near), spread(others, "row", near), mine
 
 
 def body(grad, weight, moment, second, gram_left, basis_left, gram_right, basis_right):
     block_left, block_right = grad.shape
     first = max(block_right - block_left, LANES)
     count = lax.axis_size("row")
-    grams, bases, others, mine = gather_right(gram_right[0], basis_right[0], first)
-    both, grad_after, _ = lax.optimization_barrier(((gram_left[0], basis_left[0]), grad, mine))
-    terms_right, terms_left = terms(
+    gram_right, basis_right = gram_right[0], basis_right[0]
+    window, left = pack(count, first, gram_right, basis_right, gram_left[0], basis_left[0])
+    near = distances("row")[-2::-1]
+    arrived = swap(window, "row", count // 2)
+    gram_right, basis_right, _ = lax.optimization_barrier((gram_right, basis_right, arrived))
+    grams, bases = spread([(0, gram_right)], "row", near), spread([(0, basis_right)], "row", near)
+    others = spread([(count // 2, arrived)], "row", near)
+    grad_after, left = lax.optimization_barrier((grad, left))
+    keep_right, other_right, keep_left, other_left = terms(
         grad_after, 1.0 / (block_right * lax.axis_size("col")), 1.0 / (block_left * count)
     )
-    arrived = others[0][1] if others else mine
-    sent, sums_right = sum_halves(terms_right, "row", arrived)
-    left = gather_stacked(jnp.concatenate(both, axis=1), "col")
-    piece, sums_left = sum_stacked(terms_left, "col")
-    me = jnp.stack([lax.axis_index("row"), lax.axis_index("col"), piece])
-    last, _ = lax.optimization_barrier((basis_right[0][:, first:], sent))
-    last = [(d, swap(last, "row", d)) for d in range(count // 2, count)] if count > 1 else []
-    new_gram_right, gh, gl, q_first = head(me, count, grams, bases, others, sums_right, first)
+    left = gather_stacked(left, "col")
+    sent, sums_right = sum_halves(keep_right, other_right, "row", arrived)
+    sums_left = sum_stacked(keep_left, other_left, "col")
+    last, _ = lax.optimization_barrier((basis_right[:, first:], sent))
+    last = [(d, swap(last, "row", d)) for d in range(count // 2, count)]
+    new_gram_right, gh, gl, q_first = head(count, grams, bases, others, sums_right, first)
     new_weight, new_moment, new_second, basis_rows_right, basis_rows_left, new_gram_left = rest(
-        me, gh, gl, q_first, (grad, weight, moment, second), bases, last, left, sums_left
+        gh, gl, q_first, (grad, weight, moment, second), bases, last, left, sums_left
     )
     return (
         new_weight,

time: 126 us -> 155 us (1.23)
  Pallas kernels: 71.3 us -> 104 us
  local copies, waits for them, and re-layouts: 9.17 us -> 2.3 us
  waiting for transfers between devices: 20.1 us -> 24.4 us
    pallas_call x0 -> x1, Pallas kernels: none -> 33.4 us  [pack(): pl.pallas_call(functools.partial(pack_kernel, count, width), out_shape=[j...]
    ppermute x17, waiting for transfers between devices: 20.1 us -> 24.4 us  [swap(): return lax.ppermute(x, axis, [(i, i ^ distance) for i in range(count)])]
    dynamic_slice x3 -> x1, local copies, waits for them, and re-layouts: 2.92 us -> 0.02 us  [parts(): lax.dynamic_slice_in_dim(x, at * rows, rows, 0)]
    slice x2 -> x1, local copies, waits for them, and re-layouts: 1.86 us -> 0.04 us  [body(): last, _ = lax.optimization_barrier((basis_right[:, first:], sent))]
    unnamed x35 -> x34, local copies, waits for them, and re-layouts: 3.28 us -> 2.24 us
  transfers between devices with their start and end apart: 17 -> 17, of which waited for: 5 -> 5; matrix products, arithmetic and copies ran while one was open for 8% -> 4% of each run, Pallas kernels for 21% -> 14%
where the time goes in v4:
time: 155 us; the launch traced here: 154 us
  Pallas kernels  104 us (67%)
  waiting for transfers between devices  24.4 us (16%)
  starting transfers between devices  17.6 us (11%)
  other arithmetic  5.36 us (3%)
  local copies, waits for them, and re-layouts  2.3 us (1%)
    pallas_call x1, Pallas kernels, rest(): pl.pallas_call(functools.partial(rest_kernel, *[[d for d, _ in group] for...  43.9 us
    pallas_call x1, Pallas kernels, pack(): pl.pallas_call(functools.partial(pack_kernel, count, width), out_shape=[j...  33.4 us
    ppermute x17, waiting for transfers between devices, swap(): return lax.ppermute(x, axis, [(i, i ^ distance) for i in range(count)])  24.4 us
    pallas_call x1, Pallas kernels, head(): pl.pallas_call(functools.partial(head_kernel, count, *[[d for d, _ in gro...  22.3 us
    ppermute x17, starting transfers between devices, swap(): return lax.ppermute(x, axis, [(i, i ^ distance) for i in range(count)])  17.6 us
    pallas_call x1, Pallas kernels, terms(): pl.pallas_call(functools.partial(terms_kernel, scale_left, scale_right),...  4.05 us
    convert_element_type x5, other arithmetic, add(): return (x.astype(jnp.float32) + y.astype(jnp.float32)).astype(x.dtype)  3.36 us
  transfers between devices with their start and end apart: 17, of which 5 were waited for; matrix products, arithmetic and copies ran while one was open for 4% of the time, Pallas kernels for 14%

profile of v4, /device:TPU:0, one launch (start us, length us, event | category | flops | bytes accessed | tf_op | source)
XLA Modules:
  0.0 154.4 jit_solution(13199976340867803763)
XLA Ops:
  0.6 33.4 %shard_map.135 = (f32[224,896]{1,0:T(8,128)}, f32[64,1024]{1,0:T(8,128)}) custom-call(f32[224,896]{1,0:T(8,128)} %bitcast.13, f32[224,896]{1,0:T(8,128)} %bitcast.8, f32[64,512]{1,0:T(8,128)} %bitcast.16, f32[64,512]{1,0:T(8,128)} %bitcast.17), custom_call_target="tpu_custom_call" | custom-call | tf_op jit(solution)/shard_map/pallas_call | solution.py:288
  34.1 0.0 copy-start.1
  34.1 0.0 copy-start
  34.1 4.0 %shard_map.136 = (bf16[448,512]{1,0:T(8,128)(2,1)}, bf16[448,512]{1,0:T(8,128)(2,1)}, bf16[256,384]{1,0:T(8,128)(2,1)}, bf16[256,384]{1,0:T(8,128)(2,1)}) custom-call(bf16[512,896]{1,0:T(8,128)(2,1)} %refs_3_.1), custom_call_target="tpu_custom_call" | custom-call | tf_op jit(solution)/shard_map/pallas_call | solution.py:256
  38.1 0.0 copy-start.3
  38.1 3.0 %collective-permute-start.12 = (bf16[256,384]{1,0:T(8,128)(2,1)}, bf16[256,384]{1,0:T(8,128)(2,1)S(1)}, u32[]{:S(2)}, u32[]{:S(2)}) collective-permute-start(bf16[256,384]{1,0:T(8,128)(2,1)} %get-tuple-element.43), channel_id=1, source_target_pairs={{0,1},{1,0},{2,3},{3,2},{4,5},{5,4},{6,7},{7,6},{8,9},{9,8},{10,11... | collective-permute-start | bytes 589832 | tf_op jit(solution)/shard_map/ppermute | solution.py:570
  41.2 1.5 collective-permute-start
  42.7 2.6 %collective-permute-start.9 = (f32[64,1024]{1,0:T(8,128)}, f32[64,1024]{1,0:T(8,128)S(1)}, u32[]{:S(2)}, u32[]{:S(2)}) collective-permute-start(f32[64,1024]{1,0:T(8,128)} %get-tuple-element.41.refs_11_), channel_id=1, source_target_pairs={{0,4},{1,5},{2,6},{3,7},{4,0},{5,1},{6,2},{7,3},{8,12},{9,13},{10,... | collective-permute-start | bytes 786440 | tf_op jit(solution)/shard_map/ppermute | solution.py:570
  45.3 0.0 collective-permute-start.4
  45.3 1.0 collective-permute-done.12
  46.3 1.0 add_convert_fusion.2
  47.3 0.0 copy-start.12
  47.3 1.9 %collective-permute-start.13 = (bf16[128,384]{1,0:T(8,128)(2,1)S(1)}, bf16[128,384]{1,0:T(8,128)(2,1)}, u32[]{:S(2)}, u32[]{:S(2)}) collective-permute-start(bf16[128,384]{1,0:T(8,128)(2,1)S(1)} %constant_dynamic-slice_fusion), channel_id=1, source_target_pairs={{0,2},{1,3},{2,0},{3,1},{4,6},{5,7},{6,4},{7,5},{8,10},{9,11},{10,... | collective-permute-start | bytes 294920 | tf_op jit(solution)/shard_map/ppermute | solution.py:570
  49.2 7.7 %collective-permute-done.9.refs_12_ = f32[64,1024]{1,0:T(8,128)S(1)} collective-permute-done((f32[64,1024]{1,0:T(8,128)}, f32[64,1024]{1,0:T(8,128)S(1)}, u32[]{:S(2)}, u32[]{:S(2)}) %collective-permute-start.9) | collective-permute-done | bytes 262176 | tf_op jit(solution)/shard_map/ppermute | solution.py:570
  56.9 0.0 copy-done.12
  56.9 1.9 %pad_maximum_fusion.1 = f32[128,1024]{1,0:T(8,128)} fusion(f32[64,1024]{1,0:T(8,128)S(1)} %collective-permute-done.9.refs_12_, f32[64,1024]{1,0:T(8,128)} %get-tuple-element.41.refs_11_), kind=kLoop, calls=%fused_computation.3 | loop fusion | flops 131072 | bytes 1048576 | tf_op jit(solution)/shard_map/concatenate | solution.py:593
  58.8 0.8 collective-permute-start.10
  59.6 0.0 collective-permute-done.13
  59.6 1.0 add_convert_fusion.4
  60.6 3.4 %collective-permute-start.14 = (bf16[128,384]{1,0:T(8,128)(2,1)S(1)}, bf16[128,384]{1,0:T(8,128)(2,1)S(1)}, u32[]{:S(2)}, u32[]{:S(2)}) collective-permute-start(bf16[128,384]{1,0:T(8,128)(2,1)S(1)} %add_convert_fusion.4), channel_id=1, source_target_pairs={{0,4},{1,5},{2,6},{3,7},{4,0},{5,1},{6,2},{7,3},{8,12},{9,13},{10,... | collective-permute-start | bytes 294920 | tf_op jit(solution)/shard_map/ppermute | solution.py:570
  64.0 0.0 collective-permute-done.refs_4_
  64.0 0.0 copy-done.1
  64.0 0.1 collective-permute-start.1
  64.0 0.0 copy-done
  64.0 0.5 collective-permute-start.2
  64.5 0.0 collective-permute-done.4
  64.5 1.3 add_convert_fusion.1
  65.8 0.6 collective-permute-start.5
  66.4 7.6 %collective-permute-done.10.refs_13_ = f32[128,1024]{1,0:T(8,128)S(1)} collective-permute-done((f32[128,1024]{1,0:T(8,128)}, f32[128,1024]{1,0:T(8,128)S(1)}, u32[]{:S(2)}, u32[]{:S(2)}) %collective-permute-start.10) | collective-permute-done | bytes 524320 | tf_op jit(solution)/shard_map/ppermute | solution.py:570
  74.0 0.0 copy-done.3
  74.0 0.1 pad_maximum_fusion
  74.1 0.0 copy-done.4
  74.1 0.6 collective-permute-start.11
  74.7 0.0 collective-permute-done.14
  74.7 0.0 collective-permute-start.3
  74.8 3.6 %collective-permute-done.5 = bf16[448,512]{1,0:T(8,128)(2,1)S(1)} collective-permute-done((bf16[448,512]{1,0:T(8,128)(2,1)S(1)}, bf16[448,512]{1,0:T(8,128)(2,1)S(1)}, u32[]{:S(2)}, u32[]{:S(2)}) %collective-permute-start.5) | collective-permute-done | bytes 458784 | tf_op jit(solution)/shard_map/ppermute | solution.py:570
  78.4 0.0 collective-permute-start.15
  78.4 0.1 add_convert_fusion.refs_6_
  78.5 0.0 copy-start.6
  78.5 4.5 %collective-permute-done.15.refs_16_ = bf16[128,384]{1,0:T(8,128)(2,1)S(1)} collective-permute-done((bf16[128,384]{1,0:T(8,128)(2,1)S(1)}, bf16[128,384]{1,0:T(8,128)(2,1)S(1)}, u32[]{:S(2)}, u32[]{:S(2)}) %collective-permute-start.15) | collective-permute-done | bytes 98336 | tf_op jit(solution)/shard_map/ppermute | solution.py:570
  83.0 0.0 collective-permute-start.6
  83.0 0.0 collective-permute-done.1.refs_1_
  83.0 0.0 copy-start.10
  83.0 0.7 collective-permute-start.8
  83.7 0.0 collective-permute-done.2.refs_3_.refs_8_
  83.7 1.5 collective-permute-start.7
  85.2 0.0 collective-permute-done.3.refs_5_
  85.2 0.0 copy-start.11
  85.2 0.9 copy-done.11
  86.1 0.5 collective-permute-start.16
  86.6 0.0 collective-permute-done.6.refs_7_
  86.6 0.0 copy-done.6
  86.6 22.3 %shard_map.137 = (f32[224,896]{1,0:T(8,128)}, bf16[896,896]{1,0:T(8,128)(2,1)}, bf16[896,896]{1,0:T(8,128)(2,1)}, f32[896,384]{1,0:T(8,128)}) custom-call(f32[224,896]{1,0:T(8,128)} %bitcast.14, f32[224,896]{1,0:T(8,128)} %copy-done.10, f32[224,896]{1,0:T(8,128)} %bitcast.9, f32[224,896]{1,0:T(8,128)} %copy-done.2, f32[224,896]{1,0:T(8,128)} %copy-done.9, ...), custom_call_target="tpu_custom_call" | custom-call | tf_op jit(solution)/shard_map/pallas_call | solution.py:408
  108.9 0.0 collective-permute-done.16.refs_17_
  108.9 0.0 copy-start.16
  108.9 0.0 collective-permute-done.8.refs_10_
  109.0 0.0 collective-permute-done.7.refs_9_
  109.0 0.0 collective-permute-done.11.refs_14_
  109.0 0.0 copy-start.7
  109.0 0.6 copy-done.16
  109.6 0.2 copy-done.13
  109.8 0.1 copy-done.14
  110.0 0.3 copy-done.7
  110.3 43.9 %shard_map.138 = (f32[512,896]{1,0:T(8,128)}, f32[512,896]{1,0:T(8,128)}, f32[512,896]{1,0:T(8,128)}, f32[224,896]{1,0:T(8,128)}, f32[64,512]{1,0:T(8,128)}, /*index=5*/f32[64,512]{1,0:T(8,128)}) custom-call(bf16[896,896]{1,0:T(8,128)(2,1)} %get-tuple-element.37.refs_0_, bf16[896,896]{1,0:T(8,128)(2,1)} %get-tuple-element.38.refs_1_, ...), custom_call_target="tpu_custom_call" | custom-call | tf_op jit(solution)/shard_map/pallas_call | solution.py:527
  (18 shorter events, 0.1 us)
Async XLA Ops:
  34.1 29.9 %copy-start.1 = (f32[1,224,896]{2,1,0:T(8,128)S(1)}, f32[1,224,896]{2,1,0:T(8,128)}, u32[]{:S(2)}) copy-start(f32[1,224,896]{2,1,0:T(8,128)} %param.14) | copy-start | bytes 2408452
  34.1 30.0 %copy-start = (f32[1,224,896]{2,1,0:T(8,128)S(1)}, f32[1,224,896]{2,1,0:T(8,128)}, u32[]{:S(2)}) copy-start(f32[1,224,896]{2,1,0:T(8,128)} %param.15) | copy-start | bytes 2408452
  38.1 35.9 %copy-start.3 = (f32[64,1024]{1,0:T(8,128)S(1)}, f32[64,1024]{1,0:T(8,128)}, u32[]{:S(2)}) copy-start(f32[64,1024]{1,0:T(8,128)} %get-tuple-element.41.refs_11_) | copy-start | bytes 786436
  38.1 8.1 %collective-permute-start.12 = (bf16[256,384]{1,0:T(8,128)(2,1)}, bf16[256,384]{1,0:T(8,128)(2,1)S(1)}, u32[]{:S(2)}, u32[]{:S(2)}) collective-permute-start(bf16[256,384]{1,0:T(8,128)(2,1)} %get-tuple-element.43), channel_id=1, source_target_pairs={{0,1},{1,0},{2,3},{3,2},{4,5},{5,4},{6,7},{7,6},{8,9},{9,8},{10,11... | collective-permute-start | bytes 589832 | tf_op jit(solution)/shard_map/ppermute | solution.py:570
  41.2 22.8 %collective-permute-start = (f32[224,896]{1,0:T(8,128)}, f32[224,896]{1,0:T(8,128)S(1)}, u32[]{:S(2)}, u32[]{:S(2)}) collective-permute-start(f32[224,896]{1,0:T(8,128)} %get-tuple-element.29), channel_id=1, source_target_pairs={{0,16},{8,24},{16,0},{24,8},{1,17},{9,25},{17,1},{25,9},{2,18},{10... | collective-permute-start | bytes 2408456 | tf_op jit(solution)/shard_map/ppermute | solution.py:570
  42.7 14.2 %collective-permute-start.9 = (f32[64,1024]{1,0:T(8,128)}, f32[64,1024]{1,0:T(8,128)S(1)}, u32[]{:S(2)}, u32[]{:S(2)}) collective-permute-start(f32[64,1024]{1,0:T(8,128)} %get-tuple-element.41.refs_11_), channel_id=1, source_target_pairs={{0,4},{1,5},{2,6},{3,7},{4,0},{5,1},{6,2},{7,3},{8,12},{9,13},{10,... | collective-permute-start | bytes 786440 | tf_op jit(solution)/shard_map/ppermute | solution.py:570
  45.3 19.3 %collective-permute-start.4 = (bf16[448,512]{1,0:T(8,128)(2,1)}, bf16[448,512]{1,0:T(8,128)(2,1)}, u32[]{:S(2)}, u32[]{:S(2)}) collective-permute-start(bf16[448,512]{1,0:T(8,128)(2,1)} %get-tuple-element.35), channel_id=1, source_target_pairs={{0,8},{8,0},{16,24},{24,16},{1,9},{9,1},{17,25},{25,17},{2,10},{10... | collective-permute-start | bytes 1376264 | tf_op jit(solution)/shard_map/ppermute | solution.py:570
  47.3 9.6 %copy-start.12 = (bf16[256,384]{1,0:T(8,128)(2,1)}, bf16[256,384]{1,0:T(8,128)(2,1)S(1)}, u32[]{:S(2)}) copy-start(bf16[256,384]{1,0:T(8,128)(2,1)S(1)} %add_convert_fusion.2) | copy-start | bytes 589828
  47.3 12.3 %collective-permute-start.13 = (bf16[128,384]{1,0:T(8,128)(2,1)S(1)}, bf16[128,384]{1,0:T(8,128)(2,1)}, u32[]{:S(2)}, u32[]{:S(2)}) collective-permute-start(bf16[128,384]{1,0:T(8,128)(2,1)S(1)} %constant_dynamic-slice_fusion), channel_id=1, source_target_pairs={{0,2},{1,3},{2,0},{3,1},{4,6},{5,7},{6,4},{7,5},{8,10},{9,11},{10,... | collective-permute-start | bytes 294920 | tf_op jit(solution)/shard_map/ppermute | solution.py:570
  56.9 17.2 %copy-start.4 = (f32[64,1024]{1,0:T(8,128)}, f32[64,1024]{1,0:T(8,128)S(1)}, u32[]{:S(2)}) copy-start(f32[64,1024]{1,0:T(8,128)S(1)} %collective-permute-done.9.refs_12_) | copy-start | bytes 786436
  58.8 15.2 %collective-permute-start.10 = (f32[128,1024]{1,0:T(8,128)}, f32[128,1024]{1,0:T(8,128)S(1)}, u32[]{:S(2)}, u32[]{:S(2)}) collective-permute-start(f32[128,1024]{1,0:T(8,128)} %pad_maximum_fusion.1), channel_id=1, source_target_pairs={{0,2},{1,3},{2,0},{3,1},{4,6},{5,7},{6,4},{7,5},{8,10},{9,11},{10,... | collective-permute-start | bytes 1572872 | tf_op jit(solution)/shard_map/ppermute | solution.py:570
  60.6 14.1 %collective-permute-start.14 = (bf16[128,384]{1,0:T(8,128)(2,1)S(1)}, bf16[128,384]{1,0:T(8,128)(2,1)S(1)}, u32[]{:S(2)}, u32[]{:S(2)}) collective-permute-start(bf16[128,384]{1,0:T(8,128)(2,1)S(1)} %add_convert_fusion.4), channel_id=1, source_target_pairs={{0,4},{1,5},{2,6},{3,7},{4,0},{5,1},{6,2},{7,3},{8,12},{9,13},{10,... | collective-permute-start | bytes 294920 | tf_op jit(solution)/shard_map/ppermute | solution.py:570
  64.0 10.8 %copy-start.9 = (f32[224,896]{1,0:T(8,128)}, f32[224,896]{1,0:T(8,128)S(1)}, u32[]{:S(2)}) copy-start(f32[224,896]{1,0:T(8,128)S(1)} %collective-permute-done.refs_4_) | copy-start | bytes 2408452
  64.0 19.1 %collective-permute-start.1 = (f32[224,896]{1,0:T(8,128)S(1)}, f32[224,896]{1,0:T(8,128)S(1)}, u32[]{:S(2)}, u32[]{:S(2)}) collective-permute-start(f32[224,896]{1,0:T(8,128)S(1)} %bitcast.15), channel_id=1, source_target_pairs={{0,8},{8,0},{16,24},{24,16},{1,9},{9,1},{17,25},{25,17},{2,10},{10... | collective-permute-start | bytes 2408456 | tf_op jit(solution)/shard_map/ppermute | solution.py:570
  64.0 19.6 %collective-permute-start.2 = (f32[224,896]{1,0:T(8,128)S(1)}, f32[224,896]{1,0:T(8,128)S(1)}, u32[]{:S(2)}, u32[]{:S(2)}) collective-permute-start(f32[224,896]{1,0:T(8,128)S(1)} %bitcast.11), channel_id=1, source_target_pairs={{0,8},{8,0},{16,24},{24,16},{1,9},{9,1},{17,25},{25,17},{2,10},{10... | collective-permute-start | bytes 2408456 | tf_op jit(solution)/shard_map/ppermute | solution.py:570
  65.8 12.6 %collective-permute-start.5 = (bf16[448,512]{1,0:T(8,128)(2,1)S(1)}, bf16[448,512]{1,0:T(8,128)(2,1)S(1)}, u32[]{:S(2)}, u32[]{:S(2)}) collective-permute-start(bf16[448,512]{1,0:T(8,128)(2,1)S(1)} %add_convert_fusion.1), channel_id=1, source_target_pairs={{0,16},{8,24},{16,0},{24,8},{1,17},{9,25},{17,1},{25,9},{2,18},{10... | collective-permute-start | bytes 1376264 | tf_op jit(solution)/shard_map/ppermute | solution.py:570
  74.0 4.5 %copy-start.5 = (f32[128,1024]{1,0:T(8,128)}, f32[128,1024]{1,0:T(8,128)S(1)}, u32[]{:S(2)}) copy-start(f32[128,1024]{1,0:T(8,128)S(1)} %collective-permute-done.10.refs_13_) | copy-start | bytes 1572868
  74.1 34.9 %collective-permute-start.11 = (f32[256,1024]{1,0:T(8,128)S(1)}, f32[256,1024]{1,0:T(8,128)S(1)}, u32[]{:S(2)}, u32[]{:S(2)}) collective-permute-start(f32[256,1024]{1,0:T(8,128)S(1)} %pad_maximum_fusion), channel_id=1, source_target_pairs={{0,1},{1,0},{2,3},{3,2},{4,5},{5,4},{6,7},{7,6},{8,9},{9,8},{10,11... | collective-permute-start | bytes 3145736 | tf_op jit(solution)/shard_map/ppermute | solution.py:570
  74.7 10.5 %collective-permute-start.3 = (f32[224,896]{1,0:T(8,128)S(1)}, f32[224,896]{1,0:T(8,128)S(1)}, u32[]{:S(2)}, u32[]{:S(2)}) collective-permute-start(f32[224,896]{1,0:T(8,128)S(1)} %collective-permute-done.refs_4_), channel_id=1, source_target_pairs={{0,8},{8,0},{16,24},{24,16},{1,9},{9,1},{17,25},{25,17},{2,10},{10... | collective-permute-start | bytes 2408456 | tf_op jit(solution)/shard_map/ppermute | solution.py:570
  74.7 34.2 %copy-start.8 = (bf16[128,384]{1,0:T(8,128)(2,1)}, bf16[128,384]{1,0:T(8,128)(2,1)S(1)}, u32[]{:S(2)}) copy-start(bf16[128,384]{1,0:T(8,128)(2,1)S(1)} %add_convert_fusion.3.refs_15_) | copy-start | bytes 294916
  78.4 4.6 %collective-permute-start.15 = (bf16[128,384]{1,0:T(8,128)(2,1)S(1)}, bf16[128,384]{1,0:T(8,128)(2,1)S(1)}, u32[]{:S(2)}, u32[]{:S(2)}) collective-permute-start(bf16[128,384]{1,0:T(8,128)(2,1)S(1)} %add_convert_fusion.3.refs_15_), channel_id=1, source_target_pairs={{0,2},{1,3},{2,0},{3,1},{4,6},{5,7},{6,4},{7,5},{8,10},{9,11},{10,... | collective-permute-start | bytes 294920 | tf_op jit(solution)/shard_map/ppermute | solution.py:570
  78.5 8.1 %copy-start.6 = (bf16[448,512]{1,0:T(8,128)(2,1)}, bf16[448,512]{1,0:T(8,128)(2,1)S(1)}, u32[]{:S(2)}) copy-start(bf16[448,512]{1,0:T(8,128)(2,1)S(1)} %add_convert_fusion.refs_6_) | copy-start | bytes 1376260
  83.0 25.9 %copy-start.15 = (bf16[128,384]{1,0:T(8,128)(2,1)}, bf16[128,384]{1,0:T(8,128)(2,1)S(1)}, u32[]{:S(2)}) copy-start(bf16[128,384]{1,0:T(8,128)(2,1)S(1)} %collective-permute-done.15.refs_16_) | copy-start | bytes 294916
  83.0 3.6 %collective-permute-start.6 = (bf16[448,512]{1,0:T(8,128)(2,1)S(1)}, bf16[448,512]{1,0:T(8,128)(2,1)}, u32[]{:S(2)}, u32[]{:S(2)}) collective-permute-start(bf16[448,512]{1,0:T(8,128)(2,1)S(1)} %add_convert_fusion.refs_6_), channel_id=1, source_target_pairs={{0,8},{8,0},{16,24},{24,16},{1,9},{9,1},{17,25},{25,17},{2,10},{10... | collective-permute-start | bytes 1376264 | tf_op jit(solution)/shard_map/ppermute | solution.py:570
  83.0 3.6 %copy-start.10 = (f32[224,896]{1,0:T(8,128)}, f32[224,896]{1,0:T(8,128)S(1)}, u32[]{:S(2)}) copy-start(f32[224,896]{1,0:T(8,128)S(1)} %collective-permute-done.1.refs_1_) | copy-start | bytes 2408452
  83.0 25.9 %collective-permute-start.8 = (f32[224,512]{1,0:T(8,128)S(1)}, f32[224,512]{1,0:T(8,128)S(1)}, u32[]{:S(2)}, u32[]{:S(2)}) collective-permute-start(f32[224,512]{1,0:T(8,128)S(1)} %slice.3), channel_id=1, source_target_pairs={{0,24},{8,16},{16,8},{24,0},{1,25},{9,17},{17,9},{25,1},{2,26},{10... | collective-permute-start | bytes 1376264 | tf_op jit(solution)/shard_map/ppermute | solution.py:570
  83.7 2.9 %copy-start.2 = (f32[224,896]{1,0:T(8,128)}, f32[224,896]{1,0:T(8,128)S(1)}, u32[]{:S(2)}) copy-start(f32[224,896]{1,0:T(8,128)S(1)} %collective-permute-done.2.refs_3_.refs_8_) | copy-start | bytes 2408452
  83.7 25.3 %collective-permute-start.7 = (f32[224,512]{1,0:T(8,128)S(1)}, f32[224,512]{1,0:T(8,128)S(1)}, u32[]{:S(2)}, u32[]{:S(2)}) collective-permute-start(f32[224,512]{1,0:T(8,128)S(1)} %slice.3), channel_id=1, source_target_pairs={{0,16},{8,24},{16,0},{24,8},{1,17},{9,25},{17,1},{25,9},{2,18},{10... | collective-permute-start | bytes 1376264 | tf_op jit(solution)/shard_map/ppermute | solution.py:570
  85.2 0.9 copy-start.11
  86.1 22.8 %collective-permute-start.16 = (bf16[256,384]{1,0:T(8,128)(2,1)S(1)}, bf16[256,384]{1,0:T(8,128)(2,1)S(1)}, u32[]{:S(2)}, u32[]{:S(2)}) collective-permute-start(bf16[256,384]{1,0:T(8,128)(2,1)S(1)} %pad_maximum_fusion.2), channel_id=1, source_target_pairs={{0,1},{1,0},{2,3},{3,2},{4,5},{5,4},{6,7},{7,6},{8,9},{9,8},{10,11... | collective-permute-start | bytes 589832 | tf_op jit(solution)/shard_map/ppermute | solution.py:570
  108.9 0.7 copy-start.16
  109.0 0.9 copy-start.13
  109.0 1.0 copy-start.14
  109.0 1.3 copy-start.7

commit v5 on v4

--- a/solution.py
+++ b/solution.py
@@ -233,12 +233,27 @@
             out_ref[block(i), block(o)] = (term * scale).astype(out_ref.dtype)
 
 
-def terms_kernel(scale_left, scale_right, grad_ref, *refs):
-    right_refs, left_refs, (right, left, semaphores) = refs[:2], refs[2:4], refs[4:]
+def first_kernel(count, scale_left, scale_right, grad_in, gram, basis, gram_left, basis_left, *refs):
+    window_ref, both_ref, right_refs, left_refs = refs[0], refs[1], refs[2:4], refs[4:6]
+    grad_ref, window_vmem, both_vmem, right, left, semaphores = refs[6:]
     rows, columns = grad_ref.shape
     copies = Copies(semaphores)
+    window = half_window(gram.shape[1])
+    width = window_vmem.shape[1] - window
+    half = lax.div(2 * lax.axis_index("row"), count)
+    at = pl.ds(pl.multiple_of(half * (gram.shape[1] - window), LANES), window)
+    size = gram_left.shape[1]
+    packing = [
+        copies.start(gram.at[:, at], window_vmem.at[:, pl.ds(0, window)]),
+        copies.start(basis.at[:, pl.ds(0, width)], window_vmem.at[:, pl.ds(window, width)]),
+        copies.start(gram_left, both_vmem.at[:, pl.ds(0, size)]),
+        copies.start(basis_left, both_vmem.at[:, pl.ds(size, size)]),
+    ]
+    loading = [copies.start(grad_in, grad_ref)]
+    wait(packing)
+    out = [copies.start(window_vmem, window_ref), copies.start(both_vmem, both_ref)]
+    wait(loading)
     pack_products([grad_ref[:, block(i)] for i in range(columns // LANES)], right, ((0,), (0,)), scale_right)
-    out = []
     for axis, packed, targets in (("row", right, right_refs), ("col", left, left_refs)):
         if axis == "col":
             pack_products([grad_ref[block(i), :] for i in range(rows // LANES)], left, ((1,), (1,)), scale_left)
@@ -250,52 +265,28 @@
     wait(out)
 
 
-def terms(grad, scale_left, scale_right):
+def first_sends(count, width, grad, gram, basis, gram_left, basis_left, scale_left, scale_right):
     rows, columns = grad.shape
     right, left = (columns, offsets(columns) * LANES), (rows, offsets(rows) * LANES)
+    window = (gram.shape[0], half_window(gram.shape[1]) + width)
+    both = (gram_left.shape[0], 2 * gram_left.shape[1])
+    f32, bf16 = jnp.float32, jnp.bfloat16
     return pl.pallas_call(
-        functools.partial(terms_kernel, scale_left, scale_right),
-        out_shape=[
-            jax.ShapeDtypeStruct((shape[0] // 2, shape[1]), jnp.bfloat16) for shape in (right, right, left, left)
-        ],
-        out_specs=any_specs(4),
+        functools.partial(first_kernel, count, scale_left, scale_right),
+        out_shape=[jax.ShapeDtypeStruct(shape, f32) for shape in (window, both)]
+        + [jax.ShapeDtypeStruct((shape[0] // 2, shape[1]), bf16) for shape in (right, right, left, left)],
+        in_specs=any_specs(5),
+        out_specs=any_specs(6),
         scratch_shapes=[
-            pltpu.VMEM(right, jnp.bfloat16),
-            pltpu.VMEM(left, jnp.bfloat16),
-            pltpu.SemaphoreType.DMA((4,)),
+            pltpu.VMEM(grad.shape, bf16),
+            pltpu.VMEM(window, f32),
+            pltpu.VMEM(both, f32),
+            pltpu.VMEM(right, bf16),
+            pltpu.VMEM(left, bf16),
+            pltpu.SemaphoreType.DMA((11,)),
         ],
         compiler_params=pltpu.CompilerParams(vmem_limit_bytes=VMEM_LIMIT),
-    )(grad)
-
-
-def pack_kernel(count, width, gram, basis, gram_left, basis_left, right_ref, left_ref, semaphores):
-    copies = Copies(semaphores)
-    window = half_window(gram.shape[1])
-    half = lax.div(2 * lax.axis_index("row"), count)
-    at = pl.ds(pl.multiple_of(half * (gram.shape[1] - window), LANES), window)
-    size = gram_left.shape[1]
-    wait(
-        [
-            copies.start(gram.at[:, at], right_ref.at[:, pl.ds(0, window)]),
-            copies.start(basis.at[:, pl.ds(0, width)], right_ref.at[:, pl.ds(window, width)]),
-            copies.start(gram_left, left_ref.at[:, pl.ds(0, size)]),
-            copies.start(basis_left, left_ref.at[:, pl.ds(size, size)]),
-        ]
-    )
-
-
-def pack(count, width, gram, basis, gram_left, basis_left):
-    return pl.pallas_call(
-        functools.partial(pack_kernel, count, width),
-        out_shape=[
-            jax.ShapeDtypeStruct((gram.shape[0], half_window(gram.shape[1]) + width), jnp.float32),
-            jax.ShapeDtypeStruct((gram_left.shape[0], 2 * gram_left.shape[1]), jnp.float32),
-        ],
-        in_specs=any_specs(4),
-        out_specs=any_specs(2),
-        scratch_shapes=[pltpu.SemaphoreType.DMA((4,))],
-        compiler_params=pltpu.CompilerParams(vmem_limit_bytes=VMEM_LIMIT),
-    )(gram, basis, gram_left, basis_left)
+    )(grad, gram, basis, gram_left, basis_left)
 
 
 def rows_at(me, distance, rows):
@@ -625,8 +616,8 @@
     return held
 
 
-def sum_halves(keep, other, axis, after):
-    total, _ = lax.optimization_barrier((add(keep, swap(other, axis, 1)), after))
+def sum_halves(keep, other, axis):
+    total = add(keep, swap(other, axis, 1))
     for distance in distances(axis)[1:]:
         total = add(total, swap(total, axis, distance))
     return total, [(0, total), (1, swap(total, axis, 1))]
@@ -637,18 +628,24 @@
     first = max(block_right - block_left, LANES)
     count = lax.axis_size("row")
     gram_right, basis_right = gram_right[0], basis_right[0]
-    window, left = pack(count, first, gram_right, basis_right, gram_left[0], basis_left[0])
+    window, left, keep_right, other_right, keep_left, other_left = first_sends(
+        count,
+        first,
+        grad,
+        gram_right,
+        basis_right,
+        gram_left[0],
+        basis_left[0],
+        1.0 / (block_right * lax.axis_size("col")),
+        1.0 / (block_left * count),
+    )
     near = distances("row")[-2::-1]
     arrived = swap(window, "row", count // 2)
     gram_right, basis_right, _ = lax.optimization_barrier((gram_right, basis_right, arrived))
     grams, bases = spread([(0, gram_right)], "row", near), spread([(0, basis_right)], "row", near)
     others = spread([(count // 2, arrived)], "row", near)
-    grad_after, left = lax.optimization_barrier((grad, left))
-    keep_right, other_right, keep_left, other_left = terms(
-        grad_after, 1.0 / (block_right * lax.axis_size("col")), 1.0 / (block_left * count)
-    )
     left = gather_stacked(left, "col")
-    sent, sums_right = sum_halves(keep_right, other_right, "row", arrived)
+    sent, sums_right = sum_halves(keep_right, other_right, "row")
     sums_left = sum_stacked(keep_left, other_left, "col")
     last, _ = lax.optimization_barrier((basis_right[:, first:], sent))
     last = [(d, swap(last, "row", d)) for d in range(count // 2, count)]

time: 155 us -> 121 us (0.78)
  Pallas kernels: 104 us -> 70.5 us
  waiting for transfers between devices: 24.4 us -> 18.9 us
  starting transfers between devices: 17.6 us -> 21 us
    pallas_call x2 -> x1, Pallas kernels: 37.5 us -> 4.33 us  [first_sends(): pl.pallas_call(functools.partial(first_kernel, count, scale_left, scale_r...]
    ppermute x17, waiting for transfers between devices: 24.4 us -> 18.9 us  [swap(): return lax.ppermute(x, axis, [(i, i ^ distance) for i in range(count)])]
    ppermute x17, starting transfers between devices: 17.6 us -> 21 us  [swap(): return lax.ppermute(x, axis, [(i, i ^ distance) for i in range(count)])]
  transfers between devices with their start and end apart: 17 -> 17, of which waited for: 5 -> 5; matrix products, arithmetic and copies ran while one was open for 4% -> 5% of each run, Pallas kernels for 14% -> 18%
where the time goes in v5:
time: 121 us
  Pallas kernels  70.5 us (58%)
  starting transfers between devices  21 us (17%)
  waiting for transfers between devices  18.9 us (16%)
  other arithmetic  6.1 us (5%)
  local copies, waits for them, and re-layouts  3.06 us (3%)
    pallas_call x1, Pallas kernels, rest(): pl.pallas_call(functools.partial(rest_kernel, *[[d for d, _ in group] for...  43.9 us
    pallas_call x1, Pallas kernels, head(): pl.pallas_call(functools.partial(head_kernel, count, *[[d for d, _ in gro...  22.3 us
    ppermute x17, starting transfers between devices, swap(): return lax.ppermute(x, axis, [(i, i ^ distance) for i in range(count)])  21 us
    ppermute x17, waiting for transfers between devices, swap(): return lax.ppermute(x, axis, [(i, i ^ distance) for i in range(count)])  18.9 us
    pallas_call x1, Pallas kernels, first_sends(): pl.pallas_call(functools.partial(first_kernel, count, scale_left, scale_r...  4.33 us
    convert_element_type x5, other arithmetic, add(): return (x.astype(jnp.float32) + y.astype(jnp.float32)).astype(x.dtype)  3.42 us
    unnamed x36, local copies, waits for them, and re-layouts  3 us
  transfers between devices with their start and end apart: 17, of which 5 were waited for; matrix products, arithmetic and copies ran while one was open for 5% of the time, Pallas kernels for 18%

profile of v5, /device:TPU:0, one launch (start us, length us, event | category | flops | bytes accessed | tf_op | source)
XLA Modules:
  0.0 120.6 jit_solution(6659112186116663651)
XLA Ops:
  0.6 4.3 %shard_map.135 = (f32[224,896]{1,0:T(8,128)}, f32[64,1024]{1,0:T(8,128)}, bf16[448,512]{1,0:T(8,128)(2,1)}, bf16[448,512]{1,0:T(8,128)(2,1)}, bf16[256,384]{1,0:T(8,128)(2,1)}, /*index=5*/bf16[256,384]{1,0:T(8,128)(2,1)}) custom-call(bf16[512,896]{1,0:T(8,128)(2,1)} %refs_3_.1, f32[224,896]{1,0:T(8,128)} %bitcast.13, f32[224,896]{1,0:T(8,128)} %bitcast.8, ...), custom_call_target="tpu_custom_call" | custom-call | tf_op jit(solution)/shard_map/pallas_call | solution.py:274
  5.0 0.0 copy-start.3
  5.0 3.0 %collective-permute-start.12 = (bf16[256,384]{1,0:T(8,128)(2,1)}, bf16[256,384]{1,0:T(8,128)(2,1)S(1)}, u32[]{:S(2)}, u32[]{:S(2)}) collective-permute-start(bf16[256,384]{1,0:T(8,128)(2,1)} %get-tuple-element.37), channel_id=1, source_target_pairs={{0,1},{1,0},{2,3},{3,2},{4,5},{5,4},{6,7},{7,6},{8,9},{9,8},{10,11... | collective-permute-start | bytes 589832 | tf_op jit(solution)/shard_map/ppermute | solution.py:561
  8.0 2.6 %collective-permute-start.9 = (f32[64,1024]{1,0:T(8,128)}, f32[64,1024]{1,0:T(8,128)S(1)}, u32[]{:S(2)}, u32[]{:S(2)}) collective-permute-start(f32[64,1024]{1,0:T(8,128)} %get-tuple-element.35.refs_11_), channel_id=1, source_target_pairs={{0,4},{1,5},{2,6},{3,7},{4,0},{5,1},{6,2},{7,3},{8,12},{9,13},{10,... | collective-permute-start | bytes 786440 | tf_op jit(solution)/shard_map/ppermute | solution.py:561
  10.6 0.0 collective-permute-start.4
  10.6 1.5 %collective-permute-start = (f32[224,896]{1,0:T(8,128)}, f32[224,896]{1,0:T(8,128)}, u32[]{:S(2)}, u32[]{:S(2)}) collective-permute-start(f32[224,896]{1,0:T(8,128)} %get-tuple-element.26), channel_id=1, source_target_pairs={{0,16},{8,24},{16,0},{24,8},{1,17},{9,25},{17,1},{25,9},{2,18},{10... | collective-permute-start | bytes 2408456 | tf_op jit(solution)/shard_map/ppermute | solution.py:561
  12.1 1.0 collective-permute-done.12
  13.1 1.0 add_convert_fusion.2
  14.1 1.9 %collective-permute-start.13 = (bf16[128,384]{1,0:T(8,128)(2,1)S(1)}, bf16[128,384]{1,0:T(8,128)(2,1)S(1)}, u32[]{:S(2)}, u32[]{:S(2)}) collective-permute-start(bf16[128,384]{1,0:T(8,128)(2,1)S(1)} %constant_dynamic-slice_fusion), channel_id=1, source_target_pairs={{0,2},{1,3},{2,0},{3,1},{4,6},{5,7},{6,4},{7,5},{8,10},{9,11},{10,... | collective-permute-start | bytes 294920 | tf_op jit(solution)/shard_map/ppermute | solution.py:561
  16.0 6.6 %collective-permute-done.9.refs_12_ = f32[64,1024]{1,0:T(8,128)S(1)} collective-permute-done((f32[64,1024]{1,0:T(8,128)}, f32[64,1024]{1,0:T(8,128)S(1)}, u32[]{:S(2)}, u32[]{:S(2)}) %collective-permute-start.9) | collective-permute-done | bytes 262176 | tf_op jit(solution)/shard_map/ppermute | solution.py:561
  22.6 1.9 %pad_maximum_fusion.1 = f32[128,1024]{1,0:T(8,128)} fusion(f32[64,1024]{1,0:T(8,128)S(1)} %collective-permute-done.9.refs_12_, f32[64,1024]{1,0:T(8,128)} %get-tuple-element.35.refs_11_), kind=kLoop, calls=%fused_computation.3 | loop fusion | flops 131072 | bytes 1048576 | tf_op jit(solution)/shard_map/concatenate | solution.py:584
  24.5 0.7 collective-permute-start.10
  25.2 0.0 collective-permute-done.4
  25.2 0.8 copy-done.12
  26.0 0.0 copy-done.11
  26.0 1.3 %add_convert_fusion.1 = bf16[448,512]{1,0:T(8,128)(2,1)S(1)} fusion(bf16[448,512]{1,0:T(8,128)(2,1)} %copy-done.12, bf16[448,512]{1,0:T(8,128)(2,1)S(1)} %copy-done.11), kind=kLoop, calls=%fused_computation.2 | loop fusion | flops 917504 | bytes 1376256 | tf_op jit(solution)/shard_map/convert_element_type | solution.py:590
  27.3 1.6 %collective-permute-start.5 = (bf16[448,512]{1,0:T(8,128)(2,1)S(1)}, bf16[448,512]{1,0:T(8,128)(2,1)}, u32[]{:S(2)}, u32[]{:S(2)}) collective-permute-start(bf16[448,512]{1,0:T(8,128)(2,1)S(1)} %add_convert_fusion.1), channel_id=1, source_target_pairs={{0,16},{8,24},{16,0},{24,8},{1,17},{9,25},{17,1},{25,9},{2,18},{10... | collective-permute-start | bytes 1376264 | tf_op jit(solution)/shard_map/ppermute | solution.py:561
  28.8 0.0 collective-permute-done.13
  28.8 3.4 %collective-permute-start.14 = (bf16[128,384]{1,0:T(8,128)(2,1)S(1)}, bf16[128,384]{1,0:T(8,128)(2,1)S(1)}, u32[]{:S(2)}, u32[]{:S(2)}) collective-permute-start(bf16[128,384]{1,0:T(8,128)(2,1)S(1)} %add_convert_fusion.4), channel_id=1, source_target_pairs={{0,4},{1,5},{2,6},{3,7},{4,0},{5,1},{6,2},{7,3},{8,12},{9,13},{10,... | collective-permute-start | bytes 294920 | tf_op jit(solution)/shard_map/ppermute | solution.py:561
  32.2 7.4 %collective-permute-done.10.refs_13_ = f32[128,1024]{1,0:T(8,128)S(1)} collective-permute-done((f32[128,1024]{1,0:T(8,128)}, f32[128,1024]{1,0:T(8,128)S(1)}, u32[]{:S(2)}, u32[]{:S(2)}) %collective-permute-start.10) | collective-permute-done | bytes 524320 | tf_op jit(solution)/shard_map/ppermute | solution.py:561
  39.6 0.0 copy-done.3
  39.6 0.1 pad_maximum_fusion
  39.7 0.0 copy-done.4
  39.7 0.6 collective-permute-start.11
  40.3 0.0 collective-permute-done.refs_4_
  40.3 0.0 copy-done.1
  40.3 0.0 collective-permute-start.1
  40.3 0.0 copy-done
  40.3 0.5 collective-permute-start.2
  40.8 0.2 collective-permute-done.5
  41.1 1.1 add_convert_fusion.refs_6_
  42.2 0.0 copy-start.6
  42.2 0.1 collective-permute-start.6
  42.3 0.0 collective-permute-done.14
  42.3 0.0 copy-done.5
  42.3 0.0 copy-start.8
  42.4 1.6 %collective-permute-start.15 = (bf16[128,384]{1,0:T(8,128)(2,1)S(1)}, bf16[128,384]{1,0:T(8,128)(2,1)S(1)}, u32[]{:S(2)}, u32[]{:S(2)}) collective-permute-start(bf16[128,384]{1,0:T(8,128)(2,1)S(1)} %add_convert_fusion.3.refs_15_), channel_id=1, source_target_pairs={{0,2},{1,3},{2,0},{3,1},{4,6},{5,7},{6,4},{7,5},{8,10},{9,11},{10,... | collective-permute-start | bytes 294920 | tf_op jit(solution)/shard_map/ppermute | solution.py:561
  44.0 3.6 %collective-permute-done.15.refs_16_ = bf16[128,384]{1,0:T(8,128)(2,1)S(1)} collective-permute-done((bf16[128,384]{1,0:T(8,128)(2,1)S(1)}, bf16[128,384]{1,0:T(8,128)(2,1)S(1)}, u32[]{:S(2)}, u32[]{:S(2)}) %collective-permute-start.15) | collective-permute-done | bytes 98336 | tf_op jit(solution)/shard_map/ppermute | solution.py:561
  47.6 0.0 collective-permute-start.3
  47.7 0.0 collective-permute-done.6.refs_7_
  47.7 0.0 copy-start.14
  47.7 1.7 %collective-permute-start.8 = (f32[224,512]{1,0:T(8,128)S(1)}, f32[224,512]{1,0:T(8,128)S(1)}, u32[]{:S(2)}, u32[]{:S(2)}) collective-permute-start(f32[224,512]{1,0:T(8,128)S(1)} %slice.3), channel_id=1, source_target_pairs={{0,24},{8,16},{16,8},{24,0},{1,25},{9,17},{17,9},{25,1},{2,26},{10... | collective-permute-start | bytes 1376264 | tf_op jit(solution)/shard_map/ppermute | solution.py:561
  49.4 0.0 collective-permute-done.1.refs_1_
  49.4 0.5 collective-permute-start.7
  49.9 0.7 pad_maximum_fusion.2
  50.6 0.0 collective-permute-done.2.refs_3_.refs_8_
  50.6 1.3 %collective-permute-start.16 = (bf16[256,384]{1,0:T(8,128)(2,1)}, bf16[256,384]{1,0:T(8,128)(2,1)S(1)}, u32[]{:S(2)}, u32[]{:S(2)}) collective-permute-start(bf16[256,384]{1,0:T(8,128)(2,1)} %pad_maximum_fusion.2), channel_id=1, source_target_pairs={{0,1},{1,0},{2,3},{3,2},{4,5},{5,4},{6,7},{7,6},{8,9},{9,8},{10,11... | collective-permute-start | bytes 589832 | tf_op jit(solution)/shard_map/ppermute | solution.py:561
  51.9 0.0 collective-permute-done.3.refs_5_
  51.9 0.0 copy-done.6
  51.9 0.0 copy-done.14
  51.9 0.0 copy-done.9
  51.9 0.0 copy-start.10
  52.0 0.9 copy-done.10
  52.8 22.3 %shard_map.136 = (f32[224,896]{1,0:T(8,128)}, bf16[896,896]{1,0:T(8,128)(2,1)}, bf16[896,896]{1,0:T(8,128)(2,1)}, f32[896,384]{1,0:T(8,128)}) custom-call(f32[224,896]{1,0:T(8,128)} %bitcast.14, f32[224,896]{1,0:T(8,128)} %copy-done.9, f32[224,896]{1,0:T(8,128)} %bitcast.9, f32[224,896]{1,0:T(8,128)} %copy-done.2, f32[224,896]{1,0:T(8,128)} %collective-permute-done.refs_4_, ...), custom_call_target="tpu_custom_call" | custom-call | tf_op jit(solution)/shard_map/pallas_call | solution.py:399
  75.1 0.0 collective-permute-done.16.refs_17_
  75.1 0.0 collective-permute-done.8.refs_10_
  75.2 0.0 collective-permute-done.7.refs_9_
  75.2 0.0 collective-permute-done.11.refs_14_
  75.2 0.0 copy-start.7
  75.2 0.6 copy-done.17
  75.8 0.2 copy-done.13
  76.0 0.1 copy-done.15
  76.1 0.3 copy-done.7
  76.5 43.9 %shard_map.137 = (f32[512,896]{1,0:T(8,128)}, f32[512,896]{1,0:T(8,128)}, f32[512,896]{1,0:T(8,128)}, f32[224,896]{1,0:T(8,128)}, f32[64,512]{1,0:T(8,128)}, /*index=5*/f32[64,512]{1,0:T(8,128)}) custom-call(bf16[896,896]{1,0:T(8,128)(2,1)} %get-tuple-element.31.refs_0_, bf16[896,896]{1,0:T(8,128)(2,1)} %get-tuple-element.32.refs_1_, ...), custom_call_target="tpu_custom_call" | custom-call | tf_op jit(solution)/shard_map/pallas_call | solution.py:518
  (19 shorter events, 0.1 us)
Async XLA Ops:
  5.0 34.7 %copy-start.3 = (f32[64,1024]{1,0:T(8,128)S(1)}, f32[64,1024]{1,0:T(8,128)}, u32[]{:S(2)}) copy-start(f32[64,1024]{1,0:T(8,128)} %get-tuple-element.35.refs_11_) | copy-start | bytes 786436
  5.0 8.1 %collective-permute-start.12 = (bf16[256,384]{1,0:T(8,128)(2,1)}, bf16[256,384]{1,0:T(8,128)(2,1)S(1)}, u32[]{:S(2)}, u32[]{:S(2)}) collective-permute-start(bf16[256,384]{1,0:T(8,128)(2,1)} %get-tuple-element.37), channel_id=1, source_target_pairs={{0,1},{1,0},{2,3},{3,2},{4,5},{5,4},{6,7},{7,6},{8,9},{9,8},{10,11... | collective-permute-start | bytes 589832 | tf_op jit(solution)/shard_map/ppermute | solution.py:561
  8.0 14.6 %collective-permute-start.9 = (f32[64,1024]{1,0:T(8,128)}, f32[64,1024]{1,0:T(8,128)S(1)}, u32[]{:S(2)}, u32[]{:S(2)}) collective-permute-start(f32[64,1024]{1,0:T(8,128)} %get-tuple-element.35.refs_11_), channel_id=1, source_target_pairs={{0,4},{1,5},{2,6},{3,7},{4,0},{5,1},{6,2},{7,3},{8,12},{9,13},{10,... | collective-permute-start | bytes 786440 | tf_op jit(solution)/shard_map/ppermute | solution.py:561
  10.6 14.6 %collective-permute-start.4 = (bf16[448,512]{1,0:T(8,128)(2,1)}, bf16[448,512]{1,0:T(8,128)(2,1)S(1)}, u32[]{:S(2)}, u32[]{:S(2)}) collective-permute-start(bf16[448,512]{1,0:T(8,128)(2,1)} %get-tuple-element.30), channel_id=1, source_target_pairs={{0,8},{8,0},{16,24},{24,16},{1,9},{9,1},{17,25},{25,17},{2,10},{10... | collective-permute-start | bytes 1376264 | tf_op jit(solution)/shard_map/ppermute | solution.py:561
  10.6 29.7 %collective-permute-start = (f32[224,896]{1,0:T(8,128)}, f32[224,896]{1,0:T(8,128)}, u32[]{:S(2)}, u32[]{:S(2)}) collective-permute-start(f32[224,896]{1,0:T(8,128)} %get-tuple-element.26), channel_id=1, source_target_pairs={{0,16},{8,24},{16,0},{24,8},{1,17},{9,25},{17,1},{25,9},{2,18},{10... | collective-permute-start | bytes 2408456 | tf_op jit(solution)/shard_map/ppermute | solution.py:561
  12.1 13.9 %copy-start.11 = (bf16[448,512]{1,0:T(8,128)(2,1)S(1)}, bf16[448,512]{1,0:T(8,128)(2,1)}, u32[]{:S(2)}) copy-start(bf16[448,512]{1,0:T(8,128)(2,1)} %get-tuple-element.29) | copy-start | bytes 1376260
  14.1 14.7 %collective-permute-start.13 = (bf16[128,384]{1,0:T(8,128)(2,1)S(1)}, bf16[128,384]{1,0:T(8,128)(2,1)S(1)}, u32[]{:S(2)}, u32[]{:S(2)}) collective-permute-start(bf16[128,384]{1,0:T(8,128)(2,1)S(1)} %constant_dynamic-slice_fusion), channel_id=1, source_target_pairs={{0,2},{1,3},{2,0},{3,1},{4,6},{5,7},{6,4},{7,5},{8,10},{9,11},{10,... | collective-permute-start | bytes 294920 | tf_op jit(solution)/shard_map/ppermute | solution.py:561
  22.6 17.1 %copy-start.4 = (f32[64,1024]{1,0:T(8,128)}, f32[64,1024]{1,0:T(8,128)S(1)}, u32[]{:S(2)}) copy-start(f32[64,1024]{1,0:T(8,128)S(1)} %collective-permute-done.9.refs_12_) | copy-start | bytes 786436
  24.5 15.1 %collective-permute-start.10 = (f32[128,1024]{1,0:T(8,128)}, f32[128,1024]{1,0:T(8,128)S(1)}, u32[]{:S(2)}, u32[]{:S(2)}) collective-permute-start(f32[128,1024]{1,0:T(8,128)} %pad_maximum_fusion.1), channel_id=1, source_target_pairs={{0,2},{1,3},{2,0},{3,1},{4,6},{5,7},{6,4},{7,5},{8,10},{9,11},{10,... | collective-permute-start | bytes 1572872 | tf_op jit(solution)/shard_map/ppermute | solution.py:561
  25.2 0.8 copy-start.12
  26.0 14.3 %copy-start.1 = (f32[1,224,896]{2,1,0:T(8,128)S(1)}, f32[1,224,896]{2,1,0:T(8,128)}, u32[]{:S(2)}) copy-start(f32[1,224,896]{2,1,0:T(8,128)} %param.14) | copy-start | bytes 2408452
  26.0 14.3 %copy-start = (f32[1,224,896]{2,1,0:T(8,128)S(1)}, f32[1,224,896]{2,1,0:T(8,128)}, u32[]{:S(2)}) copy-start(f32[1,224,896]{2,1,0:T(8,128)} %param.15) | copy-start | bytes 2408452
  27.3 13.8 %collective-permute-start.5 = (bf16[448,512]{1,0:T(8,128)(2,1)S(1)}, bf16[448,512]{1,0:T(8,128)(2,1)}, u32[]{:S(2)}, u32[]{:S(2)}) collective-permute-start(bf16[448,512]{1,0:T(8,128)(2,1)S(1)} %add_convert_fusion.1), channel_id=1, source_target_pairs={{0,16},{8,24},{16,0},{24,8},{1,17},{9,25},{17,1},{25,9},{2,18},{10... | collective-permute-start | bytes 1376264 | tf_op jit(solution)/shard_map/ppermute | solution.py:561
  28.8 13.4 %collective-permute-start.14 = (bf16[128,384]{1,0:T(8,128)(2,1)S(1)}, bf16[128,384]{1,0:T(8,128)(2,1)S(1)}, u32[]{:S(2)}, u32[]{:S(2)}) collective-permute-start(bf16[128,384]{1,0:T(8,128)(2,1)S(1)} %add_convert_fusion.4), channel_id=1, source_target_pairs={{0,4},{1,5},{2,6},{3,7},{4,0},{5,1},{6,2},{7,3},{8,12},{9,13},{10,... | collective-permute-start | bytes 294920 | tf_op jit(solution)/shard_map/ppermute | solution.py:561
  39.6 2.7 %copy-start.5 = (f32[128,1024]{1,0:T(8,128)}, f32[128,1024]{1,0:T(8,128)S(1)}, u32[]{:S(2)}) copy-start(f32[128,1024]{1,0:T(8,128)S(1)} %collective-permute-done.10.refs_13_) | copy-start | bytes 1572868
  39.7 35.4 %collective-permute-start.11 = (f32[256,1024]{1,0:T(8,128)S(1)}, f32[256,1024]{1,0:T(8,128)S(1)}, u32[]{:S(2)}, u32[]{:S(2)}) collective-permute-start(f32[256,1024]{1,0:T(8,128)S(1)} %pad_maximum_fusion), channel_id=1, source_target_pairs={{0,1},{1,0},{2,3},{3,2},{4,5},{5,4},{6,7},{7,6},{8,9},{9,8},{10,11... | collective-permute-start | bytes 3145736 | tf_op jit(solution)/shard_map/ppermute | solution.py:561
  40.3 9.0 %collective-permute-start.1 = (f32[224,896]{1,0:T(8,128)S(1)}, f32[224,896]{1,0:T(8,128)S(1)}, u32[]{:S(2)}, u32[]{:S(2)}) collective-permute-start(f32[224,896]{1,0:T(8,128)S(1)} %bitcast.15), channel_id=1, source_target_pairs={{0,8},{8,0},{16,24},{24,16},{1,9},{9,1},{17,25},{25,17},{2,10},{10... | collective-permute-start | bytes 2408456 | tf_op jit(solution)/shard_map/ppermute | solution.py:561
  40.3 10.3 %collective-permute-start.2 = (f32[224,896]{1,0:T(8,128)S(1)}, f32[224,896]{1,0:T(8,128)S(1)}, u32[]{:S(2)}, u32[]{:S(2)}) collective-permute-start(f32[224,896]{1,0:T(8,128)S(1)} %bitcast.11), channel_id=1, source_target_pairs={{0,8},{8,0},{16,24},{24,16},{1,9},{9,1},{17,25},{25,17},{2,10},{10... | collective-permute-start | bytes 2408456 | tf_op jit(solution)/shard_map/ppermute | solution.py:561
  42.2 9.7 %copy-start.6 = (bf16[448,512]{1,0:T(8,128)(2,1)}, bf16[448,512]{1,0:T(8,128)(2,1)S(1)}, u32[]{:S(2)}) copy-start(bf16[448,512]{1,0:T(8,128)(2,1)S(1)} %add_convert_fusion.refs_6_) | copy-start | bytes 1376260
  42.2 5.5 %collective-permute-start.6 = (bf16[448,512]{1,0:T(8,128)(2,1)S(1)}, bf16[448,512]{1,0:T(8,128)(2,1)S(1)}, u32[]{:S(2)}, u32[]{:S(2)}) collective-permute-start(bf16[448,512]{1,0:T(8,128)(2,1)S(1)} %add_convert_fusion.refs_6_), channel_id=1, source_target_pairs={{0,8},{8,0},{16,24},{24,16},{1,9},{9,1},{17,25},{25,17},{2,10},{10... | collective-permute-start | bytes 1376264 | tf_op jit(solution)/shard_map/ppermute | solution.py:561
  42.3 32.8 %copy-start.8 = (bf16[128,384]{1,0:T(8,128)(2,1)}, bf16[128,384]{1,0:T(8,128)(2,1)S(1)}, u32[]{:S(2)}) copy-start(bf16[128,384]{1,0:T(8,128)(2,1)S(1)} %add_convert_fusion.3.refs_15_) | copy-start | bytes 294916
  42.4 5.2 %collective-permute-start.15 = (bf16[128,384]{1,0:T(8,128)(2,1)S(1)}, bf16[128,384]{1,0:T(8,128)(2,1)S(1)}, u32[]{:S(2)}, u32[]{:S(2)}) collective-permute-start(bf16[128,384]{1,0:T(8,128)(2,1)S(1)} %add_convert_fusion.3.refs_15_), channel_id=1, source_target_pairs={{0,2},{1,3},{2,0},{3,1},{4,6},{5,7},{6,4},{7,5},{8,10},{9,11},{10,... | collective-permute-start | bytes 294920 | tf_op jit(solution)/shard_map/ppermute | solution.py:561
  47.6 27.5 %copy-start.16 = (bf16[128,384]{1,0:T(8,128)(2,1)}, bf16[128,384]{1,0:T(8,128)(2,1)S(1)}, u32[]{:S(2)}) copy-start(bf16[128,384]{1,0:T(8,128)(2,1)S(1)} %collective-permute-done.15.refs_16_) | copy-start | bytes 294916
  47.6 4.3 %collective-permute-start.3 = (f32[224,896]{1,0:T(8,128)}, f32[224,896]{1,0:T(8,128)S(1)}, u32[]{:S(2)}, u32[]{:S(2)}) collective-permute-start(f32[224,896]{1,0:T(8,128)} %collective-permute-done.refs_4_), channel_id=1, source_target_pairs={{0,8},{8,0},{16,24},{24,16},{1,9},{9,1},{17,25},{25,17},{2,10},{10... | collective-permute-start | bytes 2408456 | tf_op jit(solution)/shard_map/ppermute | solution.py:561
  47.7 4.3 %copy-start.14 = (bf16[448,512]{1,0:T(8,128)(2,1)}, bf16[448,512]{1,0:T(8,128)(2,1)S(1)}, u32[]{:S(2)}) copy-start(bf16[448,512]{1,0:T(8,128)(2,1)S(1)} %collective-permute-done.6.refs_7_) | copy-start | bytes 1376260
  47.7 27.5 %collective-permute-start.8 = (f32[224,512]{1,0:T(8,128)S(1)}, f32[224,512]{1,0:T(8,128)S(1)}, u32[]{:S(2)}, u32[]{:S(2)}) collective-permute-start(f32[224,512]{1,0:T(8,128)S(1)} %slice.3), channel_id=1, source_target_pairs={{0,24},{8,16},{16,8},{24,0},{1,25},{9,17},{17,9},{25,1},{2,26},{10... | collective-permute-start | bytes 1376264 | tf_op jit(solution)/shard_map/ppermute | solution.py:561
  49.4 2.6 %copy-start.9 = (f32[224,896]{1,0:T(8,128)}, f32[224,896]{1,0:T(8,128)S(1)}, u32[]{:S(2)}) copy-start(f32[224,896]{1,0:T(8,128)S(1)} %collective-permute-done.1.refs_1_) | copy-start | bytes 2408452
  49.4 25.8 %collective-permute-start.7 = (f32[224,512]{1,0:T(8,128)S(1)}, f32[224,512]{1,0:T(8,128)S(1)}, u32[]{:S(2)}, u32[]{:S(2)}) collective-permute-start(f32[224,512]{1,0:T(8,128)S(1)} %slice.3), channel_id=1, source_target_pairs={{0,16},{8,24},{16,0},{24,8},{1,17},{9,25},{17,1},{25,9},{2,18},{10... | collective-permute-start | bytes 1376264 | tf_op jit(solution)/shard_map/ppermute | solution.py:561
  50.6 1.3 %copy-start.2 = (f32[224,896]{1,0:T(8,128)}, f32[224,896]{1,0:T(8,128)S(1)}, u32[]{:S(2)}) copy-start(f32[224,896]{1,0:T(8,128)S(1)} %collective-permute-done.2.refs_3_.refs_8_) | copy-start | bytes 2408452
  50.6 24.5 %collective-permute-start.16 = (bf16[256,384]{1,0:T(8,128)(2,1)}, bf16[256,384]{1,0:T(8,128)(2,1)S(1)}, u32[]{:S(2)}, u32[]{:S(2)}) collective-permute-start(bf16[256,384]{1,0:T(8,128)(2,1)} %pad_maximum_fusion.2), channel_id=1, source_target_pairs={{0,1},{1,0},{2,3},{3,2},{4,5},{5,4},{6,7},{7,6},{8,9},{9,8},{10,11... | collective-permute-start | bytes 589832 | tf_op jit(solution)/shard_map/ppermute | solution.py:561
  51.9 0.9 copy-start.10
  75.1 0.7 copy-start.17
  75.1 0.9 copy-start.13
  75.2 1.0 copy-start.15
  75.2 1.3 %copy-start.7 = (f32[256,1024]{1,0:T(8,128)}, f32[256,1024]{1,0:T(8,128)S(1)}, u32[]{:S(2)}) copy-start(f32[256,1024]{1,0:T(8,128)S(1)} %collective-permute-done.11.refs_14_) | copy-start | bytes 3145732

commit v6 on v5

--- a/solution.py
+++ b/solution.py
@@ -32,6 +32,12 @@
     return guess * (2.0 - p * guess)
 
 
+def sum_tree(terms):
+    while len(terms) > 1:
+        terms = [a + b for a, b in zip(terms[::2], terms[1::2])]
+    return terms[0]
+
+
 def inverse_factor(rows):
     count = LANES // ROWS
     rows = list(rows)
@@ -42,7 +48,12 @@
         base = s * ROWS
         pivot = rows[s]
         here = (lanes >= base) & (lanes < base + ROWS)
-        cols = [lane_col(pivot, base + k) for k in range(ROWS)]
+        if s == 0:
+            cols = [lane_col(pivot, k) for k in range(ROWS)]
+        ahead = range(base + ROWS, base + 2 * ROWS) if s < count - 1 else ()
+        across = [lane_col(pivot, c) for c in ahead]
+        next_cols = [lane_col(rows[s + 1], c) for c in ahead]
+        next_coeffs = [lane_col(rows[s + 1], base + k) for k in range(ROWS)] if ahead else None
         full = jnp.where(here, (lanes == subs + base).astype(jnp.float32), pivot)
         forward = full
         pivots = jnp.ones((ROWS, LANES), jnp.float32)
@@ -63,6 +74,11 @@
             for k in range(j + 4, ROWS):
                 x, y = sub_row(cols[k], j), sub_row(cols[k], j + 1)
                 cols[k] = jnp.where(pair, 0.0, cols[k]) - (one * x + two * y)
+            yield
+            across = [
+                jnp.where(pair, 0.0, c) - (one * sub_row(c, j) + two * sub_row(c, j + 1)) for c in across
+            ]
+            yield
             full = jnp.where(pair, 0.0, full) - (one * sub_row(full, j) + two * sub_row(full, j + 1))
             inner = b * reciprocal(a)
             below = subs > j + 1
@@ -75,13 +91,15 @@
             yield
         out.append(jnp.where(lanes < base + ROWS, forward * lax.rsqrt(pivots), 0.0))
         if s < count - 1:
+            cols = [
+                own - sum_tree([next_coeffs[k] * sub_row(c, k) for k in range(ROWS)])
+                for own, c in zip(next_cols, across)
+            ]
+            yield
             spread = [sub_row(full, k) for k in range(ROWS)]
             for i in range(s + 1, count):
-                coeffs = [lane_col(rows[i], base + k) for k in range(ROWS)]
-                terms = [coeffs[k] * spread[k] for k in range(ROWS)]
-                while len(terms) > 1:
-                    terms = [a + b for a, b in zip(terms[::2], terms[1::2])]
-                rows[i] = jnp.where(here, 0.0, rows[i]) - terms[0]
+                coeffs = next_coeffs if i == s + 1 else [lane_col(rows[i], base + k) for k in range(ROWS)]
+                rows[i] = jnp.where(here, 0.0, rows[i]) - sum_tree([coeffs[k] * spread[k] for k in range(ROWS)])
                 yield
     return out
 
@@ -90,7 +108,7 @@
     results = [None] * len(generators)
     live = list(enumerate(generators))
     fills = list(fills)
-    total, turn, done = 250, 0, 0
+    total, turn, done = 350, 0, 0
     while live:
         for at, generator in list(live):
             try:
@@ -578,9 +596,12 @@
     return tuple(lax.dynamic_slice_in_dim(x, at * rows, rows, 0) for at in (own, 1 - own))
 
 
-def gather_stacked(x, axis):
+def gather_stacked(x, axis, after):
     held = [([0], x)]
-    for distance in reversed(distances(axis)):
+    for n, distance in enumerate(reversed(distances(axis))):
+        if 0 < n <= len(after):
+            (ats, piece), (piece_after, _) = held[-1], lax.optimization_barrier((held[-1][1], after[n - 1]))
+            held[-1] = (ats, piece_after)
         sent = jnp.concatenate([piece for _, piece in held]) if len(held) > 1 else x
         held.append(([at ^ distance for ats, _ in held for at in ats], swap(sent, axis, distance)))
     return held
@@ -604,23 +625,27 @@
 def sum_stacked(keep, other, axis):
     steps, weights = distances(axis), piece_weights(axis)
     x = None
+    sums = []
     for distance in steps[:-1]:
         if x is not None:
             keep, other = parts(x, axis, distance)
         x = add(keep, swap(other, axis, distance))
+        sums.append(x)
     x = add(x, swap(x, axis, steps[-1]))
     held = [([0], x)]
     for distance, weight in reversed(list(zip(steps, weights))):
         sent = jnp.concatenate([piece for _, piece in held]) if len(held) > 1 else x
         held.append(([at ^ weight for ats, _ in held for at in ats], swap(sent, axis, distance)))
-    return held
+    return sums + [x], held
 
 
 def sum_halves(keep, other, axis):
     total = add(keep, swap(other, axis, 1))
+    steps = [total]
     for distance in distances(axis)[1:]:
         total = add(total, swap(total, axis, distance))
-    return total, [(0, total), (1, swap(total, axis, 1))]
+        steps.append(total)
+    return steps, [(0, total), (1, swap(total, axis, 1))]
 
 
 def body(grad, weight, moment, second, gram_left, basis_left, gram_right, basis_right):
@@ -644,10 +669,10 @@
     gram_right, basis_right, _ = lax.optimization_barrier((gram_right, basis_right, arrived))
     grams, bases = spread([(0, gram_right)], "row", near), spread([(0, basis_right)], "row", near)
     others = spread([(count // 2, arrived)], "row", near)
-    left = gather_stacked(left, "col")
-    sent, sums_right = sum_halves(keep_right, other_right, "row")
-    sums_left = sum_stacked(keep_left, other_left, "col")
-    last, _ = lax.optimization_barrier((basis_right[:, first:], sent))
+    steps_right, sums_right = sum_halves(keep_right, other_right, "row")
+    steps_left, sums_left = sum_stacked(keep_left, other_left, "col")
+    left = gather_stacked(left, "col", [(steps_right[0], steps_left[-2]), (steps_right[-1], sums_left[min(1, len(sums_left) - 1)][1])])
+    last, _ = lax.optimization_barrier((basis_right[:, first:], steps_right[-1]))
     last = [(d, swap(last, "row", d)) for d in range(count // 2, count)]
     new_gram_right, gh, gl, q_first = head(count, grams, bases, others, sums_right, first)
     new_weight, new_moment, new_second, basis_rows_right, basis_rows_left, new_gram_left = rest(

time: 121 us -> 118 us (0.975)
  starting transfers between devices: 21 us -> 24.8 us
  other arithmetic: 6.1 us -> 2.52 us
  waiting for transfers between devices: 18.9 us -> 16 us
  Pallas kernels: 70.5 us -> 72.3 us
  local copies, waits for them, and re-layouts: 3.06 us -> 1.48 us
    ppermute x17, starting transfers between devices: 21 us -> 24.8 us  [swap(): return lax.ppermute(x, axis, [(i, i ^ distance) for i in range(count)])]
    pallas_call x1, Pallas kernels: 43.9 us -> 47.1 us  [rest(): pl.pallas_call(functools.partial(rest_kernel, *[[d for d, _ in group] for...]
    ppermute x17, waiting for transfers between devices: 18.9 us -> 16 us  [swap(): return lax.ppermute(x, axis, [(i, i ^ distance) for i in range(count)])]
    concatenate x2, other arithmetic: 1.97 us -> 0.14 us  [gather_stacked(): sent = jnp.concatenate([piece for _, piece in held]) if len(held) > 1 else x]
    unnamed x36 -> x30, local copies, waits for them, and re-layouts: 3 us -> 1.41 us
    pallas_call x1, Pallas kernels: 22.3 us -> 20.9 us  [head(): pl.pallas_call(functools.partial(head_kernel, count, *[[d for d, _ in gro...]
  transfers between devices with their start and end apart: 17 -> 17, of which waited for: 5 -> 6; matrix products, arithmetic and copies ran while one was open for 5% -> 2% of each run, Pallas kernels for 18% -> 18%
where the time goes in v6:
time: 118 us
  Pallas kernels  72.3 us (61%)
  starting transfers between devices  24.8 us (21%)
  waiting for transfers between devices  16 us (14%)
  other arithmetic  2.52 us (2%)
  local copies, waits for them, and re-layouts  1.48 us (1%)
    pallas_call x1, Pallas kernels, rest(): pl.pallas_call(functools.partial(rest_kernel, *[[d for d, _ in group] for...  47.1 us
    ppermute x17, starting transfers between devices, swap(): return lax.ppermute(x, axis, [(i, i ^ distance) for i in range(count)])  24.8 us
    pallas_call x1, Pallas kernels, head(): pl.pallas_call(functools.partial(head_kernel, count, *[[d for d, _ in gro...  20.9 us
    ppermute x17, waiting for transfers between devices, swap(): return lax.ppermute(x, axis, [(i, i ^ distance) for i in range(count)])  16 us
    pallas_call x1, Pallas kernels, first_sends(): pl.pallas_call(functools.partial(first_kernel, count, scale_left, scale_r...  4.33 us
  transfers between devices with their start and end apart: 17, of which 6 were waited for; matrix products, arithmetic and copies ran while one was open for 2% of the time, Pallas kernels for 18%

profile of v6, /device:TPU:0, one launch (start us, length us, event | category | flops | bytes accessed | tf_op | source)
XLA Modules:
  0.0 118.2 jit_solution(16443176021270461190)
XLA Ops:
  0.6 4.3 %shard_map.135 = (f32[224,896]{1,0:T(8,128)}, f32[64,1024]{1,0:T(8,128)}, bf16[448,512]{1,0:T(8,128)(2,1)}, bf16[448,512]{1,0:T(8,128)(2,1)}, bf16[256,384]{1,0:T(8,128)(2,1)}, /*index=5*/bf16[256,384]{1,0:T(8,128)(2,1)}) custom-call(bf16[512,896]{1,0:T(8,128)(2,1)} %refs_3_.1, f32[224,896]{1,0:T(8,128)} %bitcast.13, f32[224,896]{1,0:T(8,128)} %bitcast.8, ...), custom_call_target="tpu_custom_call" | custom-call | tf_op jit(solution)/shard_map/pallas_call | solution.py:292
  5.0 0.0 copy-start.3
  5.0 3.0 %collective-permute-start.10 = (bf16[256,384]{1,0:T(8,128)(2,1)}, bf16[256,384]{1,0:T(8,128)(2,1)S(1)}, u32[]{:S(2)}, u32[]{:S(2)}) collective-permute-start(bf16[256,384]{1,0:T(8,128)(2,1)} %get-tuple-element.39), channel_id=1, source_target_pairs={{0,1},{1,0},{2,3},{3,2},{4,5},{5,4},{6,7},{7,6},{8,9},{9,8},{10,11... | collective-permute-start | bytes 589832 | tf_op jit(solution)/shard_map/ppermute | solution.py:579
  8.0 0.0 collective-permute-start.4
  8.0 2.6 %collective-permute-start.9 = (f32[64,1024]{1,0:T(8,128)}, f32[64,1024]{1,0:T(8,128)S(1)}, u32[]{:S(2)}, u32[]{:S(2)}) collective-permute-start(f32[64,1024]{1,0:T(8,128)} %get-tuple-element.37.refs_11_), channel_id=1, source_target_pairs={{0,4},{1,5},{2,6},{3,7},{4,0},{5,1},{6,2},{7,3},{8,12},{9,13},{10,... | collective-permute-start | bytes 786440 | tf_op jit(solution)/shard_map/ppermute | solution.py:579
  10.6 1.5 %collective-permute-start = (f32[224,896]{1,0:T(8,128)}, f32[224,896]{1,0:T(8,128)S(1)}, u32[]{:S(2)}, u32[]{:S(2)}) collective-permute-start(f32[224,896]{1,0:T(8,128)} %get-tuple-element.28), channel_id=1, source_target_pairs={{0,16},{8,24},{16,0},{24,8},{1,17},{9,25},{17,1},{25,9},{2,18},{10... | collective-permute-start | bytes 2408456 | tf_op jit(solution)/shard_map/ppermute | solution.py:579
  12.1 1.0 collective-permute-done.10
  13.1 1.1 add_convert_fusion.2
  14.2 1.9 %collective-permute-start.11 = (bf16[128,384]{1,0:T(8,128)(2,1)S(1)}, bf16[128,384]{1,0:T(8,128)(2,1)S(1)}, u32[]{:S(2)}, u32[]{:S(2)}) collective-permute-start(bf16[128,384]{1,0:T(8,128)(2,1)S(1)} %constant_dynamic-slice_fusion), channel_id=1, source_target_pairs={{0,2},{1,3},{2,0},{3,1},{4,6},{5,7},{6,4},{7,5},{8,10},{9,11},{10,... | collective-permute-start | bytes 294920 | tf_op jit(solution)/shard_map/ppermute | solution.py:579
  16.1 0.0 collective-permute-done.4
  16.1 1.1 add_convert_fusion.1
  17.2 1.6 %collective-permute-start.5 = (bf16[448,512]{1,0:T(8,128)(2,1)S(1)}, bf16[448,512]{1,0:T(8,128)(2,1)S(1)}, u32[]{:S(2)}, u32[]{:S(2)}) collective-permute-start(bf16[448,512]{1,0:T(8,128)(2,1)S(1)} %add_convert_fusion.1), channel_id=1, source_target_pairs={{0,16},{8,24},{16,0},{24,8},{1,17},{9,25},{17,1},{25,9},{2,18},{10... | collective-permute-start | bytes 1376264 | tf_op jit(solution)/shard_map/ppermute | solution.py:579
  18.8 0.4 collective-permute-done.11
  19.2 5.1 %collective-permute-start.13 = (bf16[128,384]{1,0:T(8,128)(2,1)S(1)}, bf16[128,384]{1,0:T(8,128)(2,1)S(1)}, u32[]{:S(2)}, u32[]{:S(2)}) collective-permute-start(bf16[128,384]{1,0:T(8,128)(2,1)S(1)} %add_convert_fusion.4), channel_id=1, source_target_pairs={{0,4},{1,5},{2,6},{3,7},{4,0},{5,1},{6,2},{7,3},{8,12},{9,13},{10,... | collective-permute-start | bytes 294920 | tf_op jit(solution)/shard_map/ppermute | solution.py:579
  24.4 0.0 collective-permute-done.9.refs_12_
  24.4 0.0 copy-done.3
  24.4 0.0 copy-start
  24.4 2.5 %collective-permute-start.12 = (f32[128,1024]{1,0:T(8,128)S(1)}, f32[128,1024]{1,0:T(8,128)S(1)}, u32[]{:S(2)}, u32[]{:S(2)}) collective-permute-start(f32[128,1024]{1,0:T(8,128)S(1)} %pad_maximum_fusion.1), channel_id=1, source_target_pairs={{0,2},{1,3},{2,0},{3,1},{4,6},{5,7},{6,4},{7,5},{8,10},{9,11},{10,... | collective-permute-start | bytes 1572872 | tf_op jit(solution)/shard_map/ppermute | solution.py:579
  27.0 0.4 collective-permute-done.13
  27.4 0.0 copy-start.8
  27.4 2.2 %collective-permute-start.14 = (bf16[128,384]{1,0:T(8,128)(2,1)S(1)}, bf16[128,384]{1,0:T(8,128)(2,1)S(1)}, u32[]{:S(2)}, u32[]{:S(2)}) collective-permute-start(bf16[128,384]{1,0:T(8,128)(2,1)S(1)} %add_convert_fusion.3.refs_15_), channel_id=1, source_target_pairs={{0,2},{1,3},{2,0},{3,1},{4,6},{5,7},{6,4},{7,5},{8,10},{9,11},{10,... | collective-permute-start | bytes 294920 | tf_op jit(solution)/shard_map/ppermute | solution.py:579
  29.6 2.0 %collective-permute-done.refs_4_ = f32[224,896]{1,0:T(8,128)S(1)} collective-permute-done((f32[224,896]{1,0:T(8,128)}, f32[224,896]{1,0:T(8,128)S(1)}, u32[]{:S(2)}, u32[]{:S(2)}) %collective-permute-start) | collective-permute-done | bytes 802848 | tf_op jit(solution)/shard_map/ppermute | solution.py:579
  31.5 0.0 copy-done.1
  31.5 0.0 collective-permute-start.1
  31.6 9.1 %collective-permute-done.5 = bf16[448,512]{1,0:T(8,128)(2,1)S(1)} collective-permute-done((bf16[448,512]{1,0:T(8,128)(2,1)S(1)}, bf16[448,512]{1,0:T(8,128)(2,1)S(1)}, u32[]{:S(2)}, u32[]{:S(2)}) %collective-permute-start.5) | collective-permute-done | bytes 458784 | tf_op jit(solution)/shard_map/ppermute | solution.py:579
  40.7 0.1 add_convert_fusion.refs_6_
  40.8 0.0 copy-start.6
  40.8 0.0 collective-permute-done.14.refs_16_
  40.8 0.0 copy-start.13
  40.8 0.0 collective-permute-done.12.refs_13_
  40.8 0.0 copy-start.5
  40.8 0.1 pad_maximum_fusion
  41.0 0.0 copy-done.4
  41.0 1.4 %collective-permute-start.15 = (f32[256,1024]{1,0:T(8,128)S(1)}, f32[256,1024]{1,0:T(8,128)S(1)}, u32[]{:S(2)}, u32[]{:S(2)}) collective-permute-start(f32[256,1024]{1,0:T(8,128)S(1)} %pad_maximum_fusion), channel_id=1, source_target_pairs={{0,1},{1,0},{2,3},{3,2},{4,5},{5,4},{6,7},{7,6},{8,9},{9,8},{10,11... | collective-permute-start | bytes 3145736 | tf_op jit(solution)/shard_map/ppermute | solution.py:579
  42.4 0.0 copy-done
  42.4 0.0 collective-permute-start.2
  42.4 0.5 collective-permute-start.6
  42.9 0.0 collective-permute-start.3
  43.0 0.0 copy-done.9
  43.0 3.0 %collective-permute-done.6.refs_7_ = bf16[448,512]{1,0:T(8,128)(2,1)S(1)} collective-permute-done((bf16[448,512]{1,0:T(8,128)(2,1)S(1)}, bf16[448,512]{1,0:T(8,128)(2,1)S(1)}, u32[]{:S(2)}, u32[]{:S(2)}) %collective-permute-start.6) | collective-permute-done | bytes 458784 | tf_op jit(solution)/shard_map/ppermute | solution.py:579
  46.0 1.2 %collective-permute-start.8 = (f32[224,512]{1,0:T(8,128)S(1)}, f32[224,512]{1,0:T(8,128)}, u32[]{:S(2)}, u32[]{:S(2)}) collective-permute-start(f32[224,512]{1,0:T(8,128)S(1)} %slice.3), channel_id=1, source_target_pairs={{0,24},{8,16},{16,8},{24,0},{1,25},{9,17},{17,9},{25,1},{2,26},{10... | collective-permute-start | bytes 1376264 | tf_op jit(solution)/shard_map/ppermute | solution.py:579
  47.2 0.0 collective-permute-done.1.refs_1_
  47.2 0.6 collective-permute-start.7
  47.8 0.0 copy-done.8
  47.8 0.0 collective-permute-done.2.refs_3_.refs_8_
  47.8 0.0 copy-done.12
  47.9 0.0 copy-start.2
  47.9 0.7 collective-permute-start.16
  48.6 0.0 collective-permute-done.3.refs_5_
  48.6 0.0 copy-done.6
  48.6 0.0 copy-done.10
  48.6 0.1 copy-done.2
  48.8 20.9 %shard_map.136 = (f32[224,896]{1,0:T(8,128)}, bf16[896,896]{1,0:T(8,128)(2,1)}, bf16[896,896]{1,0:T(8,128)(2,1)}, f32[896,384]{1,0:T(8,128)}) custom-call(f32[224,896]{1,0:T(8,128)} %bitcast.14, f32[224,896]{1,0:T(8,128)} %copy-done.10, f32[224,896]{1,0:T(8,128)} %bitcast.9, f32[224,896]{1,0:T(8,128)} %copy-done.2, f32[224,896]{1,0:T(8,128)} %copy-done.9, ...), custom_call_target="tpu_custom_call" | custom-call | tf_op jit(solution)/shard_map/pallas_call | solution.py:417
  69.7 0.0 copy-done.13
  69.7 0.0 collective-permute-done.16.refs_17_
  69.7 0.0 copy-start.14
  69.7 0.0 collective-permute-done.8.refs_10_
  69.7 0.0 collective-permute-done.7.refs_9_
  69.8 0.0 collective-permute-done.15.refs_14_
  69.8 0.0 copy-start.7
  69.8 0.6 copy-done.14
  70.4 0.2 copy-done.11
  70.6 0.4 copy-done.7
  71.0 47.1 %shard_map.137 = (f32[512,896]{1,0:T(8,128)}, f32[512,896]{1,0:T(8,128)}, f32[512,896]{1,0:T(8,128)}, f32[224,896]{1,0:T(8,128)}, f32[64,512]{1,0:T(8,128)}, /*index=5*/f32[64,512]{1,0:T(8,128)}) custom-call(bf16[896,896]{1,0:T(8,128)(2,1)} %get-tuple-element.33.refs_0_, bf16[896,896]{1,0:T(8,128)(2,1)} %get-tuple-element.34.refs_1_, ...), custom_call_target="tpu_custom_call" | custom-call | tf_op jit(solution)/shard_map/pallas_call | solution.py:536
  (13 shorter events, 0.2 us)
Async XLA Ops:
  5.0 19.4 %copy-start.3 = (f32[64,1024]{1,0:T(8,128)S(1)}, f32[64,1024]{1,0:T(8,128)}, u32[]{:S(2)}) copy-start(f32[64,1024]{1,0:T(8,128)} %get-tuple-element.37.refs_11_) | copy-start | bytes 786436
  5.0 8.1 %collective-permute-start.10 = (bf16[256,384]{1,0:T(8,128)(2,1)}, bf16[256,384]{1,0:T(8,128)(2,1)S(1)}, u32[]{:S(2)}, u32[]{:S(2)}) collective-permute-start(bf16[256,384]{1,0:T(8,128)(2,1)} %get-tuple-element.39), channel_id=1, source_target_pairs={{0,1},{1,0},{2,3},{3,2},{4,5},{5,4},{6,7},{7,6},{8,9},{9,8},{10,11... | collective-permute-start | bytes 589832 | tf_op jit(solution)/shard_map/ppermute | solution.py:579
  8.0 8.1 %collective-permute-start.4 = (bf16[448,512]{1,0:T(8,128)(2,1)}, bf16[448,512]{1,0:T(8,128)(2,1)S(1)}, u32[]{:S(2)}, u32[]{:S(2)}) collective-permute-start(bf16[448,512]{1,0:T(8,128)(2,1)} %get-tuple-element.32), channel_id=1, source_target_pairs={{0,8},{8,0},{16,24},{24,16},{1,9},{9,1},{17,25},{25,17},{2,10},{10... | collective-permute-start | bytes 1376264 | tf_op jit(solution)/shard_map/ppermute | solution.py:579
  8.0 16.3 %collective-permute-start.9 = (f32[64,1024]{1,0:T(8,128)}, f32[64,1024]{1,0:T(8,128)S(1)}, u32[]{:S(2)}, u32[]{:S(2)}) collective-permute-start(f32[64,1024]{1,0:T(8,128)} %get-tuple-element.37.refs_11_), channel_id=1, source_target_pairs={{0,4},{1,5},{2,6},{3,7},{4,0},{5,1},{6,2},{7,3},{8,12},{9,13},{10,... | collective-permute-start | bytes 786440 | tf_op jit(solution)/shard_map/ppermute | solution.py:579
  10.6 20.9 %collective-permute-start = (f32[224,896]{1,0:T(8,128)}, f32[224,896]{1,0:T(8,128)S(1)}, u32[]{:S(2)}, u32[]{:S(2)}) collective-permute-start(f32[224,896]{1,0:T(8,128)} %get-tuple-element.28), channel_id=1, source_target_pairs={{0,16},{8,24},{16,0},{24,8},{1,17},{9,25},{17,1},{25,9},{2,18},{10... | collective-permute-start | bytes 2408456 | tf_op jit(solution)/shard_map/ppermute | solution.py:579
  13.1 18.4 %copy-start.1 = (f32[1,224,896]{2,1,0:T(8,128)S(1)}, f32[1,224,896]{2,1,0:T(8,128)}, u32[]{:S(2)}) copy-start(f32[1,224,896]{2,1,0:T(8,128)} %param.14) | copy-start | bytes 2408452
  14.2 5.0 %collective-permute-start.11 = (bf16[128,384]{1,0:T(8,128)(2,1)S(1)}, bf16[128,384]{1,0:T(8,128)(2,1)S(1)}, u32[]{:S(2)}, u32[]{:S(2)}) collective-permute-start(bf16[128,384]{1,0:T(8,128)(2,1)S(1)} %constant_dynamic-slice_fusion), channel_id=1, source_target_pairs={{0,2},{1,3},{2,0},{3,1},{4,6},{5,7},{6,4},{7,5},{8,10},{9,11},{10,... | collective-permute-start | bytes 294920 | tf_op jit(solution)/shard_map/ppermute | solution.py:579
  17.2 23.5 %collective-permute-start.5 = (bf16[448,512]{1,0:T(8,128)(2,1)S(1)}, bf16[448,512]{1,0:T(8,128)(2,1)S(1)}, u32[]{:S(2)}, u32[]{:S(2)}) collective-permute-start(bf16[448,512]{1,0:T(8,128)(2,1)S(1)} %add_convert_fusion.1), channel_id=1, source_target_pairs={{0,16},{8,24},{16,0},{24,8},{1,17},{9,25},{17,1},{25,9},{2,18},{10... | collective-permute-start | bytes 1376264 | tf_op jit(solution)/shard_map/ppermute | solution.py:579
  19.2 8.1 %collective-permute-start.13 = (bf16[128,384]{1,0:T(8,128)(2,1)S(1)}, bf16[128,384]{1,0:T(8,128)(2,1)S(1)}, u32[]{:S(2)}, u32[]{:S(2)}) collective-permute-start(bf16[128,384]{1,0:T(8,128)(2,1)S(1)} %add_convert_fusion.4), channel_id=1, source_target_pairs={{0,4},{1,5},{2,6},{3,7},{4,0},{5,1},{6,2},{7,3},{8,12},{9,13},{10,... | collective-permute-start | bytes 294920 | tf_op jit(solution)/shard_map/ppermute | solution.py:579
  24.4 16.6 %copy-start.4 = (f32[64,1024]{1,0:T(8,128)}, f32[64,1024]{1,0:T(8,128)S(1)}, u32[]{:S(2)}) copy-start(f32[64,1024]{1,0:T(8,128)S(1)} %collective-permute-done.9.refs_12_) | copy-start | bytes 786436
  24.4 18.0 %copy-start = (f32[1,224,896]{2,1,0:T(8,128)S(1)}, f32[1,224,896]{2,1,0:T(8,128)}, u32[]{:S(2)}) copy-start(f32[1,224,896]{2,1,0:T(8,128)} %param.15) | copy-start | bytes 2408452
  24.4 16.4 %collective-permute-start.12 = (f32[128,1024]{1,0:T(8,128)S(1)}, f32[128,1024]{1,0:T(8,128)S(1)}, u32[]{:S(2)}, u32[]{:S(2)}) collective-permute-start(f32[128,1024]{1,0:T(8,128)S(1)} %pad_maximum_fusion.1), channel_id=1, source_target_pairs={{0,2},{1,3},{2,0},{3,1},{4,6},{5,7},{6,4},{7,5},{8,10},{9,11},{10,... | collective-permute-start | bytes 1572872 | tf_op jit(solution)/shard_map/ppermute | solution.py:579
  27.4 20.4 %copy-start.8 = (bf16[128,384]{1,0:T(8,128)(2,1)}, bf16[128,384]{1,0:T(8,128)(2,1)S(1)}, u32[]{:S(2)}) copy-start(bf16[128,384]{1,0:T(8,128)(2,1)S(1)} %add_convert_fusion.3.refs_15_) | copy-start | bytes 294916
  27.4 13.4 %collective-permute-start.14 = (bf16[128,384]{1,0:T(8,128)(2,1)S(1)}, bf16[128,384]{1,0:T(8,128)(2,1)S(1)}, u32[]{:S(2)}, u32[]{:S(2)}) collective-permute-start(bf16[128,384]{1,0:T(8,128)(2,1)S(1)} %add_convert_fusion.3.refs_15_), channel_id=1, source_target_pairs={{0,2},{1,3},{2,0},{3,1},{4,6},{5,7},{6,4},{7,5},{8,10},{9,11},{10,... | collective-permute-start | bytes 294920 | tf_op jit(solution)/shard_map/ppermute | solution.py:579
  31.5 11.4 %copy-start.9 = (f32[224,896]{1,0:T(8,128)}, f32[224,896]{1,0:T(8,128)S(1)}, u32[]{:S(2)}) copy-start(f32[224,896]{1,0:T(8,128)S(1)} %collective-permute-done.refs_4_) | copy-start | bytes 2408452
  31.5 15.7 %collective-permute-start.1 = (f32[224,896]{1,0:T(8,128)S(1)}, f32[224,896]{1,0:T(8,128)S(1)}, u32[]{:S(2)}, u32[]{:S(2)}) collective-permute-start(f32[224,896]{1,0:T(8,128)S(1)} %bitcast.15), channel_id=1, source_target_pairs={{0,8},{8,0},{16,24},{24,16},{1,9},{9,1},{17,25},{25,17},{2,10},{10... | collective-permute-start | bytes 2408456 | tf_op jit(solution)/shard_map/ppermute | solution.py:579
  40.8 7.8 %copy-start.6 = (bf16[448,512]{1,0:T(8,128)(2,1)}, bf16[448,512]{1,0:T(8,128)(2,1)S(1)}, u32[]{:S(2)}) copy-start(bf16[448,512]{1,0:T(8,128)(2,1)S(1)} %add_convert_fusion.refs_6_) | copy-start | bytes 1376260
  40.8 28.9 %copy-start.13 = (bf16[128,384]{1,0:T(8,128)(2,1)}, bf16[128,384]{1,0:T(8,128)(2,1)S(1)}, u32[]{:S(2)}) copy-start(bf16[128,384]{1,0:T(8,128)(2,1)S(1)} %collective-permute-done.14.refs_16_) | copy-start | bytes 294916
  40.8 28.9 %copy-start.5 = (f32[128,1024]{1,0:T(8,128)}, f32[128,1024]{1,0:T(8,128)S(1)}, u32[]{:S(2)}) copy-start(f32[128,1024]{1,0:T(8,128)S(1)} %collective-permute-done.12.refs_13_) | copy-start | bytes 1572868
  41.0 28.8 %collective-permute-start.15 = (f32[256,1024]{1,0:T(8,128)S(1)}, f32[256,1024]{1,0:T(8,128)S(1)}, u32[]{:S(2)}, u32[]{:S(2)}) collective-permute-start(f32[256,1024]{1,0:T(8,128)S(1)} %pad_maximum_fusion), channel_id=1, source_target_pairs={{0,1},{1,0},{2,3},{3,2},{4,5},{5,4},{6,7},{7,6},{8,9},{9,8},{10,11... | collective-permute-start | bytes 3145736 | tf_op jit(solution)/shard_map/ppermute | solution.py:579
  42.4 5.4 %collective-permute-start.2 = (f32[224,896]{1,0:T(8,128)S(1)}, f32[224,896]{1,0:T(8,128)S(1)}, u32[]{:S(2)}, u32[]{:S(2)}) collective-permute-start(f32[224,896]{1,0:T(8,128)S(1)} %bitcast.11), channel_id=1, source_target_pairs={{0,8},{8,0},{16,24},{24,16},{1,9},{9,1},{17,25},{25,17},{2,10},{10... | collective-permute-start | bytes 2408456 | tf_op jit(solution)/shard_map/ppermute | solution.py:579
  42.4 3.6 %collective-permute-start.6 = (bf16[448,512]{1,0:T(8,128)(2,1)S(1)}, bf16[448,512]{1,0:T(8,128)(2,1)S(1)}, u32[]{:S(2)}, u32[]{:S(2)}) collective-permute-start(bf16[448,512]{1,0:T(8,128)(2,1)S(1)} %add_convert_fusion.refs_6_), channel_id=1, source_target_pairs={{0,8},{8,0},{16,24},{24,16},{1,9},{9,1},{17,25},{25,17},{2,10},{10... | collective-permute-start | bytes 1376264 | tf_op jit(solution)/shard_map/ppermute | solution.py:579
  42.9 5.7 %collective-permute-start.3 = (f32[224,896]{1,0:T(8,128)S(1)}, f32[224,896]{1,0:T(8,128)}, u32[]{:S(2)}, u32[]{:S(2)}) collective-permute-start(f32[224,896]{1,0:T(8,128)S(1)} %collective-permute-done.refs_4_), channel_id=1, source_target_pairs={{0,8},{8,0},{16,24},{24,16},{1,9},{9,1},{17,25},{25,17},{2,10},{10... | collective-permute-start | bytes 2408456 | tf_op jit(solution)/shard_map/ppermute | solution.py:579
  46.0 1.8 %copy-start.12 = (bf16[448,512]{1,0:T(8,128)(2,1)}, bf16[448,512]{1,0:T(8,128)(2,1)S(1)}, u32[]{:S(2)}) copy-start(bf16[448,512]{1,0:T(8,128)(2,1)S(1)} %collective-permute-done.6.refs_7_) | copy-start | bytes 1376260
  46.0 23.7 %collective-permute-start.8 = (f32[224,512]{1,0:T(8,128)S(1)}, f32[224,512]{1,0:T(8,128)}, u32[]{:S(2)}, u32[]{:S(2)}) collective-permute-start(f32[224,512]{1,0:T(8,128)S(1)} %slice.3), channel_id=1, source_target_pairs={{0,24},{8,16},{16,8},{24,0},{1,25},{9,17},{17,9},{25,1},{2,26},{10... | collective-permute-start | bytes 1376264 | tf_op jit(solution)/shard_map/ppermute | solution.py:579
  47.2 1.4 %copy-start.10 = (f32[224,896]{1,0:T(8,128)}, f32[224,896]{1,0:T(8,128)S(1)}, u32[]{:S(2)}) copy-start(f32[224,896]{1,0:T(8,128)S(1)} %collective-permute-done.1.refs_1_) | copy-start | bytes 2408452
  47.2 22.5 %collective-permute-start.7 = (f32[224,512]{1,0:T(8,128)S(1)}, f32[224,512]{1,0:T(8,128)S(1)}, u32[]{:S(2)}, u32[]{:S(2)}) collective-permute-start(f32[224,512]{1,0:T(8,128)S(1)} %slice.3), channel_id=1, source_target_pairs={{0,16},{8,24},{16,0},{24,8},{1,17},{9,25},{17,1},{25,9},{2,18},{10... | collective-permute-start | bytes 1376264 | tf_op jit(solution)/shard_map/ppermute | solution.py:579
  47.9 0.9 copy-start.2
  47.9 21.9 %collective-permute-start.16 = (bf16[256,384]{1,0:T(8,128)(2,1)S(1)}, bf16[256,384]{1,0:T(8,128)(2,1)S(1)}, u32[]{:S(2)}, u32[]{:S(2)}) collective-permute-start(bf16[256,384]{1,0:T(8,128)(2,1)S(1)} %pad_maximum_fusion.2), channel_id=1, source_target_pairs={{0,1},{1,0},{2,3},{3,2},{4,5},{5,4},{6,7},{7,6},{8,9},{9,8},{10,11... | collective-permute-start | bytes 589832 | tf_op jit(solution)/shard_map/ppermute | solution.py:579
  69.7 0.7 copy-start.14
  69.8 0.9 copy-start.11
  69.8 1.2 %copy-start.7 = (f32[256,1024]{1,0:T(8,128)}, f32[256,1024]{1,0:T(8,128)S(1)}, u32[]{:S(2)}) copy-start(f32[256,1024]{1,0:T(8,128)S(1)} %collective-permute-done.15.refs_14_) | copy-start | bytes 3145732

commit v7 on v6

--- a/solution.py
+++ b/solution.py
@@ -38,7 +38,7 @@
     return terms[0]
 
 
-def inverse_factor(rows):
+def inverse_factor(rows, carry):
     count = LANES // ROWS
     rows = list(rows)
     subs = lax.broadcasted_iota(jnp.int32, (ROWS, LANES), 0)
@@ -48,9 +48,9 @@
         base = s * ROWS
         pivot = rows[s]
         here = (lanes >= base) & (lanes < base + ROWS)
-        if s == 0:
-            cols = [lane_col(pivot, k) for k in range(ROWS)]
-        ahead = range(base + ROWS, base + 2 * ROWS) if s < count - 1 else ()
+        if s == 0 or not carry:
+            cols = [lane_col(pivot, base + k) for k in range(ROWS)]
+        ahead = range(base + ROWS, base + 2 * ROWS) if carry and s < count - 1 else ()
         across = [lane_col(pivot, c) for c in ahead]
         next_cols = [lane_col(rows[s + 1], c) for c in ahead]
         next_coeffs = [lane_col(rows[s + 1], base + k) for k in range(ROWS)] if ahead else None
@@ -74,11 +74,12 @@
             for k in range(j + 4, ROWS):
                 x, y = sub_row(cols[k], j), sub_row(cols[k], j + 1)
                 cols[k] = jnp.where(pair, 0.0, cols[k]) - (one * x + two * y)
-            yield
-            across = [
-                jnp.where(pair, 0.0, c) - (one * sub_row(c, j) + two * sub_row(c, j + 1)) for c in across
-            ]
-            yield
+            if carry:
+                yield
+                across = [
+                    jnp.where(pair, 0.0, c) - (one * sub_row(c, j) + two * sub_row(c, j + 1)) for c in across
+                ]
+                yield
             full = jnp.where(pair, 0.0, full) - (one * sub_row(full, j) + two * sub_row(full, j + 1))
             inner = b * reciprocal(a)
             below = subs > j + 1
@@ -91,14 +92,15 @@
             yield
         out.append(jnp.where(lanes < base + ROWS, forward * lax.rsqrt(pivots), 0.0))
         if s < count - 1:
-            cols = [
-                own - sum_tree([next_coeffs[k] * sub_row(c, k) for k in range(ROWS)])
-                for own, c in zip(next_cols, across)
-            ]
+            if carry:
+                cols = [
+                    own - sum_tree([next_coeffs[k] * sub_row(c, k) for k in range(ROWS)])
+                    for own, c in zip(next_cols, across)
+                ]
             yield
             spread = [sub_row(full, k) for k in range(ROWS)]
             for i in range(s + 1, count):
-                coeffs = next_coeffs if i == s + 1 else [lane_col(rows[i], base + k) for k in range(ROWS)]
+                coeffs = next_coeffs if carry and i == s + 1 else [lane_col(rows[i], base + k) for k in range(ROWS)]
                 rows[i] = jnp.where(here, 0.0, rows[i]) - sum_tree([coeffs[k] * spread[k] for k in range(ROWS)])
                 yield
     return out
@@ -108,7 +110,7 @@
     results = [None] * len(generators)
     live = list(enumerate(generators))
     fills = list(fills)
-    total, turn, done = 350, 0, 0
+    total, turn, done = 250, 0, 0
     while live:
         for at, generator in list(live):
             try:
@@ -209,7 +211,7 @@
         def step(j, carry):
             rows = [chain.look(j) for chain in members]
             fills = [fill for several in zip_longest(*[chain.fills() for chain in members]) for fill in several if fill]
-            for chain, out in zip(members, in_turns([inverse_factor(r) for r in rows], fills)):
+            for chain, out in zip(members, in_turns([inverse_factor(r, len(members) == 1) for r in rows], fills)):
                 chain.store(out)
             return carry
 

time: 118 us -> 115 us (0.975)
  Pallas kernels: 72.3 us -> 69.1 us
    pallas_call x1, Pallas kernels: 47.1 us -> 43.9 us  [rest(): pl.pallas_call(functools.partial(rest_kernel, *[[d for d, _ in group] for...]
where the time goes in v7:
time: 115 us
  Pallas kernels  69.1 us (60%)
  starting transfers between devices  24.8 us (22%)
  waiting for transfers between devices  16 us (14%)
  other arithmetic  2.52 us (2%)
  local copies, waits for them, and re-layouts  1.48 us (1%)
    pallas_call x1, Pallas kernels, rest(): pl.pallas_call(functools.partial(rest_kernel, *[[d for d, _ in group] for...  43.9 us
    ppermute x17, starting transfers between devices, swap(): return lax.ppermute(x, axis, [(i, i ^ distance) for i in range(count)])  24.8 us
    pallas_call x1, Pallas kernels, head(): pl.pallas_call(functools.partial(head_kernel, count, *[[d for d, _ in gro...  20.9 us
    ppermute x17, waiting for transfers between devices, swap(): return lax.ppermute(x, axis, [(i, i ^ distance) for i in range(count)])  16 us
    pallas_call x1, Pallas kernels, first_sends(): pl.pallas_call(functools.partial(first_kernel, count, scale_left, scale_r...  4.33 us
    convert_element_type x5, other arithmetic, add(): return (x.astype(jnp.float32) + y.astype(jnp.float32)).astype(x.dtype)  2.36 us
  transfers between devices with their start and end apart: 17, of which 6 were waited for; matrix products, arithmetic and copies ran while one was open for 2% of the time, Pallas kernels for 18%

profile of v7, /device:TPU:0, one launch (start us, length us, event | category | flops | bytes accessed | tf_op | source)
XLA Modules:
  0.0 115.1 jit_solution(1665439562480151482)
XLA Ops:
  0.6 4.3 %shard_map.135 = (f32[224,896]{1,0:T(8,128)}, f32[64,1024]{1,0:T(8,128)}, bf16[448,512]{1,0:T(8,128)(2,1)}, bf16[448,512]{1,0:T(8,128)(2,1)}, bf16[256,384]{1,0:T(8,128)(2,1)}, /*index=5*/bf16[256,384]{1,0:T(8,128)(2,1)}) custom-call(bf16[512,896]{1,0:T(8,128)(2,1)} %refs_3_.1, f32[224,896]{1,0:T(8,128)} %bitcast.13, f32[224,896]{1,0:T(8,128)} %bitcast.8, ...), custom_call_target="tpu_custom_call" | custom-call | tf_op jit(solution)/shard_map/pallas_call | solution.py:294
  5.0 0.0 copy-start.3
  5.0 3.0 %collective-permute-start.10 = (bf16[256,384]{1,0:T(8,128)(2,1)}, bf16[256,384]{1,0:T(8,128)(2,1)S(1)}, u32[]{:S(2)}, u32[]{:S(2)}) collective-permute-start(bf16[256,384]{1,0:T(8,128)(2,1)} %get-tuple-element.39), channel_id=1, source_target_pairs={{0,1},{1,0},{2,3},{3,2},{4,5},{5,4},{6,7},{7,6},{8,9},{9,8},{10,11... | collective-permute-start | bytes 589832 | tf_op jit(solution)/shard_map/ppermute | solution.py:581
  8.0 0.0 collective-permute-start.4
  8.0 2.6 %collective-permute-start.9 = (f32[64,1024]{1,0:T(8,128)}, f32[64,1024]{1,0:T(8,128)S(1)}, u32[]{:S(2)}, u32[]{:S(2)}) collective-permute-start(f32[64,1024]{1,0:T(8,128)} %get-tuple-element.37.refs_11_), channel_id=1, source_target_pairs={{0,4},{1,5},{2,6},{3,7},{4,0},{5,1},{6,2},{7,3},{8,12},{9,13},{10,... | collective-permute-start | bytes 786440 | tf_op jit(solution)/shard_map/ppermute | solution.py:581
  10.6 1.5 %collective-permute-start = (f32[224,896]{1,0:T(8,128)}, f32[224,896]{1,0:T(8,128)S(1)}, u32[]{:S(2)}, u32[]{:S(2)}) collective-permute-start(f32[224,896]{1,0:T(8,128)} %get-tuple-element.28), channel_id=1, source_target_pairs={{0,16},{8,24},{16,0},{24,8},{1,17},{9,25},{17,1},{25,9},{2,18},{10... | collective-permute-start | bytes 2408456 | tf_op jit(solution)/shard_map/ppermute | solution.py:581
  12.1 1.0 collective-permute-done.10
  13.1 1.1 add_convert_fusion.2
  14.2 1.9 %collective-permute-start.11 = (bf16[128,384]{1,0:T(8,128)(2,1)S(1)}, bf16[128,384]{1,0:T(8,128)(2,1)S(1)}, u32[]{:S(2)}, u32[]{:S(2)}) collective-permute-start(bf16[128,384]{1,0:T(8,128)(2,1)S(1)} %constant_dynamic-slice_fusion), channel_id=1, source_target_pairs={{0,2},{1,3},{2,0},{3,1},{4,6},{5,7},{6,4},{7,5},{8,10},{9,11},{10,... | collective-permute-start | bytes 294920 | tf_op jit(solution)/shard_map/ppermute | solution.py:581
  16.1 0.0 collective-permute-done.4
  16.1 1.1 add_convert_fusion.1
  17.2 1.6 %collective-permute-start.5 = (bf16[448,512]{1,0:T(8,128)(2,1)S(1)}, bf16[448,512]{1,0:T(8,128)(2,1)S(1)}, u32[]{:S(2)}, u32[]{:S(2)}) collective-permute-start(bf16[448,512]{1,0:T(8,128)(2,1)S(1)} %add_convert_fusion.1), channel_id=1, source_target_pairs={{0,16},{8,24},{16,0},{24,8},{1,17},{9,25},{17,1},{25,9},{2,18},{10... | collective-permute-start | bytes 1376264 | tf_op jit(solution)/shard_map/ppermute | solution.py:581
  18.8 0.4 collective-permute-done.11
  19.2 5.1 %collective-permute-start.13 = (bf16[128,384]{1,0:T(8,128)(2,1)S(1)}, bf16[128,384]{1,0:T(8,128)(2,1)S(1)}, u32[]{:S(2)}, u32[]{:S(2)}) collective-permute-start(bf16[128,384]{1,0:T(8,128)(2,1)S(1)} %add_convert_fusion.4), channel_id=1, source_target_pairs={{0,4},{1,5},{2,6},{3,7},{4,0},{5,1},{6,2},{7,3},{8,12},{9,13},{10,... | collective-permute-start | bytes 294920 | tf_op jit(solution)/shard_map/ppermute | solution.py:581
  24.4 0.0 collective-permute-done.9.refs_12_
  24.4 0.0 copy-done.3
  24.4 0.0 copy-start
  24.4 2.5 %collective-permute-start.12 = (f32[128,1024]{1,0:T(8,128)S(1)}, f32[128,1024]{1,0:T(8,128)S(1)}, u32[]{:S(2)}, u32[]{:S(2)}) collective-permute-start(f32[128,1024]{1,0:T(8,128)S(1)} %pad_maximum_fusion.1), channel_id=1, source_target_pairs={{0,2},{1,3},{2,0},{3,1},{4,6},{5,7},{6,4},{7,5},{8,10},{9,11},{10,... | collective-permute-start | bytes 1572872 | tf_op jit(solution)/shard_map/ppermute | solution.py:581
  27.0 0.4 collective-permute-done.13
  27.4 0.0 copy-start.8
  27.4 2.2 %collective-permute-start.14 = (bf16[128,384]{1,0:T(8,128)(2,1)S(1)}, bf16[128,384]{1,0:T(8,128)(2,1)S(1)}, u32[]{:S(2)}, u32[]{:S(2)}) collective-permute-start(bf16[128,384]{1,0:T(8,128)(2,1)S(1)} %add_convert_fusion.3.refs_15_), channel_id=1, source_target_pairs={{0,2},{1,3},{2,0},{3,1},{4,6},{5,7},{6,4},{7,5},{8,10},{9,11},{10,... | collective-permute-start | bytes 294920 | tf_op jit(solution)/shard_map/ppermute | solution.py:581
  29.6 2.0 %collective-permute-done.refs_4_ = f32[224,896]{1,0:T(8,128)S(1)} collective-permute-done((f32[224,896]{1,0:T(8,128)}, f32[224,896]{1,0:T(8,128)S(1)}, u32[]{:S(2)}, u32[]{:S(2)}) %collective-permute-start) | collective-permute-done | bytes 802848 | tf_op jit(solution)/shard_map/ppermute | solution.py:581
  31.5 0.0 copy-done.1
  31.5 0.0 collective-permute-start.1
  31.6 9.1 %collective-permute-done.5 = bf16[448,512]{1,0:T(8,128)(2,1)S(1)} collective-permute-done((bf16[448,512]{1,0:T(8,128)(2,1)S(1)}, bf16[448,512]{1,0:T(8,128)(2,1)S(1)}, u32[]{:S(2)}, u32[]{:S(2)}) %collective-permute-start.5) | collective-permute-done | bytes 458784 | tf_op jit(solution)/shard_map/ppermute | solution.py:581
  40.7 0.1 add_convert_fusion.refs_6_
  40.8 0.0 copy-start.6
  40.8 0.0 collective-permute-done.14.refs_16_
  40.8 0.0 copy-start.13
  40.8 0.0 collective-permute-done.12.refs_13_
  40.8 0.0 copy-start.5
  40.8 0.1 pad_maximum_fusion
  41.0 0.0 copy-done.4
  41.0 1.4 %collective-permute-start.15 = (f32[256,1024]{1,0:T(8,128)S(1)}, f32[256,1024]{1,0:T(8,128)S(1)}, u32[]{:S(2)}, u32[]{:S(2)}) collective-permute-start(f32[256,1024]{1,0:T(8,128)S(1)} %pad_maximum_fusion), channel_id=1, source_target_pairs={{0,1},{1,0},{2,3},{3,2},{4,5},{5,4},{6,7},{7,6},{8,9},{9,8},{10,11... | collective-permute-start | bytes 3145736 | tf_op jit(solution)/shard_map/ppermute | solution.py:581
  42.4 0.0 copy-done
  42.4 0.0 collective-permute-start.2
  42.4 0.5 collective-permute-start.6
  42.9 0.0 collective-permute-start.3
  43.0 0.0 copy-done.9
  43.0 3.0 %collective-permute-done.6.refs_7_ = bf16[448,512]{1,0:T(8,128)(2,1)S(1)} collective-permute-done((bf16[448,512]{1,0:T(8,128)(2,1)S(1)}, bf16[448,512]{1,0:T(8,128)(2,1)S(1)}, u32[]{:S(2)}, u32[]{:S(2)}) %collective-permute-start.6) | collective-permute-done | bytes 458784 | tf_op jit(solution)/shard_map/ppermute | solution.py:581
  46.0 1.2 %collective-permute-start.8 = (f32[224,512]{1,0:T(8,128)S(1)}, f32[224,512]{1,0:T(8,128)}, u32[]{:S(2)}, u32[]{:S(2)}) collective-permute-start(f32[224,512]{1,0:T(8,128)S(1)} %slice.3), channel_id=1, source_target_pairs={{0,24},{8,16},{16,8},{24,0},{1,25},{9,17},{17,9},{25,1},{2,26},{10... | collective-permute-start | bytes 1376264 | tf_op jit(solution)/shard_map/ppermute | solution.py:581
  47.2 0.0 collective-permute-done.1.refs_1_
  47.2 0.6 collective-permute-start.7
  47.8 0.0 copy-done.8
  47.8 0.0 collective-permute-done.2.refs_3_.refs_8_
  47.8 0.0 copy-done.12
  47.9 0.0 copy-start.2
  47.9 0.7 collective-permute-start.16
  48.6 0.0 collective-permute-done.3.refs_5_
  48.6 0.0 copy-done.6
  48.6 0.0 copy-done.10
  48.6 0.1 copy-done.2
  48.8 20.9 %shard_map.136 = (f32[224,896]{1,0:T(8,128)}, bf16[896,896]{1,0:T(8,128)(2,1)}, bf16[896,896]{1,0:T(8,128)(2,1)}, f32[896,384]{1,0:T(8,128)}) custom-call(f32[224,896]{1,0:T(8,128)} %bitcast.14, f32[224,896]{1,0:T(8,128)} %copy-done.10, f32[224,896]{1,0:T(8,128)} %bitcast.9, f32[224,896]{1,0:T(8,128)} %copy-done.2, f32[224,896]{1,0:T(8,128)} %copy-done.9, ...), custom_call_target="tpu_custom_call" | custom-call | tf_op jit(solution)/shard_map/pallas_call | solution.py:419
  69.7 0.0 copy-done.13
  69.7 0.0 collective-permute-done.16.refs_17_
  69.7 0.0 copy-start.14
  69.7 0.0 collective-permute-done.8.refs_10_
  69.7 0.0 collective-permute-done.7.refs_9_
  69.8 0.0 collective-permute-done.15.refs_14_
  69.8 0.0 copy-start.7
  69.8 0.6 copy-done.14
  70.4 0.2 copy-done.11
  70.6 0.4 copy-done.7
  71.0 43.9 %shard_map.137 = (f32[512,896]{1,0:T(8,128)}, f32[512,896]{1,0:T(8,128)}, f32[512,896]{1,0:T(8,128)}, f32[224,896]{1,0:T(8,128)}, f32[64,512]{1,0:T(8,128)}, /*index=5*/f32[64,512]{1,0:T(8,128)}) custom-call(bf16[896,896]{1,0:T(8,128)(2,1)} %get-tuple-element.33.refs_0_, bf16[896,896]{1,0:T(8,128)(2,1)} %get-tuple-element.34.refs_1_, ...), custom_call_target="tpu_custom_call" | custom-call | tf_op jit(solution)/shard_map/pallas_call | solution.py:538
  (13 shorter events, 0.2 us)
Async XLA Ops:
  5.0 19.4 %copy-start.3 = (f32[64,1024]{1,0:T(8,128)S(1)}, f32[64,1024]{1,0:T(8,128)}, u32[]{:S(2)}) copy-start(f32[64,1024]{1,0:T(8,128)} %get-tuple-element.37.refs_11_) | copy-start | bytes 786436
  5.0 8.1 %collective-permute-start.10 = (bf16[256,384]{1,0:T(8,128)(2,1)}, bf16[256,384]{1,0:T(8,128)(2,1)S(1)}, u32[]{:S(2)}, u32[]{:S(2)}) collective-permute-start(bf16[256,384]{1,0:T(8,128)(2,1)} %get-tuple-element.39), channel_id=1, source_target_pairs={{0,1},{1,0},{2,3},{3,2},{4,5},{5,4},{6,7},{7,6},{8,9},{9,8},{10,11... | collective-permute-start | bytes 589832 | tf_op jit(solution)/shard_map/ppermute | solution.py:581
  8.0 8.1 %collective-permute-start.4 = (bf16[448,512]{1,0:T(8,128)(2,1)}, bf16[448,512]{1,0:T(8,128)(2,1)S(1)}, u32[]{:S(2)}, u32[]{:S(2)}) collective-permute-start(bf16[448,512]{1,0:T(8,128)(2,1)} %get-tuple-element.32), channel_id=1, source_target_pairs={{0,8},{8,0},{16,24},{24,16},{1,9},{9,1},{17,25},{25,17},{2,10},{10... | collective-permute-start | bytes 1376264 | tf_op jit(solution)/shard_map/ppermute | solution.py:581
  8.0 16.3 %collective-permute-start.9 = (f32[64,1024]{1,0:T(8,128)}, f32[64,1024]{1,0:T(8,128)S(1)}, u32[]{:S(2)}, u32[]{:S(2)}) collective-permute-start(f32[64,1024]{1,0:T(8,128)} %get-tuple-element.37.refs_11_), channel_id=1, source_target_pairs={{0,4},{1,5},{2,6},{3,7},{4,0},{5,1},{6,2},{7,3},{8,12},{9,13},{10,... | collective-permute-start | bytes 786440 | tf_op jit(solution)/shard_map/ppermute | solution.py:581
  10.6 20.9 %collective-permute-start = (f32[224,896]{1,0:T(8,128)}, f32[224,896]{1,0:T(8,128)S(1)}, u32[]{:S(2)}, u32[]{:S(2)}) collective-permute-start(f32[224,896]{1,0:T(8,128)} %get-tuple-element.28), channel_id=1, source_target_pairs={{0,16},{8,24},{16,0},{24,8},{1,17},{9,25},{17,1},{25,9},{2,18},{10... | collective-permute-start | bytes 2408456 | tf_op jit(solution)/shard_map/ppermute | solution.py:581
  13.1 18.4 %copy-start.1 = (f32[1,224,896]{2,1,0:T(8,128)S(1)}, f32[1,224,896]{2,1,0:T(8,128)}, u32[]{:S(2)}) copy-start(f32[1,224,896]{2,1,0:T(8,128)} %param.14) | copy-start | bytes 2408452
  14.2 5.0 %collective-permute-start.11 = (bf16[128,384]{1,0:T(8,128)(2,1)S(1)}, bf16[128,384]{1,0:T(8,128)(2,1)S(1)}, u32[]{:S(2)}, u32[]{:S(2)}) collective-permute-start(bf16[128,384]{1,0:T(8,128)(2,1)S(1)} %constant_dynamic-slice_fusion), channel_id=1, source_target_pairs={{0,2},{1,3},{2,0},{3,1},{4,6},{5,7},{6,4},{7,5},{8,10},{9,11},{10,... | collective-permute-start | bytes 294920 | tf_op jit(solution)/shard_map/ppermute | solution.py:581
  17.2 23.5 %collective-permute-start.5 = (bf16[448,512]{1,0:T(8,128)(2,1)S(1)}, bf16[448,512]{1,0:T(8,128)(2,1)S(1)}, u32[]{:S(2)}, u32[]{:S(2)}) collective-permute-start(bf16[448,512]{1,0:T(8,128)(2,1)S(1)} %add_convert_fusion.1), channel_id=1, source_target_pairs={{0,16},{8,24},{16,0},{24,8},{1,17},{9,25},{17,1},{25,9},{2,18},{10... | collective-permute-start | bytes 1376264 | tf_op jit(solution)/shard_map/ppermute | solution.py:581
  19.2 8.1 %collective-permute-start.13 = (bf16[128,384]{1,0:T(8,128)(2,1)S(1)}, bf16[128,384]{1,0:T(8,128)(2,1)S(1)}, u32[]{:S(2)}, u32[]{:S(2)}) collective-permute-start(bf16[128,384]{1,0:T(8,128)(2,1)S(1)} %add_convert_fusion.4), channel_id=1, source_target_pairs={{0,4},{1,5},{2,6},{3,7},{4,0},{5,1},{6,2},{7,3},{8,12},{9,13},{10,... | collective-permute-start | bytes 294920 | tf_op jit(solution)/shard_map/ppermute | solution.py:581
  24.4 16.6 %copy-start.4 = (f32[64,1024]{1,0:T(8,128)}, f32[64,1024]{1,0:T(8,128)S(1)}, u32[]{:S(2)}) copy-start(f32[64,1024]{1,0:T(8,128)S(1)} %collective-permute-done.9.refs_12_) | copy-start | bytes 786436
  24.4 18.0 %copy-start = (f32[1,224,896]{2,1,0:T(8,128)S(1)}, f32[1,224,896]{2,1,0:T(8,128)}, u32[]{:S(2)}) copy-start(f32[1,224,896]{2,1,0:T(8,128)} %param.15) | copy-start | bytes 2408452
  24.4 16.4 %collective-permute-start.12 = (f32[128,1024]{1,0:T(8,128)S(1)}, f32[128,1024]{1,0:T(8,128)S(1)}, u32[]{:S(2)}, u32[]{:S(2)}) collective-permute-start(f32[128,1024]{1,0:T(8,128)S(1)} %pad_maximum_fusion.1), channel_id=1, source_target_pairs={{0,2},{1,3},{2,0},{3,1},{4,6},{5,7},{6,4},{7,5},{8,10},{9,11},{10,... | collective-permute-start | bytes 1572872 | tf_op jit(solution)/shard_map/ppermute | solution.py:581
  27.4 20.4 %copy-start.8 = (bf16[128,384]{1,0:T(8,128)(2,1)}, bf16[128,384]{1,0:T(8,128)(2,1)S(1)}, u32[]{:S(2)}) copy-start(bf16[128,384]{1,0:T(8,128)(2,1)S(1)} %add_convert_fusion.3.refs_15_) | copy-start | bytes 294916
  27.4 13.4 %collective-permute-start.14 = (bf16[128,384]{1,0:T(8,128)(2,1)S(1)}, bf16[128,384]{1,0:T(8,128)(2,1)S(1)}, u32[]{:S(2)}, u32[]{:S(2)}) collective-permute-start(bf16[128,384]{1,0:T(8,128)(2,1)S(1)} %add_convert_fusion.3.refs_15_), channel_id=1, source_target_pairs={{0,2},{1,3},{2,0},{3,1},{4,6},{5,7},{6,4},{7,5},{8,10},{9,11},{10,... | collective-permute-start | bytes 294920 | tf_op jit(solution)/shard_map/ppermute | solution.py:581
  31.5 11.4 %copy-start.9 = (f32[224,896]{1,0:T(8,128)}, f32[224,896]{1,0:T(8,128)S(1)}, u32[]{:S(2)}) copy-start(f32[224,896]{1,0:T(8,128)S(1)} %collective-permute-done.refs_4_) | copy-start | bytes 2408452
  31.5 15.7 %collective-permute-start.1 = (f32[224,896]{1,0:T(8,128)S(1)}, f32[224,896]{1,0:T(8,128)S(1)}, u32[]{:S(2)}, u32[]{:S(2)}) collective-permute-start(f32[224,896]{1,0:T(8,128)S(1)} %bitcast.15), channel_id=1, source_target_pairs={{0,8},{8,0},{16,24},{24,16},{1,9},{9,1},{17,25},{25,17},{2,10},{10... | collective-permute-start | bytes 2408456 | tf_op jit(solution)/shard_map/ppermute | solution.py:581
  40.8 7.8 %copy-start.6 = (bf16[448,512]{1,0:T(8,128)(2,1)}, bf16[448,512]{1,0:T(8,128)(2,1)S(1)}, u32[]{:S(2)}) copy-start(bf16[448,512]{1,0:T(8,128)(2,1)S(1)} %add_convert_fusion.refs_6_) | copy-start | bytes 1376260
  40.8 28.9 %copy-start.13 = (bf16[128,384]{1,0:T(8,128)(2,1)}, bf16[128,384]{1,0:T(8,128)(2,1)S(1)}, u32[]{:S(2)}) copy-start(bf16[128,384]{1,0:T(8,128)(2,1)S(1)} %collective-permute-done.14.refs_16_) | copy-start | bytes 294916
  40.8 28.9 %copy-start.5 = (f32[128,1024]{1,0:T(8,128)}, f32[128,1024]{1,0:T(8,128)S(1)}, u32[]{:S(2)}) copy-start(f32[128,1024]{1,0:T(8,128)S(1)} %collective-permute-done.12.refs_13_) | copy-start | bytes 1572868
  41.0 28.8 %collective-permute-start.15 = (f32[256,1024]{1,0:T(8,128)S(1)}, f32[256,1024]{1,0:T(8,128)S(1)}, u32[]{:S(2)}, u32[]{:S(2)}) collective-permute-start(f32[256,1024]{1,0:T(8,128)S(1)} %pad_maximum_fusion), channel_id=1, source_target_pairs={{0,1},{1,0},{2,3},{3,2},{4,5},{5,4},{6,7},{7,6},{8,9},{9,8},{10,11... | collective-permute-start | bytes 3145736 | tf_op jit(solution)/shard_map/ppermute | solution.py:581
  42.4 5.4 %collective-permute-start.2 = (f32[224,896]{1,0:T(8,128)S(1)}, f32[224,896]{1,0:T(8,128)S(1)}, u32[]{:S(2)}, u32[]{:S(2)}) collective-permute-start(f32[224,896]{1,0:T(8,128)S(1)} %bitcast.11), channel_id=1, source_target_pairs={{0,8},{8,0},{16,24},{24,16},{1,9},{9,1},{17,25},{25,17},{2,10},{10... | collective-permute-start | bytes 2408456 | tf_op jit(solution)/shard_map/ppermute | solution.py:581
  42.4 3.6 %collective-permute-start.6 = (bf16[448,512]{1,0:T(8,128)(2,1)S(1)}, bf16[448,512]{1,0:T(8,128)(2,1)S(1)}, u32[]{:S(2)}, u32[]{:S(2)}) collective-permute-start(bf16[448,512]{1,0:T(8,128)(2,1)S(1)} %add_convert_fusion.refs_6_), channel_id=1, source_target_pairs={{0,8},{8,0},{16,24},{24,16},{1,9},{9,1},{17,25},{25,17},{2,10},{10... | collective-permute-start | bytes 1376264 | tf_op jit(solution)/shard_map/ppermute | solution.py:581
  42.9 5.7 %collective-permute-start.3 = (f32[224,896]{1,0:T(8,128)S(1)}, f32[224,896]{1,0:T(8,128)}, u32[]{:S(2)}, u32[]{:S(2)}) collective-permute-start(f32[224,896]{1,0:T(8,128)S(1)} %collective-permute-done.refs_4_), channel_id=1, source_target_pairs={{0,8},{8,0},{16,24},{24,16},{1,9},{9,1},{17,25},{25,17},{2,10},{10... | collective-permute-start | bytes 2408456 | tf_op jit(solution)/shard_map/ppermute | solution.py:581
  46.0 1.8 %copy-start.12 = (bf16[448,512]{1,0:T(8,128)(2,1)}, bf16[448,512]{1,0:T(8,128)(2,1)S(1)}, u32[]{:S(2)}) copy-start(bf16[448,512]{1,0:T(8,128)(2,1)S(1)} %collective-permute-done.6.refs_7_) | copy-start | bytes 1376260
  46.0 23.7 %collective-permute-start.8 = (f32[224,512]{1,0:T(8,128)S(1)}, f32[224,512]{1,0:T(8,128)}, u32[]{:S(2)}, u32[]{:S(2)}) collective-permute-start(f32[224,512]{1,0:T(8,128)S(1)} %slice.3), channel_id=1, source_target_pairs={{0,24},{8,16},{16,8},{24,0},{1,25},{9,17},{17,9},{25,1},{2,26},{10... | collective-permute-start | bytes 1376264 | tf_op jit(solution)/shard_map/ppermute | solution.py:581
  47.2 1.4 %copy-start.10 = (f32[224,896]{1,0:T(8,128)}, f32[224,896]{1,0:T(8,128)S(1)}, u32[]{:S(2)}) copy-start(f32[224,896]{1,0:T(8,128)S(1)} %collective-permute-done.1.refs_1_) | copy-start | bytes 2408452
  47.2 22.5 %collective-permute-start.7 = (f32[224,512]{1,0:T(8,128)S(1)}, f32[224,512]{1,0:T(8,128)S(1)}, u32[]{:S(2)}, u32[]{:S(2)}) collective-permute-start(f32[224,512]{1,0:T(8,128)S(1)} %slice.3), channel_id=1, source_target_pairs={{0,16},{8,24},{16,0},{24,8},{1,17},{9,25},{17,1},{25,9},{2,18},{10... | collective-permute-start | bytes 1376264 | tf_op jit(solution)/shard_map/ppermute | solution.py:581
  47.9 0.9 copy-start.2
  47.9 21.9 %collective-permute-start.16 = (bf16[256,384]{1,0:T(8,128)(2,1)S(1)}, bf16[256,384]{1,0:T(8,128)(2,1)S(1)}, u32[]{:S(2)}, u32[]{:S(2)}) collective-permute-start(bf16[256,384]{1,0:T(8,128)(2,1)S(1)} %pad_maximum_fusion.2), channel_id=1, source_target_pairs={{0,1},{1,0},{2,3},{3,2},{4,5},{5,4},{6,7},{7,6},{8,9},{9,8},{10,11... | collective-permute-start | bytes 589832 | tf_op jit(solution)/shard_map/ppermute | solution.py:581
  69.7 0.7 copy-start.14
  69.8 0.9 copy-start.11
  69.8 1.2 %copy-start.7 = (f32[256,1024]{1,0:T(8,128)}, f32[256,1024]{1,0:T(8,128)S(1)}, u32[]{:S(2)}) copy-start(f32[256,1024]{1,0:T(8,128)S(1)} %collective-permute-done.15.refs_14_) | copy-start | bytes 3145732

commit v8 on v7

--- a/solution.py
+++ b/solution.py
@@ -61,14 +61,16 @@
         for j in range(0, ROWS, 2):
             a, b, d = sub_row(cols[j], j), sub_row(cols[j], j + 1), sub_row(cols[j + 1], j + 1)
             det = a * d - b * b
-            inv = reciprocal(det)
+            guess = pl.reciprocal(det, approx=True)
+            refine = 2.0 - det * guess
+            inv = guess * refine
             pair = (subs == j) | (subs == j + 1)
             one = jnp.where(pair, jnp.where(subs == j, -1.0, 0.0), cols[j])
             two = jnp.where(pair, jnp.where(subs == j, 0.0, -1.0), cols[j + 1])
             for k in range(j + 2, min(j + 4, ROWS)):
                 x, y = sub_row(cols[k], j), sub_row(cols[k], j + 1)
                 change = one * (d * x - b * y) + two * (a * y - b * x)
-                cols[k] = jnp.where(pair, 0.0, cols[k]) - change * inv
+                cols[k] = jnp.where(pair, 0.0, cols[k]) - (change * guess) * refine
             yield
             one, two = (one * d - two * b) * inv, (two * a - one * b) * inv
             for k in range(j + 4, ROWS):

time: 115 us -> 115 us (level)
  transfers between devices with their start and end apart: 17 -> 17, of which waited for: 6 -> 7; matrix products, arithmetic and copies ran while one was open for 2% -> 2% of each run, Pallas kernels for 18% -> 18%
where the time goes in v8:
time: 115 us
  Pallas kernels  69 us (60%)
  starting transfers between devices  24.8 us (22%)
  waiting for transfers between devices  16.1 us (14%)
  other arithmetic  2.52 us (2%)
  local copies, waits for them, and re-layouts  1.49 us (1%)
    pallas_call x1, Pallas kernels, rest(): pl.pallas_call(functools.partial(rest_kernel, *[[d for d, _ in group] for...  43.8 us
    ppermute x17, starting transfers between devices, swap(): return lax.ppermute(x, axis, [(i, i ^ distance) for i in range(count)])  24.8 us
    pallas_call x1, Pallas kernels, head(): pl.pallas_call(functools.partial(head_kernel, count, *[[d for d, _ in gro...  20.9 us
    ppermute x17, waiting for transfers between devices, swap(): return lax.ppermute(x, axis, [(i, i ^ distance) for i in range(count)])  16.1 us
    pallas_call x1, Pallas kernels, first_sends(): pl.pallas_call(functools.partial(first_kernel, count, scale_left, scale_r...  4.33 us
    convert_element_type x5, other arithmetic, add(): return (x.astype(jnp.float32) + y.astype(jnp.float32)).astype(x.dtype)  2.36 us
  transfers between devices with their start and end apart: 17, of which 7 were waited for; matrix products, arithmetic and copies ran while one was open for 2% of the time, Pallas kernels for 18%

profile of v8, /device:TPU:0, one launch (start us, length us, event | category | flops | bytes accessed | tf_op | source)
XLA Modules:
  0.0 115.0 jit_solution(1198308603571536723)
XLA Ops:
  0.6 4.3 %shard_map.135 = (f32[224,896]{1,0:T(8,128)}, f32[64,1024]{1,0:T(8,128)}, bf16[448,512]{1,0:T(8,128)(2,1)}, bf16[448,512]{1,0:T(8,128)(2,1)}, bf16[256,384]{1,0:T(8,128)(2,1)}, /*index=5*/bf16[256,384]{1,0:T(8,128)(2,1)}) custom-call(bf16[512,896]{1,0:T(8,128)(2,1)} %refs_3_.1, f32[224,896]{1,0:T(8,128)} %bitcast.13, f32[224,896]{1,0:T(8,128)} %bitcast.8, ...), custom_call_target="tpu_custom_call" | custom-call | tf_op jit(solution)/shard_map/pallas_call | solution.py:296
  5.0 0.0 copy-start.3
  5.0 3.0 %collective-permute-start.10 = (bf16[256,384]{1,0:T(8,128)(2,1)}, bf16[256,384]{1,0:T(8,128)(2,1)S(1)}, u32[]{:S(2)}, u32[]{:S(2)}) collective-permute-start(bf16[256,384]{1,0:T(8,128)(2,1)} %get-tuple-element.39), channel_id=1, source_target_pairs={{0,1},{1,0},{2,3},{3,2},{4,5},{5,4},{6,7},{7,6},{8,9},{9,8},{10,11... | collective-permute-start | bytes 589832 | tf_op jit(solution)/shard_map/ppermute | solution.py:583
  8.0 0.0 collective-permute-start.4
  8.0 2.6 %collective-permute-start.9 = (f32[64,1024]{1,0:T(8,128)}, f32[64,1024]{1,0:T(8,128)S(1)}, u32[]{:S(2)}, u32[]{:S(2)}) collective-permute-start(f32[64,1024]{1,0:T(8,128)} %get-tuple-element.37.refs_11_), channel_id=1, source_target_pairs={{0,4},{1,5},{2,6},{3,7},{4,0},{5,1},{6,2},{7,3},{8,12},{9,13},{10,... | collective-permute-start | bytes 786440 | tf_op jit(solution)/shard_map/ppermute | solution.py:583
  10.6 1.5 %collective-permute-start = (f32[224,896]{1,0:T(8,128)}, f32[224,896]{1,0:T(8,128)S(1)}, u32[]{:S(2)}, u32[]{:S(2)}) collective-permute-start(f32[224,896]{1,0:T(8,128)} %get-tuple-element.28), channel_id=1, source_target_pairs={{0,16},{8,24},{16,0},{24,8},{1,17},{9,25},{17,1},{25,9},{2,18},{10... | collective-permute-start | bytes 2408456 | tf_op jit(solution)/shard_map/ppermute | solution.py:583
  12.1 1.0 collective-permute-done.10
  13.1 1.1 add_convert_fusion.2
  14.2 1.9 %collective-permute-start.11 = (bf16[128,384]{1,0:T(8,128)(2,1)S(1)}, bf16[128,384]{1,0:T(8,128)(2,1)S(1)}, u32[]{:S(2)}, u32[]{:S(2)}) collective-permute-start(bf16[128,384]{1,0:T(8,128)(2,1)S(1)} %constant_dynamic-slice_fusion), channel_id=1, source_target_pairs={{0,2},{1,3},{2,0},{3,1},{4,6},{5,7},{6,4},{7,5},{8,10},{9,11},{10,... | collective-permute-start | bytes 294920 | tf_op jit(solution)/shard_map/ppermute | solution.py:583
  16.1 0.0 collective-permute-done.4
  16.1 1.1 add_convert_fusion.1
  17.2 1.6 %collective-permute-start.5 = (bf16[448,512]{1,0:T(8,128)(2,1)S(1)}, bf16[448,512]{1,0:T(8,128)(2,1)S(1)}, u32[]{:S(2)}, u32[]{:S(2)}) collective-permute-start(bf16[448,512]{1,0:T(8,128)(2,1)S(1)} %add_convert_fusion.1), channel_id=1, source_target_pairs={{0,16},{8,24},{16,0},{24,8},{1,17},{9,25},{17,1},{25,9},{2,18},{10... | collective-permute-start | bytes 1376264 | tf_op jit(solution)/shard_map/ppermute | solution.py:583
  18.8 0.4 collective-permute-done.11
  19.2 5.1 %collective-permute-start.13 = (bf16[128,384]{1,0:T(8,128)(2,1)S(1)}, bf16[128,384]{1,0:T(8,128)(2,1)S(1)}, u32[]{:S(2)}, u32[]{:S(2)}) collective-permute-start(bf16[128,384]{1,0:T(8,128)(2,1)S(1)} %add_convert_fusion.4), channel_id=1, source_target_pairs={{0,4},{1,5},{2,6},{3,7},{4,0},{5,1},{6,2},{7,3},{8,12},{9,13},{10,... | collective-permute-start | bytes 294920 | tf_op jit(solution)/shard_map/ppermute | solution.py:583
  24.4 0.0 collective-permute-done.9.refs_12_
  24.4 0.0 copy-done.3
  24.4 0.0 copy-start
  24.4 2.5 %collective-permute-start.12 = (f32[128,1024]{1,0:T(8,128)S(1)}, f32[128,1024]{1,0:T(8,128)S(1)}, u32[]{:S(2)}, u32[]{:S(2)}) collective-permute-start(f32[128,1024]{1,0:T(8,128)S(1)} %pad_maximum_fusion.1), channel_id=1, source_target_pairs={{0,2},{1,3},{2,0},{3,1},{4,6},{5,7},{6,4},{7,5},{8,10},{9,11},{10,... | collective-permute-start | bytes 1572872 | tf_op jit(solution)/shard_map/ppermute | solution.py:583
  27.0 0.4 collective-permute-done.13
  27.4 0.0 copy-start.8
  27.4 2.2 %collective-permute-start.14 = (bf16[128,384]{1,0:T(8,128)(2,1)S(1)}, bf16[128,384]{1,0:T(8,128)(2,1)S(1)}, u32[]{:S(2)}, u32[]{:S(2)}) collective-permute-start(bf16[128,384]{1,0:T(8,128)(2,1)S(1)} %add_convert_fusion.3.refs_15_), channel_id=1, source_target_pairs={{0,2},{1,3},{2,0},{3,1},{4,6},{5,7},{6,4},{7,5},{8,10},{9,11},{10,... | collective-permute-start | bytes 294920 | tf_op jit(solution)/shard_map/ppermute | solution.py:583
  29.6 2.0 %collective-permute-done.refs_4_ = f32[224,896]{1,0:T(8,128)S(1)} collective-permute-done((f32[224,896]{1,0:T(8,128)}, f32[224,896]{1,0:T(8,128)S(1)}, u32[]{:S(2)}, u32[]{:S(2)}) %collective-permute-start) | collective-permute-done | bytes 802848 | tf_op jit(solution)/shard_map/ppermute | solution.py:583
  31.5 0.0 copy-done.1
  31.5 0.0 collective-permute-start.1
  31.6 9.1 %collective-permute-done.5 = bf16[448,512]{1,0:T(8,128)(2,1)S(1)} collective-permute-done((bf16[448,512]{1,0:T(8,128)(2,1)S(1)}, bf16[448,512]{1,0:T(8,128)(2,1)S(1)}, u32[]{:S(2)}, u32[]{:S(2)}) %collective-permute-start.5) | collective-permute-done | bytes 458784 | tf_op jit(solution)/shard_map/ppermute | solution.py:583
  40.7 0.1 add_convert_fusion.refs_6_
  40.8 0.0 copy-start.6
  40.8 0.0 collective-permute-done.14.refs_16_
  40.8 0.0 copy-start.13
  40.8 0.0 collective-permute-done.12.refs_13_
  40.8 0.0 copy-start.5
  40.8 0.1 pad_maximum_fusion
  41.0 0.0 copy-done.4
  41.0 1.4 %collective-permute-start.15 = (f32[256,1024]{1,0:T(8,128)S(1)}, f32[256,1024]{1,0:T(8,128)S(1)}, u32[]{:S(2)}, u32[]{:S(2)}) collective-permute-start(f32[256,1024]{1,0:T(8,128)S(1)} %pad_maximum_fusion), channel_id=1, source_target_pairs={{0,1},{1,0},{2,3},{3,2},{4,5},{5,4},{6,7},{7,6},{8,9},{9,8},{10,11... | collective-permute-start | bytes 3145736 | tf_op jit(solution)/shard_map/ppermute | solution.py:583
  42.4 0.0 copy-done
  42.4 0.0 collective-permute-start.2
  42.4 0.5 collective-permute-start.6
  42.9 0.0 collective-permute-start.3
  43.0 0.0 copy-done.9
  43.0 3.0 %collective-permute-done.6.refs_7_ = bf16[448,512]{1,0:T(8,128)(2,1)S(1)} collective-permute-done((bf16[448,512]{1,0:T(8,128)(2,1)S(1)}, bf16[448,512]{1,0:T(8,128)(2,1)S(1)}, u32[]{:S(2)}, u32[]{:S(2)}) %collective-permute-start.6) | collective-permute-done | bytes 458784 | tf_op jit(solution)/shard_map/ppermute | solution.py:583
  46.0 1.2 %collective-permute-start.8 = (f32[224,512]{1,0:T(8,128)S(1)}, f32[224,512]{1,0:T(8,128)}, u32[]{:S(2)}, u32[]{:S(2)}) collective-permute-start(f32[224,512]{1,0:T(8,128)S(1)} %slice.3), channel_id=1, source_target_pairs={{0,24},{8,16},{16,8},{24,0},{1,25},{9,17},{17,9},{25,1},{2,26},{10... | collective-permute-start | bytes 1376264 | tf_op jit(solution)/shard_map/ppermute | solution.py:583
  47.2 0.0 collective-permute-done.1.refs_1_
  47.2 0.6 collective-permute-start.7
  47.8 0.0 copy-done.8
  47.8 0.0 collective-permute-done.2.refs_3_.refs_8_
  47.8 0.0 copy-done.12
  47.9 0.0 copy-start.2
  47.9 0.7 collective-permute-start.16
  48.6 0.0 collective-permute-done.3.refs_5_
  48.6 0.0 copy-done.6
  48.6 0.0 copy-done.10
  48.6 0.1 copy-done.2
  48.8 20.9 %shard_map.136 = (f32[224,896]{1,0:T(8,128)}, bf16[896,896]{1,0:T(8,128)(2,1)}, bf16[896,896]{1,0:T(8,128)(2,1)}, f32[896,384]{1,0:T(8,128)}) custom-call(f32[224,896]{1,0:T(8,128)} %bitcast.14, f32[224,896]{1,0:T(8,128)} %copy-done.10, f32[224,896]{1,0:T(8,128)} %bitcast.9, f32[224,896]{1,0:T(8,128)} %copy-done.2, f32[224,896]{1,0:T(8,128)} %copy-done.9, ...), custom_call_target="tpu_custom_call" | custom-call | tf_op jit(solution)/shard_map/pallas_call | solution.py:421
  69.6 0.0 copy-done.13
  69.6 0.0 copy-done.5
  69.7 0.1 collective-permute-done.16.refs_17_
  69.7 0.0 collective-permute-done.8.refs_10_
  69.7 0.0 collective-permute-done.7.refs_9_
  69.7 0.0 copy-start.11
  69.7 0.0 collective-permute-done.15.refs_14_
  69.8 0.6 copy-done.14
  70.4 0.2 copy-done.11
  70.6 0.4 copy-done.7
  71.0 43.8 %shard_map.137 = (f32[512,896]{1,0:T(8,128)}, f32[512,896]{1,0:T(8,128)}, f32[512,896]{1,0:T(8,128)}, f32[224,896]{1,0:T(8,128)}, f32[64,512]{1,0:T(8,128)}, /*index=5*/f32[64,512]{1,0:T(8,128)}) custom-call(bf16[896,896]{1,0:T(8,128)(2,1)} %get-tuple-element.33.refs_0_, bf16[896,896]{1,0:T(8,128)(2,1)} %get-tuple-element.34.refs_1_, ...), custom_call_target="tpu_custom_call" | custom-call | tf_op jit(solution)/shard_map/pallas_call | solution.py:540
  (13 shorter events, 0.2 us)
Async XLA Ops:
  5.0 19.4 %copy-start.3 = (f32[64,1024]{1,0:T(8,128)S(1)}, f32[64,1024]{1,0:T(8,128)}, u32[]{:S(2)}) copy-start(f32[64,1024]{1,0:T(8,128)} %get-tuple-element.37.refs_11_) | copy-start | bytes 786436
  5.0 8.1 %collective-permute-start.10 = (bf16[256,384]{1,0:T(8,128)(2,1)}, bf16[256,384]{1,0:T(8,128)(2,1)S(1)}, u32[]{:S(2)}, u32[]{:S(2)}) collective-permute-start(bf16[256,384]{1,0:T(8,128)(2,1)} %get-tuple-element.39), channel_id=1, source_target_pairs={{0,1},{1,0},{2,3},{3,2},{4,5},{5,4},{6,7},{7,6},{8,9},{9,8},{10,11... | collective-permute-start | bytes 589832 | tf_op jit(solution)/shard_map/ppermute | solution.py:583
  8.0 8.1 %collective-permute-start.4 = (bf16[448,512]{1,0:T(8,128)(2,1)}, bf16[448,512]{1,0:T(8,128)(2,1)S(1)}, u32[]{:S(2)}, u32[]{:S(2)}) collective-permute-start(bf16[448,512]{1,0:T(8,128)(2,1)} %get-tuple-element.32), channel_id=1, source_target_pairs={{0,8},{8,0},{16,24},{24,16},{1,9},{9,1},{17,25},{25,17},{2,10},{10... | collective-permute-start | bytes 1376264 | tf_op jit(solution)/shard_map/ppermute | solution.py:583
  8.0 16.3 %collective-permute-start.9 = (f32[64,1024]{1,0:T(8,128)}, f32[64,1024]{1,0:T(8,128)S(1)}, u32[]{:S(2)}, u32[]{:S(2)}) collective-permute-start(f32[64,1024]{1,0:T(8,128)} %get-tuple-element.37.refs_11_), channel_id=1, source_target_pairs={{0,4},{1,5},{2,6},{3,7},{4,0},{5,1},{6,2},{7,3},{8,12},{9,13},{10,... | collective-permute-start | bytes 786440 | tf_op jit(solution)/shard_map/ppermute | solution.py:583
  10.6 20.9 %collective-permute-start = (f32[224,896]{1,0:T(8,128)}, f32[224,896]{1,0:T(8,128)S(1)}, u32[]{:S(2)}, u32[]{:S(2)}) collective-permute-start(f32[224,896]{1,0:T(8,128)} %get-tuple-element.28), channel_id=1, source_target_pairs={{0,16},{8,24},{16,0},{24,8},{1,17},{9,25},{17,1},{25,9},{2,18},{10... | collective-permute-start | bytes 2408456 | tf_op jit(solution)/shard_map/ppermute | solution.py:583
  13.1 18.4 %copy-start.1 = (f32[1,224,896]{2,1,0:T(8,128)S(1)}, f32[1,224,896]{2,1,0:T(8,128)}, u32[]{:S(2)}) copy-start(f32[1,224,896]{2,1,0:T(8,128)} %param.14) | copy-start | bytes 2408452
  14.2 5.0 %collective-permute-start.11 = (bf16[128,384]{1,0:T(8,128)(2,1)S(1)}, bf16[128,384]{1,0:T(8,128)(2,1)S(1)}, u32[]{:S(2)}, u32[]{:S(2)}) collective-permute-start(bf16[128,384]{1,0:T(8,128)(2,1)S(1)} %constant_dynamic-slice_fusion), channel_id=1, source_target_pairs={{0,2},{1,3},{2,0},{3,1},{4,6},{5,7},{6,4},{7,5},{8,10},{9,11},{10,... | collective-permute-start | bytes 294920 | tf_op jit(solution)/shard_map/ppermute | solution.py:583
  17.2 23.5 %collective-permute-start.5 = (bf16[448,512]{1,0:T(8,128)(2,1)S(1)}, bf16[448,512]{1,0:T(8,128)(2,1)S(1)}, u32[]{:S(2)}, u32[]{:S(2)}) collective-permute-start(bf16[448,512]{1,0:T(8,128)(2,1)S(1)} %add_convert_fusion.1), channel_id=1, source_target_pairs={{0,16},{8,24},{16,0},{24,8},{1,17},{9,25},{17,1},{25,9},{2,18},{10... | collective-permute-start | bytes 1376264 | tf_op jit(solution)/shard_map/ppermute | solution.py:583
  19.2 8.1 %collective-permute-start.13 = (bf16[128,384]{1,0:T(8,128)(2,1)S(1)}, bf16[128,384]{1,0:T(8,128)(2,1)S(1)}, u32[]{:S(2)}, u32[]{:S(2)}) collective-permute-start(bf16[128,384]{1,0:T(8,128)(2,1)S(1)} %add_convert_fusion.4), channel_id=1, source_target_pairs={{0,4},{1,5},{2,6},{3,7},{4,0},{5,1},{6,2},{7,3},{8,12},{9,13},{10,... | collective-permute-start | bytes 294920 | tf_op jit(solution)/shard_map/ppermute | solution.py:583
  24.4 16.6 %copy-start.4 = (f32[64,1024]{1,0:T(8,128)}, f32[64,1024]{1,0:T(8,128)S(1)}, u32[]{:S(2)}) copy-start(f32[64,1024]{1,0:T(8,128)S(1)} %collective-permute-done.9.refs_12_) | copy-start | bytes 786436
  24.4 18.0 %copy-start = (f32[1,224,896]{2,1,0:T(8,128)S(1)}, f32[1,224,896]{2,1,0:T(8,128)}, u32[]{:S(2)}) copy-start(f32[1,224,896]{2,1,0:T(8,128)} %param.15) | copy-start | bytes 2408452
  24.4 16.4 %collective-permute-start.12 = (f32[128,1024]{1,0:T(8,128)S(1)}, f32[128,1024]{1,0:T(8,128)S(1)}, u32[]{:S(2)}, u32[]{:S(2)}) collective-permute-start(f32[128,1024]{1,0:T(8,128)S(1)} %pad_maximum_fusion.1), channel_id=1, source_target_pairs={{0,2},{1,3},{2,0},{3,1},{4,6},{5,7},{6,4},{7,5},{8,10},{9,11},{10,... | collective-permute-start | bytes 1572872 | tf_op jit(solution)/shard_map/ppermute | solution.py:583
  27.4 20.4 %copy-start.8 = (bf16[128,384]{1,0:T(8,128)(2,1)}, bf16[128,384]{1,0:T(8,128)(2,1)S(1)}, u32[]{:S(2)}) copy-start(bf16[128,384]{1,0:T(8,128)(2,1)S(1)} %add_convert_fusion.3.refs_15_) | copy-start | bytes 294916
  27.4 13.4 %collective-permute-start.14 = (bf16[128,384]{1,0:T(8,128)(2,1)S(1)}, bf16[128,384]{1,0:T(8,128)(2,1)S(1)}, u32[]{:S(2)}, u32[]{:S(2)}) collective-permute-start(bf16[128,384]{1,0:T(8,128)(2,1)S(1)} %add_convert_fusion.3.refs_15_), channel_id=1, source_target_pairs={{0,2},{1,3},{2,0},{3,1},{4,6},{5,7},{6,4},{7,5},{8,10},{9,11},{10,... | collective-permute-start | bytes 294920 | tf_op jit(solution)/shard_map/ppermute | solution.py:583
  31.5 11.4 %copy-start.9 = (f32[224,896]{1,0:T(8,128)}, f32[224,896]{1,0:T(8,128)S(1)}, u32[]{:S(2)}) copy-start(f32[224,896]{1,0:T(8,128)S(1)} %collective-permute-done.refs_4_) | copy-start | bytes 2408452
  31.5 15.7 %collective-permute-start.1 = (f32[224,896]{1,0:T(8,128)S(1)}, f32[224,896]{1,0:T(8,128)S(1)}, u32[]{:S(2)}, u32[]{:S(2)}) collective-permute-start(f32[224,896]{1,0:T(8,128)S(1)} %bitcast.15), channel_id=1, source_target_pairs={{0,8},{8,0},{16,24},{24,16},{1,9},{9,1},{17,25},{25,17},{2,10},{10... | collective-permute-start | bytes 2408456 | tf_op jit(solution)/shard_map/ppermute | solution.py:583
  40.8 7.8 %copy-start.6 = (bf16[448,512]{1,0:T(8,128)(2,1)}, bf16[448,512]{1,0:T(8,128)(2,1)S(1)}, u32[]{:S(2)}) copy-start(bf16[448,512]{1,0:T(8,128)(2,1)S(1)} %add_convert_fusion.refs_6_) | copy-start | bytes 1376260
  40.8 28.8 %copy-start.13 = (bf16[128,384]{1,0:T(8,128)(2,1)}, bf16[128,384]{1,0:T(8,128)(2,1)S(1)}, u32[]{:S(2)}) copy-start(bf16[128,384]{1,0:T(8,128)(2,1)S(1)} %collective-permute-done.14.refs_16_) | copy-start | bytes 294916
  40.8 28.8 %copy-start.5 = (f32[128,1024]{1,0:T(8,128)}, f32[128,1024]{1,0:T(8,128)S(1)}, u32[]{:S(2)}) copy-start(f32[128,1024]{1,0:T(8,128)S(1)} %collective-permute-done.12.refs_13_) | copy-start | bytes 1572868
  41.0 28.8 %collective-permute-start.15 = (f32[256,1024]{1,0:T(8,128)S(1)}, f32[256,1024]{1,0:T(8,128)S(1)}, u32[]{:S(2)}, u32[]{:S(2)}) collective-permute-start(f32[256,1024]{1,0:T(8,128)S(1)} %pad_maximum_fusion), channel_id=1, source_target_pairs={{0,1},{1,0},{2,3},{3,2},{4,5},{5,4},{6,7},{7,6},{8,9},{9,8},{10,11... | collective-permute-start | bytes 3145736 | tf_op jit(solution)/shard_map/ppermute | solution.py:583
  42.4 5.4 %collective-permute-start.2 = (f32[224,896]{1,0:T(8,128)S(1)}, f32[224,896]{1,0:T(8,128)S(1)}, u32[]{:S(2)}, u32[]{:S(2)}) collective-permute-start(f32[224,896]{1,0:T(8,128)S(1)} %bitcast.11), channel_id=1, source_target_pairs={{0,8},{8,0},{16,24},{24,16},{1,9},{9,1},{17,25},{25,17},{2,10},{10... | collective-permute-start | bytes 2408456 | tf_op jit(solution)/shard_map/ppermute | solution.py:583
  42.4 3.6 %collective-permute-start.6 = (bf16[448,512]{1,0:T(8,128)(2,1)S(1)}, bf16[448,512]{1,0:T(8,128)(2,1)S(1)}, u32[]{:S(2)}, u32[]{:S(2)}) collective-permute-start(bf16[448,512]{1,0:T(8,128)(2,1)S(1)} %add_convert_fusion.refs_6_), channel_id=1, source_target_pairs={{0,8},{8,0},{16,24},{24,16},{1,9},{9,1},{17,25},{25,17},{2,10},{10... | collective-permute-start | bytes 1376264 | tf_op jit(solution)/shard_map/ppermute | solution.py:583
  42.9 5.7 %collective-permute-start.3 = (f32[224,896]{1,0:T(8,128)S(1)}, f32[224,896]{1,0:T(8,128)}, u32[]{:S(2)}, u32[]{:S(2)}) collective-permute-start(f32[224,896]{1,0:T(8,128)S(1)} %collective-permute-done.refs_4_), channel_id=1, source_target_pairs={{0,8},{8,0},{16,24},{24,16},{1,9},{9,1},{17,25},{25,17},{2,10},{10... | collective-permute-start | bytes 2408456 | tf_op jit(solution)/shard_map/ppermute | solution.py:583
  46.0 1.8 %copy-start.12 = (bf16[448,512]{1,0:T(8,128)(2,1)}, bf16[448,512]{1,0:T(8,128)(2,1)S(1)}, u32[]{:S(2)}) copy-start(bf16[448,512]{1,0:T(8,128)(2,1)S(1)} %collective-permute-done.6.refs_7_) | copy-start | bytes 1376260
  46.0 23.7 %collective-permute-start.8 = (f32[224,512]{1,0:T(8,128)S(1)}, f32[224,512]{1,0:T(8,128)}, u32[]{:S(2)}, u32[]{:S(2)}) collective-permute-start(f32[224,512]{1,0:T(8,128)S(1)} %slice.3), channel_id=1, source_target_pairs={{0,24},{8,16},{16,8},{24,0},{1,25},{9,17},{17,9},{25,1},{2,26},{10... | collective-permute-start | bytes 1376264 | tf_op jit(solution)/shard_map/ppermute | solution.py:583
  47.2 1.4 %copy-start.10 = (f32[224,896]{1,0:T(8,128)}, f32[224,896]{1,0:T(8,128)S(1)}, u32[]{:S(2)}) copy-start(f32[224,896]{1,0:T(8,128)S(1)} %collective-permute-done.1.refs_1_) | copy-start | bytes 2408452
  47.2 22.5 %collective-permute-start.7 = (f32[224,512]{1,0:T(8,128)S(1)}, f32[224,512]{1,0:T(8,128)S(1)}, u32[]{:S(2)}, u32[]{:S(2)}) collective-permute-start(f32[224,512]{1,0:T(8,128)S(1)} %slice.3), channel_id=1, source_target_pairs={{0,16},{8,24},{16,0},{24,8},{1,17},{9,25},{17,1},{25,9},{2,18},{10... | collective-permute-start | bytes 1376264 | tf_op jit(solution)/shard_map/ppermute | solution.py:583
  47.9 0.9 copy-start.2
  47.9 21.9 %collective-permute-start.16 = (bf16[256,384]{1,0:T(8,128)(2,1)S(1)}, bf16[256,384]{1,0:T(8,128)(2,1)S(1)}, u32[]{:S(2)}, u32[]{:S(2)}) collective-permute-start(bf16[256,384]{1,0:T(8,128)(2,1)S(1)} %pad_maximum_fusion.2), channel_id=1, source_target_pairs={{0,1},{1,0},{2,3},{3,2},{4,5},{5,4},{6,7},{7,6},{8,9},{9,8},{10,11... | collective-permute-start | bytes 589832 | tf_op jit(solution)/shard_map/ppermute | solution.py:583
  69.7 0.7 copy-start.14
  69.7 0.9 copy-start.11
  69.7 1.2 %copy-start.7 = (f32[256,1024]{1,0:T(8,128)}, f32[256,1024]{1,0:T(8,128)S(1)}, u32[]{:S(2)}) copy-start(f32[256,1024]{1,0:T(8,128)S(1)} %collective-permute-done.15.refs_14_) | copy-start | bytes 3145732
